TPU v7x, 32 devices: a whole 2x2x4 slice. The times are simulated.
32 devices in a mesh: grp: 2 (over y), smp: 4 (over x, core), row: 4 (over z).
Axes of the slice: x: 2, y: 2, z: 4, core: 2. Of those that a mesh axis runs over, the one named last changes fastest.
Arguments:
- positions: float32 [8, 3, 4096], P(('grp', 'smp'), None, 'row'), parts along dimension 0, may hold values from -60 to 60
- noise_draw: float32 [8, 3, 4096], P(('grp', 'smp'), None, 'row'), parts along dimension 0, may hold values from -6 to 6
- noise_level: float32 [8], P(('grp', 'smp')), parts along dimension 0, may hold values from 0.5 to 80
- atom_single: bfloat16 [8192, 128], P(('grp', 'row')), parts along dimension 0, may hold values from -6 to 6
- token_single: bfloat16 [1024, 768], P(('grp', 'row')), parts along dimension 0, may hold values from -6 to 6
- pair_cond: bfloat16 [1024, 512, 128], P(('grp', 'row'), 'smp'), parts along dimension 0, may hold values from -6 to 6
- atom_to_token: int32 [8192], P(('grp', 'row')), parts along dimension 0, may hold values from 0 to 511, as said below
- window_offsets: int32 [256], P(('grp', 'row')), parts along dimension 0, may hold values from -96 to 0
- atom_mask: int32 [8192], P('grp'), parts along dimension 0, may hold values 0 or 1
- token_mask: int32 [1024], P('grp'), parts along dimension 0, may hold values 0 or 1
- coord_in: float32 [3, 128], replicated, may hold values from -3.5 to 3.5
- atom_gain: float32 [2, 128], replicated, may hold values from 0.1 to 1.9
- atom_qkv: bfloat16 [2, 128, 384], replicated, may hold values from -1 to 1
- atom_proj: bfloat16 [2, 128, 128], replicated, may hold values from -0.5 to 0.5
- gather_in: bfloat16 [128, 768], replicated, may hold values from -0.5 to 0.5
- noise_embed: float32 [768], replicated, may hold values from -6 to 6
- pair_gain: float32 [128], replicated, may hold values from 0.1 to 1.9
- pair_heads: bfloat16 [128, 16], replicated, may hold values from -0.5 to 0.5
- token_gain: float32 [2, 768], replicated, may hold values from 0.1 to 1.9
- token_qkv: bfloat16 [768, 2304], replicated, may hold values from -1 to 1
- token_proj: bfloat16 [768, 768], replicated, may hold values from -0.21875 to 0.21875
- ffn_in: bfloat16 [768, 3072], replicated, may hold values from -0.21875 to 0.21875
- ffn_out: bfloat16 [1536, 768], replicated, may hold values from -0.15625 to 0.15625
- scatter_out: bfloat16 [768, 128], replicated, may hold values from -0.21875 to 0.21875
- out_gain: float32 [128], replicated, may hold values from 0.1 to 1.9
- coord_out: bfloat16 [3, 128], replicated, may hold values from -0.5 to 0.5
Outputs:
- token_out: bfloat16 [8, 512, 768], P(('grp', 'smp'), 'row'), parts along dimension 0
- direction: float32 [8, 3, 4096], P(('grp', 'smp'), None, 'row'), parts along dimension 0
There are 2 independent parts, one for each index of `grp`. A program takes and returns all parts, laid end to end along the dimension named above; an argument that names none is the same for every part. Nothing has to cross between parts.
Inputs may be any that keep to these rules, and one draw needn't show every extreme that they name: `atom_to_token`: never falls along the atoms; atoms k * 1024 to (k + 1) * 1024 - 1 belong to tokens k * 128 to (k + 1) * 128 - 1; some tokens have no atom.
All inputs are finite; a program needn't handle non-finite values.
Results may differ from a plain program's by a relative error of at most 0.013.
Values may be sent and summed in bfloat16 or wider, within the bound.
No kernel may reach another device: no remote copies, remote signals or barrier semaphores. Data moves between devices by JAX's collectives and lax.ppermute only.
A program may use at most 128 MiB of HBM per device.

v0:
```python
import jax
import jax.numpy as jnp
from jax import lax
from jax.sharding import PartitionSpec as P

D = 768
HEADS = 16
FF = 1536
CA = 128
AHEADS = 4
WQ = 32
WK = 128
HALO = 96


sigma_data = 16.0
gamma_boost = 0.8
norm_eps = 1e-05
masked_score = -1e30
outside_score = -2e30


def with_halo(block, sides, width):
    for axis, dim in sides:
        count = lax.axis_size(axis)
        forward = [(i, i + 1) for i in range(count - 1)]
        backward = [(target, source) for source, target in forward]
        low = lax.ppermute(
            lax.slice_in_dim(block, block.shape[dim] - width, None, axis=dim), axis, forward
        )
        high = lax.ppermute(lax.slice_in_dim(block, 0, width, axis=dim), axis, backward)
        block = jnp.concatenate([low, block, high], axis=dim)
    return block


def layer_norm(values, norm_gain):
    average = jnp.mean(values, axis=-1, keepdims=True)
    centred = values - average
    variance = jnp.mean(centred * centred, axis=-1, keepdims=True)
    return centred * lax.rsqrt(variance + norm_eps) * norm_gain


def softmax_rows(scores):
    largest = jnp.max(scores, axis=-1, keepdims=True)
    exponent = jnp.exp(scores - largest)
    return exponent / jnp.sum(exponent, axis=-1, keepdims=True)


def pair_bias_of(pair_tile, pair_gain, pair_heads):
    normed = layer_norm(pair_tile.astype(jnp.float32), pair_gain).astype(jnp.bfloat16)
    return jnp.einsum("ijc,ch->hij", normed, pair_heads, preferred_element_type=jnp.float32).astype(
        jnp.bfloat16
    )


def block_spans(extended, block_count, span_blocks):
    tail_shape = extended.shape[1:]
    grouped = extended.reshape((block_count + span_blocks - 1, WQ) + tail_shape)
    pieces = [grouped[shift : shift + block_count] for shift in range(span_blocks)]
    return jnp.stack(pieces, axis=1).reshape((block_count, span_blocks * WQ) + tail_shape)


def window_attend(queries, windows, live, inside, w_out):
    block_count = queries.shape[0] // WQ
    head_size = CA // AHEADS
    span_rows = windows.shape[1]
    query_heads = queries.reshape(block_count, WQ, AHEADS, head_size)
    key_heads = windows[:, :, :CA].reshape(block_count, span_rows, AHEADS, head_size)
    value_heads = windows[:, :, CA:].reshape(block_count, span_rows, AHEADS, head_size)
    scores = jnp.einsum(
        "bqhd,bkhd->bhqk", query_heads, key_heads, preferred_element_type=jnp.float32
    ) / jnp.sqrt(jnp.float32(head_size))
    scores = jnp.where(live[:, None, None, :], scores, masked_score)
    scores = jnp.where(inside[:, None, None, :], scores, outside_score)
    weights = softmax_rows(scores).astype(jnp.bfloat16)
    mixed_heads = jnp.einsum(
        "bhqk,bkhd->bqhd", weights, value_heads, preferred_element_type=jnp.float32
    ).astype(jnp.bfloat16)
    return jnp.dot(
        mixed_heads.reshape(block_count * WQ, CA), w_out, preferred_element_type=jnp.float32
    )


def atom_block(atom_state, norm_gain, w_qkv, w_out, offsets, live_ext):
    row_count = atom_state.shape[0]
    normed = layer_norm(atom_state, norm_gain).astype(jnp.bfloat16)
    widened = with_halo(normed, (("row", 0),), HALO)
    projected = jnp.dot(widened, w_qkv, preferred_element_type=jnp.float32).astype(jnp.bfloat16)
    queries = projected[HALO : HALO + row_count, :CA]
    extended = projected[:, CA:]
    block_count = row_count // WQ
    span_blocks = (2 * HALO + WQ) // WQ
    windows = block_spans(extended, block_count, span_blocks)
    live = block_spans(live_ext, block_count, span_blocks) > 0
    relative = jnp.arange(span_blocks * WQ, dtype=jnp.int32)[None, :]
    first_key = offsets[:, None] + HALO
    inside = (relative >= first_key) & (relative < first_key + WK)
    return atom_state + window_attend(queries, windows, live, inside, w_out)


def per_device(
    positions,
    noise_draw,
    noise_level,
    atom_single,
    token_single,
    pair_cond,
    atom_to_token,
    window_offsets,
    atom_mask,
    token_mask,
    coord_in,
    atom_gain,
    atom_qkv,
    atom_proj,
    gather_in,
    noise_embed,
    pair_gain,
    pair_heads,
    token_gain,
    token_qkv,
    token_proj,
    ffn_in,
    ffn_out,
    scatter_out,
    out_gain,
    coord_out,
):
    row_index = lax.axis_index("row")
    tok_rows = token_single.shape[0]
    atom_rows = atom_single.shape[0]
    head_size = D // HEADS
    biases = lax.all_gather(
        pair_bias_of(pair_cond, pair_gain, pair_heads), "smp", axis=2, tiled=True
    )
    local_token = atom_to_token - row_index * tok_rows
    valid_local = lax.dynamic_slice_in_dim(atom_mask, row_index * atom_rows, atom_rows)
    member = (local_token[None, :] == jnp.arange(tok_rows, dtype=jnp.int32)[:, None]) & (
        valid_local[None, :] > 0
    )
    onehot = member.astype(jnp.bfloat16)
    counts = jnp.maximum(jnp.sum(member.astype(jnp.float32), axis=1), 1.0)
    live_padded = jnp.pad(atom_mask, (HALO, HALO))
    live_ext = lax.dynamic_slice_in_dim(live_padded, row_index * atom_rows, atom_rows + 2 * HALO)
    key_live = token_mask > 0
    coords = positions[0]
    kicks = noise_draw[0]
    level_now = noise_level[0]
    level_hat = (1.0 + gamma_boost) * level_now
    noisy = coords + jnp.sqrt(level_hat * level_hat - level_now * level_now) * kicks
    scaled = noisy / jnp.sqrt(level_hat * level_hat + sigma_data * sigma_data)
    atom_state = atom_single.astype(jnp.float32) + jnp.einsum(
        "ka,kc->ac", scaled, coord_in, precision=lax.Precision.HIGHEST
    )
    atom_state = atom_block(
        atom_state, atom_gain[0], atom_qkv[0], atom_proj[0], window_offsets, live_ext
    )
    lifted = jax.nn.relu(
        jnp.dot(atom_state.astype(jnp.bfloat16), gather_in, preferred_element_type=jnp.float32)
    ).astype(jnp.bfloat16)
    pooled = jnp.dot(onehot, lifted, preferred_element_type=jnp.float32) / counts[:, None]
    token_state = (
        pooled
        + token_single.astype(jnp.float32)
        + jnp.log(level_hat / sigma_data) / 4.0 * noise_embed
    )
    normed = layer_norm(token_state, token_gain[0]).astype(jnp.bfloat16)
    projected = jnp.dot(normed, token_qkv, preferred_element_type=jnp.float32).astype(jnp.bfloat16)
    gathered = lax.all_gather(projected[:, D:], "row", axis=0, tiled=True)
    key_count = gathered.shape[0]
    query_heads = projected[:, :D].reshape(tok_rows, HEADS, head_size)
    key_heads = gathered[:, :D].reshape(key_count, HEADS, head_size)
    value_heads = gathered[:, D:].reshape(key_count, HEADS, head_size)
    scores = jnp.einsum(
        "ihd,jhd->hij", query_heads, key_heads, preferred_element_type=jnp.float32
    ) / jnp.sqrt(jnp.float32(head_size))
    scores = scores + biases.astype(jnp.float32)
    scores = jnp.where(key_live[None, None, :], scores, masked_score)
    weights = softmax_rows(scores).astype(jnp.bfloat16)
    mixed_heads = (
        jnp.einsum("hij,jhd->ihd", weights, value_heads, preferred_element_type=jnp.float32)
        .astype(jnp.bfloat16)
        .reshape(tok_rows, D)
    )
    token_state = token_state + jnp.dot(mixed_heads, token_proj, preferred_element_type=jnp.float32)
    normed = layer_norm(token_state, token_gain[1]).astype(jnp.bfloat16)
    hidden = jnp.dot(normed, ffn_in, preferred_element_type=jnp.float32)
    active = (jax.nn.silu(hidden[:, :FF]) * hidden[:, FF:]).astype(jnp.bfloat16)
    token_state = token_state + jnp.dot(active, ffn_out, preferred_element_type=jnp.float32)
    token_result = token_state.astype(jnp.bfloat16)
    spread_back = jnp.dot(token_result, scatter_out, preferred_element_type=jnp.float32).astype(
        jnp.bfloat16
    )
    atom_state = atom_state + lax.dot_general(
        onehot, spread_back, (((0,), (0,)), ((), ())), preferred_element_type=jnp.float32
    )
    atom_state = atom_block(
        atom_state, atom_gain[1], atom_qkv[1], atom_proj[1], window_offsets, live_ext
    )
    normed_out = layer_norm(atom_state, out_gain).astype(jnp.bfloat16)
    update = lax.dot_general(
        coord_out, normed_out, (((1,), (1,)), ((), ())), preferred_element_type=jnp.float32
    )
    base_square = sigma_data * sigma_data + level_hat * level_hat
    skip_scale = sigma_data * sigma_data / base_square
    out_scale = level_hat * sigma_data / jnp.sqrt(base_square)
    denoised = skip_scale * noisy + out_scale * update
    direction = (noisy - denoised) / level_hat
    return (token_result[None], direction[None])


def solution(mesh):
    in_specs = (
        P(("grp", "smp"), None, "row"),
        P(("grp", "smp"), None, "row"),
        P(("grp", "smp")),
        P(("grp", "row"), None),
        P(("grp", "row"), None),
        P(("grp", "row"), "smp", None),
        P(("grp", "row")),
        P(("grp", "row")),
        P("grp"),
        P("grp"),
        P(),
        P(),
        P(),
        P(),
        P(),
        P(),
        P(),
        P(),
        P(),
        P(),
        P(),
        P(),
        P(),
        P(),
        P(),
        P(),
    )
    out_specs = (P(("grp", "smp"), "row", None), P(("grp", "smp"), None, "row"))
    return jax.shard_map(
        per_device, mesh=mesh, in_specs=in_specs, out_specs=out_specs, check_vma=False
    )
```

profile of v0, /device:TPU:0, one launch (start us, length us, event | category | flops | bytes accessed | tf_op | source)
XLA Modules:
  0.0 203.9 jit_solution(14690072002025671553)
XLA Ops:
  8.1 2.2 %fusion.123 = (f32[1024]{0:T(1024)S(1)}, f32[1024,128]{1,0:T(8,128)S(1)}) fusion(f32[3,128]{1,0:T(4,128)} %param.36, f32[]{:T(128)S(6)} %sqrt.8, f32[1,3,1024]{2,0,1:T(1,128)} %param.27, f32[]{:T(128)S(6)} %sqrt.7, f32[1,3,1024]{2,0,1:T(1,128)} %param.26, bf16[1024,128]{1,0:T(8,128)(2,1)} %param.29), kind=kOutput, calls=%fused_computation.202 | convolution fusion | flops 5120000 | bytes 816648 | tf_op jit(solution)/shard_map/ka,kc->ac/dot_general | solution.py:152
  13.7 5.5 %collective-permute-start = (bf16[96,128]{1,0:T(8,128)(2,1)}, bf16[96,128]{1,0:T(8,128)(2,1)}, u32[]{:S(2)}, u32[]{:S(2)}) collective-permute-start(bf16[96,128]{1,0:T(8,128)(2,1)} %get-tuple-element.32), channel_id=1, source_target_pairs={{0,1},{1,2},{2,3},{4,5},{5,6},{6,7},{8,9},{9,10},{10,11},{12,13},{... | collective-permute-start | bytes 73736 | tf_op jit(solution)/shard_map/ppermute | solution.py:28
  20.5 1.7 pad_dynamic-slice_fusion.6
  31.2 1.6 stack.95
  44.0 2.5 %fusion.117 = (bf16[32,224,128]{2,1,0:T(8,128)(2,1)}, bf16[32,224,128]{2,1,0:T(8,128)(2,1)}) fusion(bf16[32,224,256]{2,1,0:T(8,128)(2,1)S(1)} %bitcast.141), kind=kLoop, calls=%fused_computation.196 | loop fusion | bytes 7340032 | tf_op jit(solution)/shard_map/slice | solution.py:68
  46.5 4.0 %copy.78 = bf16[32,224,128]{1,2,0:T(8,128)(2,1)} copy(bf16[32,224,128]{2,1,0:T(8,128)(2,1)} %get-tuple-element.12) | data formatting | bytes 3670016 | tf_op jit(solution)/shard_map/slice | solution.py:68
  50.5 2.7 %reshape.297 = bf16[32,32,4,32]{3,2,1,0:T(4,128)(2,1)} reshape(bf16[1024,128]{1,0:T(8,128)(2,1)} %slice.290) | data formatting | bytes 524288 | tf_op jit(solution)/shard_map/reshape | solution.py:67
  53.2 3.9 %copy.77 = bf16[32,224,128]{1,2,0:T(8,128)(2,1)} copy(bf16[32,224,128]{2,1,0:T(8,128)(2,1)} %get-tuple-element.13) | data formatting | bytes 3670016 | tf_op jit(solution)/shard_map/slice | solution.py:69
  57.2 2.6 %fusion.49 = f32[32,4,32,224]{3,2,1,0:T(8,128)S(1)} fusion(bf16[32,224,4,32]{1,3,2,0:T(8,128)(2,1)} %bitcast.139, bf16[32,32,4,32]{3,2,1,0:T(4,128)(2,1)} %reshape.297), kind=kOutput, calls=%fused_computation.72 | convolution fusion | flops 58720256 | bytes 5767168 | tf_op jit(solution)/shard_map/bqhd,bkhd->bhqk/dot_general | solution.py:70
  59.8 6.4 %fusion.124 = (f32[32,4,32]{2,1,0:T(4,128)S(1)}, f32[32,4,32,224]{3,2,1,0:T(8,128)S(1)}) fusion(f32[32,4,32,224]{3,2,1,0:T(8,128)S(1)} %fusion.49, pred[32,224]{1,0:T(8,128)(4,1)S(1)} %copy-done.17, pred[32,224]{1,0:T(8,128)(4,1)S(1)} %copy-done.19), kind=kOutput, calls=%fused_computation.203 | output fusion | flops 7340255 | bytes 7370752 | tf_op jit(solution)/shard_map/sub | solution.py:45
  67.3 1.7 copy.80
  69.0 2.9 %reshape.299 = bf16[1024,128]{0,1:T(8,128)(2,1)} reshape(bf16[32,32,4,32]{1,0,3,2:T(8,128)(2,1)} %copy.80) | data formatting | bytes 524288 | tf_op jit(solution)/shard_map/reshape | solution.py:80
  71.9 2.2 %convolution_add_fusion.2 = f32[1024,128]{1,0:T(8,128)} fusion(f32[1024,128]{1,0:T(8,128)} %copy-done.3, bf16[1024,128]{0,1:T(8,128)(2,1)} %reshape.299, bf16[2,128,128]{2,1,0:T(8,128)(2,1)} %param.39), kind=kOutput, calls=%fused_computation.53 | convolution fusion | flops 33685504 | bytes 1343488 | tf_op jit(solution)/shard_map/dot_general | solution.py:79
  74.1 3.3 %fusion.125 = (f32[128]{0:T(128)}, f32[128,768]{1,0:T(8,128)}) fusion(f32[768]{0:T(1024)} %broadcast_multiply_fusion.1, bf16[128,768]{1,0:T(8,128)(2,1)} %param.30, f32[128]{0:T(128)} %broadcast_maximum_fusion, bf16[128,768]{1,0:T(8,128)(2,1)} %param.40, f32[1024,128]{1,0:T(8,128)} %convolution_add_fusion.2, s32[1024]{0:T(1024)S(1)} %broadcast_subtract_fusion, ...), kind=kOutput, calls=%fused_computation.204 | convolution fusion | flops 405110656 | bytes 1319936 | tf_op jit(solution)/shard_map/dot_general | solution.py:161
  79.3 1.7 convolution_convert_fusion
  82.9 3.5 %convert_reduce_fusion = f32[128,128]{1,0:T(8,128)S(1)} fusion(bf16[128,128,128]{2,1,0:T(8,128)(2,1)} %param.31), kind=kLoop, calls=%fused_computation.4 | loop fusion | flops 4177920 | bytes 4259840 | tf_op jit(solution)/shard_map/reduce_sum | solution.py:37
  86.4 4.8 %fusion.5 = f32[128,128]{1,0:T(8,128)S(1)} fusion(bf16[128,128,128]{2,1,0:T(8,128)(2,1)S(1)} %copy-done.2, f32[128,128]{1,0:T(8,128)S(1)} %broadcast_multiply_fusion), kind=kLoop, calls=%fused_computation.7 | loop fusion | flops 8372224 | bytes 4325376 | tf_op jit(solution)/shard_map/reduce_sum | solution.py:39
  91.3 5.8 %fusion.8 = bf16[128,128,16]{1,2,0:T(8,128)(2,1)S(1)} fusion(bf16[128,128,128]{2,1,0:T(8,128)(2,1)S(1)} %copy-done.2, f32[128]{0:T(128)S(1)} %copy-done.27, f32[128,128]{1,0:T(8,128)S(1)} %add_rsqrt_fusion, f32[128,128]{1,0:T(8,128)S(1)} %broadcast_multiply_fusion, bf16[128,16]{0,1:T(8,128)(2,1)S(1)} %copy-done.25), kind=kOutput, calls=%fused_computation.10 | convolution fusion | flops 77594624 | bytes 4854272 | tf_op jit(solution)/shard_map/ijc,ch->hij/dot_general | solution.py:51
  98.3 23.8 %all-gather.3.cloned.1.call-done = bf16[512,1536]{1,0:T(8,128)(2,1)} async-done(((bf16[128,1536]{1,0:T(8,128)(2,1)}), bf16[512,1536]{1,0:T(8,128)(2,1)}) %all-gather.3.cloned.1.call-update) | async-done | bytes 1572880 | tf_op jit(solution)/shard_map/all_gather | solution.py:169
  124.2 21.2 %all-gather.5.cloned.1.call-done = bf16[16,128,512]{2,1,0:T(8,128)(2,1)} async-done(((bf16[16,128,128]{2,1,0:T(8,128)(2,1)}), bf16[16,128,512]{2,1,0:T(8,128)(2,1)}) %all-gather.5.cloned.1.call-update) | async-done | bytes 2097168 | tf_op jit(solution)/shard_map/all_gather | solution.py:133
  145.4 3.3 %fusion.128 = f32[16,128]{1,0:T(8,128)S(1)} fusion(bf16[16,128,512]{2,1,0:T(8,128)(2,1)} %all-gather.5.cloned.1.call-done, pred[512]{0:T(512)(128)(4,1)S(1)} %broadcast_compare_fusion.1, bf16[128,16,48]{0,2,1:T(8,128)(2,1)S(1)} %bitcast.165, bf16[512,16,48]{0,2,1:T(8,128)(2,1)S(1)} %bitcast.160), kind=kOutput, calls=%fused_computation.205 | convolution fusion | flops 106955264 | bytes 3088896 | tf_op jit(solution)/shard_map/sub | solution.py:45
  148.8 4.5 %fusion.40 = bf16[16,48,128]{2,1,0:T(8,128)(2,1)} fusion(bf16[512,16,48]{0,2,1:T(8,128)(2,1)S(1)} %bitcast.162, f32[16,128]{1,0:T(8,128)S(1)} %fusion.128, bf16[16,128,512]{2,1,0:T(8,128)(2,1)} %all-gather.5.cloned.1.call-done, pred[512]{0:T(512)(128)(4,1)} %copy-done.23, bf16[128,16,48]{0,2,1:T(8,128)(2,1)} %bitcast.166, bf16[512,16,48]{0,2,1:T(8,128)(2,1)S(1)} %bitcast.161), kind=kOutput, calls=%fused_computation.60 | convolution fusion | flops 208767488 | bytes 4071936 | tf_op jit(solution)/shard_map/hij,jhd->ihd/dot_general | solution.py:181
  154.9 3.3 %fusion.79 = f32[128,3072]{1,0:T(8,128)S(1)} fusion(bf16[768,3072]{1,0:T(8,128)(2,1)} %param.47, f32[128,768]{1,0:T(8,128)S(1)} %get-tuple-element.52, f32[768]{0:T(1024)S(1)} %get-tuple-element.8, f32[128]{0:T(128)S(1)} %add_rsqrt_fusion.4, f32[128]{0:T(128)S(1)} %broadcast_multiply_fusion.5), kind=kOutput, calls=%fused_computation.110 | convolution fusion | flops 604372992 | bytes 6688768 | tf_op jit(solution)/shard_map/dot_general | solution.py:187
  160.6 3.4 %collective-permute-start.2 = (bf16[96,128]{1,0:T(8,128)(2,1)S(1)}, bf16[96,128]{1,0:T(8,128)(2,1)S(1)}, u32[]{:S(2)}, u32[]{:S(2)}) collective-permute-start(bf16[96,128]{1,0:T(8,128)(2,1)S(1)} %get-tuple-element.30), channel_id=1, source_target_pairs={{0,1},{1,2},{2,3},{4,5},{5,6},{6,7},{8,9},{9,10},{10,11},{12,13},{... | collective-permute-start | bytes 73736 | tf_op jit(solution)/shard_map/ppermute | solution.py:28
  165.6 4.1 %collective-permute-done.3 = bf16[96,128]{1,0:T(8,128)(2,1)S(1)} collective-permute-done((bf16[96,128]{1,0:T(8,128)(2,1)S(1)}, bf16[96,128]{1,0:T(8,128)(2,1)S(1)}, u32[]{:S(2)}, u32[]{:S(2)}) %collective-permute-start.3) | collective-permute-done | bytes 24608 | tf_op jit(solution)/shard_map/ppermute | solution.py:31
  170.7 2.5 %fusion.116 = (bf16[32,224,128]{2,1,0:T(8,128)(2,1)}, bf16[32,224,128]{2,1,0:T(8,128)(2,1)}) fusion(bf16[32,224,256]{2,1,0:T(8,128)(2,1)S(1)} %bitcast.142), kind=kLoop, calls=%fused_computation.195 | loop fusion | bytes 7340032 | tf_op jit(solution)/shard_map/slice | solution.py:68
  173.2 3.2 %copy.93 = bf16[32,224,128]{1,2,0:T(8,128)(2,1)S(1)} copy(bf16[32,224,128]{2,1,0:T(8,128)(2,1)} %get-tuple-element.10) | data formatting | bytes 3670016 | tf_op jit(solution)/shard_map/slice | solution.py:68
  177.6 4.3 %fusion.131 = (f32[32,4,32]{2,1,0:T(4,128)}, f32[32,4,32,224]{3,2,1,0:T(8,128)}) fusion(f32[32,4,32,224]{3,2,1,0:T(8,128)S(1)} %fusion.47, pred[32,224]{1,0:T(8,128)(4,1)S(1)} %copy-done.18, pred[32,224]{1,0:T(8,128)(4,1)S(1)} %copy-done.20), kind=kOutput, calls=%fused_computation.208 | output fusion | flops 7340255 | bytes 7370752 | tf_op jit(solution)/shard_map/sub | solution.py:45
  181.8 3.1 %copy.92 = bf16[32,224,128]{1,2,0:T(8,128)(2,1)} copy(bf16[32,224,128]{2,1,0:T(8,128)(2,1)S(1)} %copy-done.5) | data formatting | bytes 3670016 | tf_op jit(solution)/shard_map/slice | solution.py:69
  184.9 3.8 %fusion.36 = bf16[32,32,4,32]{1,3,2,0:T(8,128)(2,1)S(1)} fusion(bf16[32,224,4,32]{1,3,2,0:T(8,128)(2,1)} %bitcast.159, f32[32,4,32,224]{3,2,1,0:T(8,128)} %get-tuple-element.56, f32[32,4,32]{2,1,0:T(4,128)} %get-tuple-element.55), kind=kOutput, calls=%fused_computation.50 | convolution fusion | flops 60686336 | bytes 5783552 | tf_op jit(solution)/shard_map/bhqk,bkhd->bqhd/dot_general | solution.py:76
  188.7 1.7 copy.95
  190.4 2.9 %reshape.308 = bf16[1024,128]{0,1:T(8,128)(2,1)} reshape(bf16[32,32,4,32]{1,0,3,2:T(8,128)(2,1)} %copy.95) | data formatting | bytes 524288 | tf_op jit(solution)/shard_map/reshape | solution.py:80
  (142 shorter events, 43.9 us)
Async XLA Ops:
  7.2 72.1 %copy-start = (bf16[768,2304]{1,0:T(8,128)(2,1)S(1)}, bf16[768,2304]{1,0:T(8,128)(2,1)}, u32[]{:S(2)}) copy-start(bf16[768,2304]{1,0:T(8,128)(2,1)} %param.45) | copy-start | bytes 10616836
  7.2 115.0 %all-gather.3.cloned.1.call-start = ((), (), s32[]{:S(2)}) async-start(), calls=%async_computation | async-start | bytes 1966080 | tf_op jit(solution)/shard_map/all_gather | solution.py:169
  10.3 1.7 copy-start.3
  13.7 27.6 %collective-permute-start = (bf16[96,128]{1,0:T(8,128)(2,1)}, bf16[96,128]{1,0:T(8,128)(2,1)}, u32[]{:S(2)}, u32[]{:S(2)}) collective-permute-start(bf16[96,128]{1,0:T(8,128)(2,1)} %get-tuple-element.32), channel_id=1, source_target_pairs={{0,1},{1,2},{2,3},{4,5},{5,6},{6,7},{8,9},{9,10},{10,11},{12,13},{... | collective-permute-start | bytes 73736 | tf_op jit(solution)/shard_map/ppermute | solution.py:28
  19.2 22.1 %collective-permute-start.1 = (bf16[96,128]{1,0:T(8,128)(2,1)}, bf16[96,128]{1,0:T(8,128)(2,1)}, u32[]{:S(2)}, u32[]{:S(2)}) collective-permute-start(bf16[96,128]{1,0:T(8,128)(2,1)} %get-tuple-element.33), channel_id=1, source_target_pairs={{1,0},{2,1},{3,2},{5,4},{6,5},{7,6},{9,8},{10,9},{11,10},{13,12},{... | collective-permute-start | bytes 73736 | tf_op jit(solution)/shard_map/ppermute | solution.py:31
  57.2 2.6 %copy-start.17 = (pred[32,224]{1,0:T(8,128)(4,1)S(1)}, pred[32,224]{1,0:T(8,128)(4,1)}, u32[]{:S(2)}) copy-start(pred[32,224]{1,0:T(8,128)(4,1)} %gt.27) | copy-start | bytes 21508
  57.2 2.6 %copy-start.19 = (pred[32,224]{1,0:T(8,128)(4,1)S(1)}, pred[32,224]{1,0:T(8,128)(4,1)}, u32[]{:S(2)}) copy-start(pred[32,224]{1,0:T(8,128)(4,1)} %fusion.94) | copy-start | bytes 21508
  59.8 6.4 %copy-start.8 = (bf16[32,224,128]{1,2,0:T(8,128)(2,1)S(1)}, bf16[32,224,128]{1,2,0:T(8,128)(2,1)}, u32[]{:S(2)}) copy-start(bf16[32,224,128]{1,2,0:T(8,128)(2,1)} %copy.77) | copy-start | bytes 5505028
  81.0 0.8 copy-start.7
  82.6 8.6 %copy-start.25 = (bf16[128,16]{0,1:T(8,128)(2,1)S(1)}, bf16[128,16]{0,1:T(8,128)(2,1)}, u32[]{:S(2)}) copy-start(bf16[128,16]{0,1:T(8,128)(2,1)} %param.43) | copy-start | bytes 12292
  82.6 8.6 %copy-start.27 = (f32[128]{0:T(128)S(1)}, f32[128]{0:T(128)}, u32[]{:S(2)}) copy-start(f32[128]{0:T(128)} %param.42) | copy-start | bytes 1540
  82.7 62.8 %all-gather.5.cloned.1.call-start = ((), (), s32[]{:S(2)}) async-start(), calls=%async_computation.1 | async-start | bytes 2621440 | tf_op jit(solution)/shard_map/all_gather | solution.py:133
  82.9 3.5 %copy-start.2 = (bf16[128,128,128]{2,1,0:T(8,128)(2,1)S(1)}, bf16[128,128,128]{2,1,0:T(8,128)(2,1)}, u32[]{:S(2)}) copy-start(bf16[128,128,128]{2,1,0:T(8,128)(2,1)} %param.31) | copy-start | bytes 12582916
  91.3 6.9 %copy-start.21 = (s32[512]{0:T(512)S(1)}, s32[512]{0:T(512)}, u32[]{:S(2)}) copy-start(s32[512]{0:T(512)} %param.35) | copy-start | bytes 6148
  91.3 6.9 %slice-start = ((bf16[128,2304]{1,0:T(8,128)(2,1)}), bf16[128,768]{1,0:T(8,128)(2,1)S(1)}, s32[]{:S(2)}) async-start(bf16[128,2304]{1,0:T(8,128)(2,1)} %copy-done.7), calls=%async_computation.2 | async-start | bytes 393216 | tf_op jit(solution)/shard_map/slice | solution.py:171
  98.1 50.6 %copy-start.23 = (pred[512]{0:T(512)(128)(4,1)}, pred[512]{0:T(512)(128)(4,1)S(1)}, u32[]{:S(2)}) copy-start(pred[512]{0:T(512)(128)(4,1)S(1)} %broadcast_compare_fusion.1) | copy-start | bytes 1540
  98.3 50.4 %copy-start.14 = (bf16[128,768]{0,1:T(8,128)(2,1)}, bf16[128,768]{0,1:T(8,128)(2,1)S(1)}, u32[]{:S(2)}) copy-start(bf16[128,768]{0,1:T(8,128)(2,1)S(1)} %copy.82) | copy-start | bytes 589828
  148.8 4.5 %copy-start.6 = (f32[128,768]{1,0:T(8,128)S(1)}, f32[128,768]{1,0:T(8,128)}, u32[]{:S(2)}) copy-start(f32[128,768]{1,0:T(8,128)} %get-tuple-element.50) | copy-start | bytes 1179652
  148.8 4.5 %copy-start.11 = (bf16[768,768]{1,0:T(8,128)(2,1)S(1)}, bf16[768,768]{1,0:T(8,128)(2,1)}, u32[]{:S(2)}) copy-start(bf16[768,768]{1,0:T(8,128)(2,1)} %param.46) | copy-start | bytes 3538948
  154.7 3.5 %copy-start.24 = (bf16[1536,768]{1,0:T(8,128)(2,1)S(1)}, bf16[1536,768]{1,0:T(8,128)(2,1)}, u32[]{:S(2)}) copy-start(bf16[1536,768]{1,0:T(8,128)(2,1)} %param.48) | copy-start | bytes 7077892
  158.2 1.0 copy-start.9
  158.2 1.1 copy-start.12
  158.2 2.0 copy-start.22
  158.2 11.5 %copy-start.15 = (bf16[2,128,384]{2,1,0:T(8,128)(2,1)S(1)}, bf16[2,128,384]{2,1,0:T(8,128)(2,1)}, u32[]{:S(2)}) copy-start(bf16[2,128,384]{2,1,0:T(8,128)(2,1)} %param.38) | copy-start | bytes 589828
  159.3 10.9 %copy-start.13 = (bf16[128,768]{1,0:T(8,128)(2,1)}, bf16[128,768]{1,0:T(8,128)(2,1)S(1)}, u32[]{:S(2)}) copy-start(bf16[128,768]{1,0:T(8,128)(2,1)S(1)} %fusion.41) | copy-start | bytes 589828
  159.8 5.8 %copy-start.4 = (f32[1024,128]{1,0:T(8,128)}, f32[1024,128]{1,0:T(8,128)S(1)}, u32[]{:S(2)}) copy-start(f32[1024,128]{1,0:T(8,128)S(1)} %get-tuple-element.54) | copy-start | bytes 1572868
  160.6 5.0 %collective-permute-start.2 = (bf16[96,128]{1,0:T(8,128)(2,1)S(1)}, bf16[96,128]{1,0:T(8,128)(2,1)S(1)}, u32[]{:S(2)}, u32[]{:S(2)}) collective-permute-start(bf16[96,128]{1,0:T(8,128)(2,1)S(1)} %get-tuple-element.30), channel_id=1, source_target_pairs={{0,1},{1,2},{2,3},{4,5},{5,6},{6,7},{8,9},{9,10},{10,11},{12,13},{... | collective-permute-start | bytes 73736 | tf_op jit(solution)/shard_map/ppermute | solution.py:28
  164.0 5.7 %collective-permute-start.3 = (bf16[96,128]{1,0:T(8,128)(2,1)S(1)}, bf16[96,128]{1,0:T(8,128)(2,1)S(1)}, u32[]{:S(2)}, u32[]{:S(2)}) collective-permute-start(bf16[96,128]{1,0:T(8,128)(2,1)S(1)} %get-tuple-element.31), channel_id=1, source_target_pairs={{1,0},{2,1},{3,2},{5,4},{6,5},{7,6},{9,8},{10,9},{11,10},{13,12},{... | collective-permute-start | bytes 73736 | tf_op jit(solution)/shard_map/ppermute | solution.py:31
  177.6 4.3 %copy-start.5 = (bf16[32,224,128]{2,1,0:T(8,128)(2,1)S(1)}, bf16[32,224,128]{2,1,0:T(8,128)(2,1)}, u32[]{:S(2)}) copy-start(bf16[32,224,128]{2,1,0:T(8,128)(2,1)} %get-tuple-element.11) | copy-start | bytes 5505028
  184.9 12.2 %copy-start.1 = (bf16[768,2304]{1,0:T(8,128)(2,1)S(1)}, bf16[768,2304]{1,0:T(8,128)(2,1)}, u32[]{:S(2)}) copy-start(bf16[768,2304]{1,0:T(8,128)(2,1)} %param.45) | copy-start | bytes 10616836
  188.7 6.6 %copy-start.16 = (f32[1,3,1024]{2,0,1:T(1,128)S(1)}, f32[1,3,1024]{2,0,1:T(1,128)}, u32[]{:S(2)}) copy-start(f32[1,3,1024]{2,0,1:T(1,128)} %param.27) | copy-start | bytes 36868
  188.7 6.6 %copy-start.26 = (bf16[3,128]{1,0:T(4,128)(2,1)S(1)}, bf16[3,128]{1,0:T(4,128)(2,1)}, u32[]{:S(2)}) copy-start(bf16[3,128]{1,0:T(4,128)(2,1)} %param.51) | copy-start | bytes 2308
  (3 other events, 2.1 us)
Sparse Core Ops, SparseCore 0:
  82.8 39.3 all-gather.2
  123.7 21.6 all-gather.4
where the time goes:
time: 205 us; the launch traced here: 204 us
  local copies, waits for them, and re-layouts  56.3 us (27%)
  waiting for transfers between devices  49.2 us (24%)
  matrix products  41.6 us (20%)
  other arithmetic  29 us (14%)
  between operations  15.9 us (8%)
  starting transfers between devices  12 us (6%)
    all_gather x1, waiting for transfers between devices, per_device(): gathered = lax.all_gather(projected[:, D:], 'row', axis=0, tiled=True)  23.8 us
    all_gather x1, waiting for transfers between devices, per_device(): lax.all_gather(pair_bias_of(pair_cond, pair_gain, pair_heads), 'smp', axi...  21.2 us
    slice x4, local copies, waits for them, and re-layouts, window_attend(): windows[:, :, :CA].reshape(block_count, span_rows, AHEADS, head_size)  12.1 us
    sub x2, other arithmetic, softmax_rows(): exponent = jnp.exp(scores - largest)  10.7 us
    another operation x10, local copies, waits for them, and re-layouts, block_spans(): jnp.stack(pieces, axis=1)  10.6 us
    ppermute x2, starting transfers between devices, with_halo(): lax.ppermute(lax.slice_in_dim(block, block.shape[dim] - width, None, axis...  8.92 us
    reduce_sum x6, other arithmetic, layer_norm(): variance = jnp.mean(centred * centred, axis=-1, keepdims=True)  7.22 us
    slice x2, local copies, waits for them, and re-layouts, window_attend(): windows[:, :, CA:].reshape(block_count, span_rows, AHEADS, head_size)  7.01 us
  transfers between devices with their start and end apart: 6, of which 3 were waited for; matrix products, arithmetic and copies ran while one was open for 19% of the time, Pallas kernels for 0%

commit v1 on v0

v1 whole, which is shorter than its diff:
```python
import functools
import math

import jax
import jax.numpy as jnp
from jax import lax
from jax.experimental import pallas as pl
from jax.experimental.pallas import tpu as pltpu
from jax.sharding import PartitionSpec as P

HEADS = 16
AHEADS = 4
WQ = 32
WK = 128
HALO = 96
LANES = 128

sigma_data = 16.0
gamma_boost = 0.8
norm_eps = 1e-05
masked_score = -1e30
LOG2E = math.log2(math.e)
F32 = jnp.float32
BF16 = jnp.bfloat16
NT = (((1,), (1,)), ((), ()))
TN = (((0,), (0,)), ((), ()))


def vmem(mib):
    return pltpu.CompilerParams(vmem_limit_bytes=mib * 1024 * 1024)


def whole(count):
    return [pl.BlockSpec(memory_space=pltpu.VMEM)] * count


def dot(a, b, dims=(((1,), (0,)), ((), ()))):
    return lax.dot_general(a, b, dims, preferred_element_type=F32)


def norm_rows(values, gain):
    average = jnp.mean(values, axis=-1, keepdims=True)
    centred = values - average
    variance = jnp.mean(centred * centred, axis=-1, keepdims=True)
    return centred * lax.rsqrt(variance + norm_eps) * gain


def noisy_of(level, coords, kicks):
    level_hat = (1.0 + gamma_boost) * level
    noisy = coords + jnp.sqrt(level_hat * level_hat - level * level) * kicks
    return level_hat, noisy


def column_of(row):
    size = row.shape[1]
    down = lax.broadcasted_iota(jnp.int32, (size, size), 0)
    across = lax.broadcasted_iota(jnp.int32, (size, size), 1)
    spread = jnp.where(down == across, jnp.broadcast_to(row, (size, size)), 0.0)
    return dot(spread.astype(BF16), jnp.ones((size, LANES), BF16))


def prepare_kernel(level_ref, coords_ref, kicks_ref, single_ref, coord_in_ref, gain_ref, state_ref, normed_ref):
    level_hat, noisy = noisy_of(level_ref[...], coords_ref[0], kicks_ref[0])
    scaled = noisy / jnp.sqrt(level_hat * level_hat + sigma_data * sigma_data)
    embedded = lax.dot_general(
        scaled, coord_in_ref[...], TN, precision=lax.Precision.HIGHEST, preferred_element_type=F32
    )
    state = single_ref[...].astype(F32) + embedded
    state_ref[...] = state
    normed_ref[...] = norm_rows(state, gain_ref[0:1]).astype(BF16)


def pair_kernel(tile_ref, gain_ref, heads_ref, bias_ref):
    rows, keys, channels = tile_ref.shape
    head_count = heads_ref.shape[0]
    weights = heads_ref[...].astype(F32) * gain_ref[...]
    high = weights.astype(BF16)
    low = (weights - high.astype(F32)).astype(BF16)
    total = jnp.sum(high.astype(F32) + low.astype(F32), axis=1, keepdims=True)
    ones = jnp.ones((head_count, channels), BF16)
    left = jnp.concatenate([high, low, ones], axis=0)
    tile = tile_ref[...].reshape(rows * keys, channels)
    wide = tile.astype(F32)
    square = wide * wide
    square_high = square.astype(BF16)
    square_low = (square - square_high.astype(F32)).astype(BF16)
    sums = dot(left, tile, NT)
    squares = dot(ones, square_high, NT) + dot(ones, square_low, NT)
    average = sums[2 * head_count :] / channels
    variance = jnp.maximum(squares / channels - average * average, 0.0)
    raw = sums[:head_count] + sums[head_count : 2 * head_count]
    result = (raw - average * total) * lax.rsqrt(variance + norm_eps)
    pieces = [result[:, i * keys : (i + 1) * keys] for i in range(rows)]
    stacked = jnp.stack(pieces, axis=1)
    bias_ref[...] = stacked.astype(BF16)


def window_block(
    first, last, state, low_ref, mid_ref, high_ref, gain_unused, w_qkv, w_out, offsets_ref, mask_ref, first_chunk, scratch
):
    key_scr, value_scr, live_scr, score_scr, prob_scr, out_scr = scratch
    row_count = state.shape[0]
    width = state.shape[1]
    block_count = row_count // WQ
    head_size = width // AHEADS
    low = jnp.where(first, jnp.zeros_like(low_ref[...]), low_ref[...])
    high = jnp.where(last, jnp.zeros_like(high_ref[...]), high_ref[...])
    mid = mid_ref[...]
    w_kv = w_qkv[:, width:]
    for start, part in ((0, low), (HALO, mid), (HALO + row_count, high)):
        projected = dot(part, w_kv).astype(BF16).astype(F32)
        key_scr[start : start + part.shape[0], :] = projected[:, :width]
        value_scr[start : start + part.shape[0], :] = projected[:, width:]
    queries = dot(mid, w_qkv[:, :width]).astype(BF16)

    chunk_count = row_count // LANES
    outside = -1e30
    edge = column_of(mask_ref[pl.ds(jnp.maximum(first_chunk - 1, 0), 1), :].astype(F32))
    edge = jnp.where(first, 0.0, edge)
    live_scr[0:HALO, :] = (edge[LANES - HALO :] - 1.0) * -outside
    for chunk in range(chunk_count):
        column = column_of(mask_ref[pl.ds(first_chunk + chunk, 1), :].astype(F32))
        begin = HALO + chunk * LANES
        live_scr[begin : begin + LANES, :] = (column - 1.0) * -outside
    final = mask_ref.shape[0] - 1
    edge = column_of(mask_ref[pl.ds(jnp.minimum(first_chunk + chunk_count, final), 1), :].astype(F32))
    edge = jnp.where(last, 0.0, edge)
    live_scr[HALO + row_count :, :] = (edge[:HALO] - 1.0) * -outside

    stacked_rows = AHEADS * WQ
    lane = lax.broadcasted_iota(jnp.int32, (stacked_rows, width), 1)
    line = lax.broadcasted_iota(jnp.int32, (stacked_rows, width), 0)
    own_head = lane // head_size == line // WQ
    pick = jnp.where(lane == 0, 1.0, 0.0).astype(BF16)
    ones = jnp.ones((WK, width), BF16)
    begins = []
    for b in range(block_count):
        begin = b * WQ + HALO + offsets_ref[b]
        begins.append(begin)
        keys = key_scr[pl.ds(begin, WK), :].astype(BF16)
        live = live_scr[pl.ds(begin, WK), :].astype(BF16)
        query = queries[b * WQ : (b + 1) * WQ]
        query = jnp.concatenate([query] * AHEADS, axis=0)
        query = jnp.where(own_head, query, jnp.zeros_like(query))
        score_scr[b * stacked_rows : (b + 1) * stacked_rows, :] = dot(
            jnp.concatenate([query, pick], axis=1), jnp.concatenate([keys, live], axis=1), NT
        )
    factor = LOG2E / math.sqrt(head_size)
    step = 4 * stacked_rows
    for begin in range(0, block_count * stacked_rows, step):
        scores = score_scr[begin : begin + step, :]
        largest = jnp.max(scores, axis=-1, keepdims=True)
        prob_scr[begin : begin + step, :] = jnp.exp2((scores - largest) * factor).astype(BF16)
    for b in range(block_count):
        values = value_scr[pl.ds(begins[b], WK), :].astype(BF16)
        probs = prob_scr[b * stacked_rows : (b + 1) * stacked_rows, :]
        both = dot(probs, jnp.concatenate([values, ones], axis=1))
        mixed = jnp.where(own_head, both[:, :width], 0.0)
        weight = jnp.where(own_head, both[:, width:], 0.0)
        mixed = sum(mixed[h * WQ : (h + 1) * WQ] for h in range(AHEADS))
        weight = sum(weight[h * WQ : (h + 1) * WQ] for h in range(AHEADS))
        out_scr[b * WQ : (b + 1) * WQ, :] = (mixed / weight).astype(BF16)
    return state + dot(out_scr[...], w_out)


def window_scratch(row_count, width):
    extended = row_count + 2 * HALO
    scores = row_count * AHEADS
    return [
        pltpu.VMEM((extended, width), F32),
        pltpu.VMEM((extended, width), F32),
        pltpu.VMEM((extended, LANES), F32),
        pltpu.VMEM((scores, WK), F32),
        pltpu.VMEM((scores, WK), BF16),
        pltpu.VMEM((row_count, width), BF16),
    ]


def member_of(token_ref, mask_ref, first_chunk, base, tok_rows):
    chunk_count = token_ref.shape[0]
    tokens = lax.broadcasted_iota(jnp.int32, (tok_rows, LANES), 0)
    pieces = []
    for chunk in range(chunk_count):
        local = token_ref[chunk : chunk + 1, :] - base
        valid = mask_ref[pl.ds(first_chunk + chunk, 1), :]
        local = jnp.where(valid > 0, local, -1)
        pieces.append(jnp.where(local == tokens, 1.0, 0.0).astype(BF16))
    return jnp.concatenate(pieces, axis=1)


def encoder_kernel(
    place_ref, offsets_ref, level_ref, state_ref, low_ref, mid_ref, high_ref, mask_ref, token_ref, w_qkv_ref, w_out_ref,
    lift_ref, single_ref, embed_ref, gain_ref, encoded_ref, token_state_ref, normed_ref, *scratch
):
    row, count = place_ref[0], place_ref[1]
    tok_rows = single_ref.shape[0]
    chunk_count = token_ref.shape[0]
    first_chunk = row * chunk_count
    state = window_block(
        row == 0, row == count - 1, state_ref[...], low_ref, mid_ref, high_ref, None,
        w_qkv_ref[0], w_out_ref[0], offsets_ref, mask_ref, first_chunk, scratch,
    )
    encoded_ref[...] = state
    lifted = jnp.maximum(dot(state.astype(BF16), lift_ref[...]), 0.0).astype(BF16)
    member = member_of(token_ref, mask_ref, first_chunk, row * tok_rows, tok_rows)
    counts = jnp.maximum(dot(member, jnp.ones((member.shape[1], LANES), BF16)), 1.0)
    pooled = dot(member, lifted) / counts[:, 0:1]
    level_hat = (1.0 + gamma_boost) * level_ref[...]
    token_state = (
        pooled + single_ref[...].astype(F32) + jnp.log(level_hat / sigma_data) / 4.0 * embed_ref[...]
    )
    token_state_ref[...] = token_state
    normed_ref[...] = norm_rows(token_state, gain_ref[0:1]).astype(BF16)


def token_kernel(row_count, smp_count, *refs):
    place_ref = refs[0]
    normed_refs = refs[1 : 1 + row_count]
    bias_refs = refs[1 + row_count : 1 + row_count + smp_count]
    (
        state_ref, key_mask_ref, w_qkv_ref, w_proj_ref, gain_ref, ffn_in_ref, ffn_out_ref, spread_ref,
        encoded_ref, mask_ref, token_ref, atom_gain_ref, out_ref, joined_ref, atom_normed_ref, kv_scr, score_scr, mixed_scr,
    ) = refs[1 + row_count + smp_count :]
    row, smp = place_ref[0], place_ref[2]
    tok_rows, width = state_ref.shape
    head_size = width // HEADS
    piece = bias_refs[0].shape[2]
    for d in range(row_count):
        begin = pl.multiple_of((row ^ d) * tok_rows, tok_rows)
        kv_scr[pl.ds(begin, tok_rows), :] = dot(normed_refs[d][...], w_qkv_ref[:, width:]).astype(BF16)
    queries = dot(normed_refs[0][...], w_qkv_ref[:, :width]).astype(BF16)
    scale = 1.0 / math.sqrt(head_size)
    spans = []
    for h in range(HEADS):
        begin = h * head_size // LANES * LANES
        end = -(-(h + 1) * head_size // LANES) * LANES
        spans.append((begin, end))
    order = []
    for d in range(smp_count):
        other = smp ^ d
        order.append(pl.multiple_of(other * piece, piece))
        live = key_mask_ref[pl.ds(other, 1), :] > 0
        for h in range(HEADS):
            begin, end = spans[h]
            lane = lax.broadcasted_iota(jnp.int32, (tok_rows, end - begin), 1) + begin
            query = queries[:, begin:end]
            query = jnp.where((lane >= h * head_size) & (lane < (h + 1) * head_size), query, jnp.zeros_like(query))
            keys = kv_scr[pl.ds(order[d], piece), begin:end]
            scores = dot(query, keys, NT) * scale + bias_refs[d][h].astype(F32)
            score_scr[d, h] = jnp.where(live, scores, masked_score)
    mixed_scr[...] = jnp.zeros_like(mixed_scr)
    for h in range(HEADS):
        begin, end = spans[h]
        scores = [score_scr[d, h] for d in range(smp_count)]
        largest = jnp.max(functools.reduce(jnp.maximum, scores), axis=-1, keepdims=True)
        exponents = [jnp.exp2((part - largest) * LOG2E) for part in scores]
        total = jnp.sum(functools.reduce(jnp.add, exponents), axis=-1, keepdims=True)
        mixed = functools.reduce(
            jnp.add,
            [
                dot(exponents[d].astype(BF16), kv_scr[pl.ds(order[d], piece), width + begin : width + end])
                for d in range(smp_count)
            ],
        )
        lane = lax.broadcasted_iota(jnp.int32, (tok_rows, end - begin), 1) + begin
        inside = (lane >= h * head_size) & (lane < (h + 1) * head_size)
        mixed_scr[:, begin:end] += jnp.where(inside, mixed / total, 0.0)
    state = state_ref[...] + dot(mixed_scr[...].astype(BF16), w_proj_ref[...])
    normed = norm_rows(state, gain_ref[1:2]).astype(BF16)
    hidden = dot(normed, ffn_in_ref[...])
    half = hidden.shape[1] // 2
    gate, up = hidden[:, :half], hidden[:, half:]
    active = (gate / (1.0 + jnp.exp(-gate)) * up).astype(BF16)
    state = state + dot(active, ffn_out_ref[...])
    result = state.astype(BF16)
    out_ref[0] = result
    spread = dot(result, spread_ref[...]).astype(BF16)
    chunk_count = token_ref.shape[0]
    member = member_of(token_ref, mask_ref, row * chunk_count, row * tok_rows, tok_rows)
    joined = encoded_ref[...] + dot(member, spread, TN)
    joined_ref[...] = joined
    atom_normed_ref[...] = norm_rows(joined, atom_gain_ref[1:2]).astype(BF16)


def decoder_kernel(
    place_ref, offsets_ref, level_ref, coords_ref, kicks_ref, state_ref, low_ref, mid_ref, high_ref, mask_ref,
    w_qkv_ref, w_out_ref, gain_ref, coord_out_ref, direction_ref, *scratch
):
    row, count = place_ref[0], place_ref[1]
    chunk_count = state_ref.shape[0] // LANES
    state = window_block(
        row == 0, row == count - 1, state_ref[...], low_ref, mid_ref, high_ref, None,
        w_qkv_ref[1], w_out_ref[1], offsets_ref, mask_ref, row * chunk_count, scratch,
    )
    normed = norm_rows(state, gain_ref[...]).astype(BF16)
    update = dot(coord_out_ref[...], normed, NT)
    level_hat, noisy = noisy_of(level_ref[...], coords_ref[0], kicks_ref[0])
    base_square = sigma_data * sigma_data + level_hat * level_hat
    skip_scale = sigma_data * sigma_data / base_square
    out_scale = level_hat * sigma_data / jnp.sqrt(base_square)
    denoised = skip_scale * noisy + out_scale * update
    direction_ref[0] = (noisy - denoised) / level_hat


def halos_of(normed):
    count = lax.axis_size("row")
    up = [(i, (i + 1) % count) for i in range(count)]
    down = [((i + 1) % count, i) for i in range(count)]
    low = lax.ppermute(normed[normed.shape[0] - HALO :], "row", up)
    high = lax.ppermute(normed[:HALO], "row", down)
    return low, high


def spread_over(block, axis):
    count = lax.axis_size(axis)
    found = [block]
    bits = []
    bit = count // 2
    have = {0: block}
    while bit:
        pairs = [(i, i ^ bit) for i in range(count)]
        for d in list(have):
            have[d | bit] = lax.ppermute(have[d], axis, pairs)
        bit //= 2
    return [have[d] for d in range(count)]


def per_device(
    positions,
    noise_draw,
    noise_level,
    atom_single,
    token_single,
    pair_cond,
    atom_to_token,
    window_offsets,
    atom_mask,
    token_mask,
    coord_in,
    atom_gain,
    atom_qkv,
    atom_proj,
    gather_in,
    noise_embed,
    pair_gain,
    pair_heads,
    token_gain,
    token_qkv,
    token_proj,
    ffn_in,
    ffn_out,
    scatter_out,
    out_gain,
    coord_out,
):
    row_count, smp_count = lax.axis_size("row"), lax.axis_size("smp")
    atoms, width = atom_single.shape
    tok_rows, token_width = token_single.shape
    heads = pair_heads.shape[1]
    keys = pair_cond.shape[1]
    place = jnp.stack(
        [lax.axis_index("row"), jnp.int32(row_count), lax.axis_index("smp")]
    ).astype(jnp.int32)
    level = noise_level.reshape(1, 1)
    mask = atom_mask.reshape(-1, LANES)
    tokens = atom_to_token.reshape(-1, LANES)
    smem = pl.BlockSpec(memory_space=pltpu.SMEM)
    shape = jax.ShapeDtypeStruct

    state, normed = pl.pallas_call(
        prepare_kernel,
        out_shape=(shape((atoms, width), F32), shape((atoms, width), BF16)),
        in_specs=whole(6),
        out_specs=tuple(whole(2)),
        compiler_params=vmem(32),
    )(level, positions, noise_draw, atom_single, coord_in, atom_gain)
    low, high = halos_of(normed)

    pair_rows = 16
    bias = pl.pallas_call(
        pair_kernel,
        grid=(pair_cond.shape[0] // pair_rows,),
        out_shape=shape((heads, pair_cond.shape[0], keys), BF16),
        in_specs=[
            pl.BlockSpec((pair_rows, keys, pair_cond.shape[2]), lambda i: (i, 0, 0)),
            pl.BlockSpec((1, pair_cond.shape[2]), lambda i: (0, 0)),
            pl.BlockSpec((heads, pair_cond.shape[2]), lambda i: (0, 0)),
        ],
        out_specs=pl.BlockSpec((heads, pair_rows, keys), lambda i: (0, i, 0)),
        compiler_params=vmem(32),
    )(pair_cond, pair_gain.reshape(1, -1), pair_heads.T)
    biases = spread_over(bias, "smp")

    encoded, token_state, token_normed = pl.pallas_call(
        encoder_kernel,
        out_shape=(
            shape((atoms, width), F32),
            shape((tok_rows, token_width), F32),
            shape((tok_rows, token_width), BF16),
        ),
        in_specs=[smem, smem] + whole(13),
        out_specs=tuple(whole(3)),
        scratch_shapes=window_scratch(atoms, width),
        compiler_params=vmem(40),
    )(
        place, window_offsets, level, state, low, normed, high, mask, tokens, atom_qkv, atom_proj, gather_in,
        token_single, noise_embed.reshape(1, -1), token_gain,
    )
    gathered = spread_over(token_normed, "row")

    key_mask = token_mask.reshape(-1, keys)
    token_result, joined, atom_normed = pl.pallas_call(
        functools.partial(token_kernel, row_count, smp_count),
        out_shape=(
            shape((1, tok_rows, token_width), BF16),
            shape((atoms, width), F32),
            shape((atoms, width), BF16),
        ),
        in_specs=[smem] + whole(row_count + smp_count + 12),
        out_specs=tuple(whole(3)),
        scratch_shapes=[
            pltpu.VMEM((token_mask.shape[0], 2 * token_width), BF16),
            pltpu.VMEM((smp_count, heads, tok_rows, keys), F32),
            pltpu.VMEM((tok_rows, token_width), F32),
        ],
        compiler_params=vmem(56),
    )(
        place, *gathered, *biases, token_state, key_mask, token_qkv, token_proj, token_gain, ffn_in, ffn_out,
        scatter_out, encoded, mask, tokens, atom_gain,
    )
    low, high = halos_of(atom_normed)

    direction = pl.pallas_call(
        decoder_kernel,
        out_shape=shape((1,) + positions.shape[1:], F32),
        in_specs=[smem, smem] + whole(12),
        out_specs=whole(1)[0],
        scratch_shapes=window_scratch(atoms, width),
        compiler_params=vmem(40),
    )(
        place, window_offsets, level, positions, noise_draw, joined, low, atom_normed, high, mask, atom_qkv, atom_proj,
        out_gain.reshape(1, -1), coord_out,
    )
    return (token_result, direction)


def solution(mesh):
    in_specs = (
        P(("grp", "smp"), None, "row"),
        P(("grp", "smp"), None, "row"),
        P(("grp", "smp")),
        P(("grp", "row"), None),
        P(("grp", "row"), None),
        P(("grp", "row"), "smp", None),
        P(("grp", "row")),
        P(("grp", "row")),
        P("grp"),
        P("grp"),
        P(),
        P(),
        P(),
        P(),
        P(),
        P(),
        P(),
        P(),
        P(),
        P(),
        P(),
        P(),
        P(),
        P(),
        P(),
        P(),
    )
    out_specs = (P(("grp", "smp"), "row", None), P(("grp", "smp"), None, "row"))
    return jax.shard_map(
        per_device, mesh=mesh, in_specs=in_specs, out_specs=out_specs, check_vma=False
    )
```

time: 205 us -> 82.6 us (0.40)
  local copies, waits for them, and re-layouts: 56.3 us -> 10 us
  matrix products: 41.6 us -> 0 us
  other arithmetic: 29 us -> 0.08 us
  Pallas kernels: 0 us -> 25.1 us
  between operations: 15.9 us -> 1.61 us
  waiting for transfers between devices: 49.2 us -> 35.9 us
  starting transfers between devices: 12 us -> 9.52 us
    all_gather x2 -> x0, waiting for transfers between devices: 45 us -> none  [the longest x1 23.8 us: per_device(): gathered = lax.all_gather(projected[:, D:], 'row', axis=0, tiled=True)]
    dot_general x18 -> x0, matrix products: 38.3 us -> none  [the longest x1 5.85 us: pair_bias_of(): jnp.einsum('ijc,ch->hij', normed, pair_heads, preferred_element_type=jnp....]
    ppermute x4 -> x10, waiting for transfers between devices: 4.1 us -> 35.9 us  [the longest x6 25.4 us: spread_over(): have[d | bit] = lax.ppermute(have[d], axis, pairs)]
    slice x21 -> x2, local copies, waits for them, and re-layouts: 26.4 us -> 0.76 us  [halos_of(): high = lax.ppermute(normed[:HALO], 'row', down)]
    pallas_call x0 -> x5, Pallas kernels: none -> 25.1 us  [the longest x1 12.6 us: per_device(): pl.pallas_call(functools.partial(token_kernel, row_count, smp_count), out...]
    sub x3 -> x0, other arithmetic: 11.4 us -> none  [the longest x2 10.7 us: softmax_rows(): exponent = jnp.exp(scores - largest)]
    reduce_sum x8 -> x0, other arithmetic: 10.9 us -> none  [the longest x6 7.22 us: layer_norm(): variance = jnp.mean(centred * centred, axis=-1, keepdims=True)]
    another operation x10 -> x0, local copies, waits for them, and re-layouts: 10.6 us -> none  [block_spans(): jnp.stack(pieces, axis=1)]
  transfers between devices with their start and end apart: 6 -> 10, of which waited for: 3 -> 8; matrix products, arithmetic and copies ran while one was open for 19% -> 0% of each run, Pallas kernels for 0% -> 5%
where the time goes in v1:
time: 82.6 us; the launch traced here: 82.2 us
  waiting for transfers between devices  35.9 us (43%)
  Pallas kernels  25.1 us (30%)
  local copies, waits for them, and re-layouts  10 us (12%)
  starting transfers between devices  9.52 us (12%)
  between operations  1.61 us (2%)
    ppermute x6, waiting for transfers between devices, spread_over(): have[d | bit] = lax.ppermute(have[d], axis, pairs)  25.4 us
    pallas_call x1, Pallas kernels, per_device(): pl.pallas_call(functools.partial(token_kernel, row_count, smp_count), out...  12.6 us
    unnamed x69, local copies, waits for them, and re-layouts  9.28 us
    ppermute x2, waiting for transfers between devices, halos_of(): low = lax.ppermute(normed[normed.shape[0] - HALO:], 'row', up)  7.16 us
    ppermute x2, starting transfers between devices, halos_of(): high = lax.ppermute(normed[:HALO], 'row', down)  5.23 us
    pallas_call x1, Pallas kernels, per_device(): pl.pallas_call(pair_kernel, grid=(pair_cond.shape[0] // pair_rows,), out_...  5.14 us
    ppermute x6, starting transfers between devices, spread_over(): have[d | bit] = lax.ppermute(have[d], axis, pairs)  3.58 us
    pallas_call x1, Pallas kernels, per_device(): pl.pallas_call(encoder_kernel, out_shape=(shape((atoms, width), F32), sha...  3.47 us
  transfers between devices with their start and end apart: 10, of which 8 were waited for; matrix products, arithmetic and copies ran while one was open for 0% of the time, Pallas kernels for 5%

profile of v1, /device:TPU:0, one launch (start us, length us, event | category | flops | bytes accessed | tf_op | source)
XLA Modules:
  0.0 82.2 jit_solution(5499994669921655253)
XLA Ops:
  0.6 0.0 copy-start.18
  0.7 2.2 %copy-done = bf16[128,128,128]{2,1,0:T(8,128)(2,1)S(1)} copy-done((bf16[128,128,128]{2,1,0:T(8,128)(2,1)S(1)}, bf16[128,128,128]{2,1,0:T(8,128)(2,1)}, u32[]{:S(2)}) %copy-start) | copy-done | bytes 4194328
  2.9 0.7 copy-done.19
  3.6 0.7 copy-done.23
  4.3 5.1 %shard_map.259.refs_5_ = bf16[16,128,128]{2,1,0:T(8,128)(2,1)S(1)} custom-call(bf16[128,128,128]{2,1,0:T(8,128)(2,1)S(1)} %copy-done, f32[1,128]{1,0:T(1,128)S(1)} %bitcast.18, bf16[16,128]{1,0:T(8,128)(2,1)S(1)} %bitcast.17), custom_call_target="tpu_custom_call" | custom-call | tf_op jit(solution)/shard_map/pallas_call | solution.py:380
  9.5 3.0 %collective-permute-start.6 = (bf16[16,128,128]{2,1,0:T(8,128)(2,1)S(1)}, bf16[16,128,128]{2,1,0:T(8,128)(2,1)S(1)}, u32[]{:S(2)}, u32[]{:S(2)}) collective-permute-start(bf16[16,128,128]{2,1,0:T(8,128)(2,1)S(1)} %shard_map.259.refs_5_), channel_id=1, source_target_pairs={{0,8},{4,12},{8,0},{12,4},{1,9},{5,13},{9,1},{13,5},{2,10},{6,14},... | collective-permute-start | bytes 1572872 | tf_op jit(solution)/shard_map/ppermute | solution.py:323
  13.2 1.0 %shard_map.257 = (f32[1024,128]{1,0:T(8,128)S(1)}, bf16[1024,128]{1,0:T(8,128)(2,1)S(1)}) custom-call(f32[1,1]{1,0:T(1,128)} %bitcast.9.level_ref, f32[1,3,1024]{2,1,0:T(4,128)S(1)} %copy.28.coords_ref, f32[1,3,1024]{2,1,0:T(4,128)S(1)} %copy.29.kicks_ref, bf16[1024,128]{1,0:T(8,128)(2,1)S(1)} %copy-done.7, f32[3,128]{1,0:T(4,128)S(1)} %copy-done.20, ...), custom_call_target="tpu_custom_call" | custom-call | tf_op jit(solution)/shard_map/pallas_call | solution.py:370
  14.2 10.2 %collective-permute-done.6.refs_7_ = bf16[16,128,128]{2,1,0:T(8,128)(2,1)S(1)} collective-permute-done((bf16[16,128,128]{2,1,0:T(8,128)(2,1)S(1)}, bf16[16,128,128]{2,1,0:T(8,128)(2,1)S(1)}, u32[]{:S(2)}, u32[]{:S(2)}) %collective-permute-start.6) | collective-permute-done | bytes 524320 | tf_op jit(solution)/shard_map/ppermute | solution.py:323
  24.4 3.9 %collective-permute-start.1 = (bf16[96,128]{1,0:T(8,128)(2,1)S(1)}, bf16[96,128]{1,0:T(8,128)(2,1)S(1)}, u32[]{:S(2)}, u32[]{:S(2)}) collective-permute-start(bf16[96,128]{1,0:T(8,128)(2,1)S(1)} %get-tuple-element.22), channel_id=1, source_target_pairs={{1,0},{2,1},{3,2},{0,3},{5,4},{6,5},{7,6},{4,7},{9,8},{10,9},{11,1... | collective-permute-start | bytes 73736 | tf_op jit(solution)/shard_map/ppermute | solution.py:310
  28.3 0.1 pad_add_fusion.place_ref.refs_0_
  28.4 1.4 %collective-permute-done.1.high_ref = bf16[96,128]{1,0:T(8,128)(2,1)S(1)} collective-permute-done((bf16[96,128]{1,0:T(8,128)(2,1)S(1)}, bf16[96,128]{1,0:T(8,128)(2,1)S(1)}, u32[]{:S(2)}, u32[]{:S(2)}) %collective-permute-start.1) | collective-permute-done | bytes 24608 | tf_op jit(solution)/shard_map/ppermute | solution.py:310
  29.8 4.1 %collective-permute-done.low_ref = bf16[96,128]{1,0:T(8,128)(2,1)S(1)} collective-permute-done((bf16[96,128]{1,0:T(8,128)(2,1)S(1)}, bf16[96,128]{1,0:T(8,128)(2,1)S(1)}, u32[]{:S(2)}, u32[]{:S(2)}) %collective-permute-start) | collective-permute-done | bytes 24608 | tf_op jit(solution)/shard_map/ppermute | solution.py:309
  34.0 3.5 %shard_map.258 = (f32[1024,128]{1,0:T(8,128)S(1)}, f32[128,768]{1,0:T(8,128)S(1)}, bf16[128,768]{1,0:T(8,128)(2,1)S(1)}) custom-call(s32[3]{0:T(128)S(1)} %pad_add_fusion.place_ref.refs_0_, s32[32]{0:T(128)S(1)} %copy-done.21, f32[1,1]{1,0:T(1,128)} %bitcast.10.level_ref, f32[1024,128]{1,0:T(8,128)S(1)} %get-tuple-element.10.state_ref, ...), custom_call_target="tpu_custom_call" | custom-call | tf_op jit(solution)/shard_map/pallas_call | solution.py:394
  37.5 0.8 copy-done.3
  38.3 0.7 copy-done.5
  39.0 0.6 collective-permute-start.2
  39.6 8.7 %collective-permute-done.3.refs_3_ = bf16[128,768]{1,0:T(8,128)(2,1)S(1)} collective-permute-done((bf16[128,768]{1,0:T(8,128)(2,1)S(1)}, bf16[128,768]{1,0:T(8,128)(2,1)S(1)}, u32[]{:S(2)}, u32[]{:S(2)}) %collective-permute-start.3) | collective-permute-done | bytes 196640 | tf_op jit(solution)/shard_map/ppermute | solution.py:323
  48.4 0.7 collective-permute-done.2.refs_2_
  49.1 5.7 %collective-permute-done.4.refs_4_ = bf16[128,768]{1,0:T(8,128)(2,1)S(1)} collective-permute-done((bf16[128,768]{1,0:T(8,128)(2,1)S(1)}, bf16[128,768]{1,0:T(8,128)(2,1)S(1)}, u32[]{:S(2)}, u32[]{:S(2)}) %collective-permute-start.4) | collective-permute-done | bytes 196640 | tf_op jit(solution)/shard_map/ppermute | solution.py:323
  54.9 0.6 copy-done.29
  55.5 0.2 copy-done.26
  55.7 12.6 %shard_map.260 = (bf16[1,128,768]{2,1,0:T(8,128)(2,1)}, f32[1024,128]{1,0:T(8,128)}, bf16[1024,128]{1,0:T(8,128)(2,1)}) custom-call(s32[3]{0:T(128)} %copy-done.16, bf16[128,768]{1,0:T(8,128)(2,1)} %copy-done.9, bf16[128,768]{1,0:T(8,128)(2,1)} %copy-done.28, bf16[128,768]{1,0:T(8,128)(2,1)} %copy-done.27, bf16[128,768]{1,0:T(8,128)(2,1)} %copy-done.29, ...), custom_call_target="tpu_custom_call" | custom-call | tf_op jit(solution)/shard_map/pallas_call | solution.py:412
  68.3 0.8 fusion
  69.1 1.3 %collective-permute-start.9 = (bf16[96,128]{1,0:T(8,128)(2,1)S(1)}, bf16[96,128]{1,0:T(8,128)(2,1)S(1)}, u32[]{:S(2)}, u32[]{:S(2)}) collective-permute-start(bf16[96,128]{1,0:T(8,128)(2,1)S(1)} %get-tuple-element.20), channel_id=1, source_target_pairs={{1,0},{2,1},{3,2},{0,3},{5,4},{6,5},{7,6},{4,7},{9,8},{10,9},{11,1... | collective-permute-start | bytes 73736 | tf_op jit(solution)/shard_map/ppermute | solution.py:310
  70.4 0.7 collective-permute-start.8
  71.1 1.9 %collective-permute-done.9.high_ref = bf16[96,128]{1,0:T(8,128)(2,1)S(1)} collective-permute-done((bf16[96,128]{1,0:T(8,128)(2,1)S(1)}, bf16[96,128]{1,0:T(8,128)(2,1)S(1)}, u32[]{:S(2)}, u32[]{:S(2)}) %collective-permute-start.9) | collective-permute-done | bytes 24608 | tf_op jit(solution)/shard_map/ppermute | solution.py:310
  73.0 3.1 %collective-permute-done.8.low_ref = bf16[96,128]{1,0:T(8,128)(2,1)S(1)} collective-permute-done((bf16[96,128]{1,0:T(8,128)(2,1)S(1)}, bf16[96,128]{1,0:T(8,128)(2,1)S(1)}, u32[]{:S(2)}, u32[]{:S(2)}) %collective-permute-start.8) | collective-permute-done | bytes 24608 | tf_op jit(solution)/shard_map/ppermute | solution.py:309
  76.1 1.0 %copy-done.4 = f32[1024,128]{1,0:T(8,128)S(1)} copy-done((f32[1024,128]{1,0:T(8,128)S(1)}, f32[1024,128]{1,0:T(8,128)}, u32[]{:S(2)}) %copy-start.4) | copy-done | bytes 524312
  77.1 0.9 %copy-done.6 = bf16[1024,128]{1,0:T(8,128)(2,1)S(1)} copy-done((bf16[1024,128]{1,0:T(8,128)(2,1)S(1)}, bf16[1024,128]{1,0:T(8,128)(2,1)}, u32[]{:S(2)}) %copy-start.6) | copy-done | bytes 262168
  78.0 0.7 copy-done.17
  78.7 2.9 %shard_map.261 = f32[1,3,1024]{2,1,0:T(4,128)S(1)} custom-call(s32[3]{0:T(128)S(1)} %copy-done.17, s32[32]{0:T(128)S(1)} %copy-done.21, f32[1,1]{1,0:T(1,128)} %bitcast.11.level_ref, f32[1,3,1024]{2,1,0:T(4,128)S(1)} %copy.28.coords_ref, f32[1,3,1024]{2,1,0:T(4,128)S(1)} %copy.29.kicks_ref, f32[1024,128]{1,0:T(8,128)S(1)} %copy-done.4, ...), custom_call_target="tpu_custom_call" | custom-call | tf_op jit(solution)/shard_map/pallas_call | solution.py:433
  81.6 0.6 copy.32
  (66 shorter events, 0.1 us)
Async XLA Ops:
  0.6 12.5 %copy-start.18 = (f32[2,128]{1,0:T(2,128)S(1)}, f32[2,128]{1,0:T(2,128)}, u32[]{:S(2)}) copy-start(f32[2,128]{1,0:T(2,128)} %refs_20_.1) | copy-start | bytes 3076
  0.6 12.5 %copy-start.20 = (f32[3,128]{1,0:T(4,128)S(1)}, f32[3,128]{1,0:T(4,128)}, u32[]{:S(2)}) copy-start(f32[3,128]{1,0:T(4,128)} %coord_in_ref.1) | copy-start | bytes 4612
  0.7 33.3 %copy-start.21 = (s32[32]{0:T(128)S(1)}, s32[32]{0:T(128)}, u32[]{:S(2)}) copy-start(s32[32]{0:T(128)} %offsets_ref.3) | copy-start | bytes 388
  4.2 8.9 %copy-start.30 = (f32[1,3,1024]{2,0,1:T(1,128)S(1)}, f32[1,3,1024]{2,0,1:T(1,128)}, u32[]{:S(2)}) copy-start(f32[1,3,1024]{2,0,1:T(1,128)} %param.26) | copy-start | bytes 36868
  4.2 8.9 %copy-start.31 = (f32[1,3,1024]{2,0,1:T(1,128)S(1)}, f32[1,3,1024]{2,0,1:T(1,128)}, u32[]{:S(2)}) copy-start(f32[1,3,1024]{2,0,1:T(1,128)} %param.27) | copy-start | bytes 36868
  4.2 9.0 %copy-start.7 = (bf16[1024,128]{1,0:T(8,128)(2,1)S(1)}, bf16[1024,128]{1,0:T(8,128)(2,1)}, u32[]{:S(2)}) copy-start(bf16[1024,128]{1,0:T(8,128)(2,1)} %single_ref.2) | copy-start | bytes 786436
  4.2 24.2 %copy-start.32 = (f32[768]{0:T(1024)S(1)}, f32[768]{0:T(1024)}, u32[]{:S(2)}) copy-start(f32[768]{0:T(1024)} %param.41) | copy-start | bytes 9220
  4.2 29.7 %copy-start.2 = (bf16[2,128,384]{2,1,0:T(8,128)(2,1)S(1)}, bf16[2,128,384]{2,1,0:T(8,128)(2,1)}, u32[]{:S(2)}) copy-start(bf16[2,128,384]{2,1,0:T(8,128)(2,1)} %w_qkv_ref.3) | copy-start | bytes 589828
  4.2 29.7 %copy-start.8 = (bf16[2,128,128]{2,1,0:T(8,128)(2,1)S(1)}, bf16[2,128,128]{2,1,0:T(8,128)(2,1)}, u32[]{:S(2)}) copy-start(bf16[2,128,128]{2,1,0:T(8,128)(2,1)} %w_out_ref.3) | copy-start | bytes 196612
  4.2 29.7 %copy-start.10 = (bf16[128,768]{1,0:T(8,128)(2,1)S(1)}, bf16[128,768]{1,0:T(8,128)(2,1)}, u32[]{:S(2)}) copy-start(bf16[128,768]{1,0:T(8,128)(2,1)} %lift_ref.1) | copy-start | bytes 589828
  4.3 29.7 %copy-start.11 = (bf16[128,768]{1,0:T(8,128)(2,1)S(1)}, bf16[128,768]{1,0:T(8,128)(2,1)}, u32[]{:S(2)}) copy-start(bf16[128,768]{1,0:T(8,128)(2,1)} %single_ref.3) | copy-start | bytes 589828
  4.3 29.7 %copy-start.12 = (s32[4096]{0:T(1024)S(1)}, s32[4096]{0:T(1024)}, u32[]{:S(2)}) copy-start(s32[4096]{0:T(1024)} %param.34) | copy-start | bytes 49156
  4.3 29.7 %copy-start.14 = (f32[2,768]{1,0:T(2,128)S(1)}, f32[2,768]{1,0:T(2,128)}, u32[]{:S(2)}) copy-start(f32[2,768]{1,0:T(2,128)} %refs_13_.1) | copy-start | bytes 18436
  4.3 29.7 %copy-start.15 = (s32[1024]{0:T(1024)S(1)}, s32[1024]{0:T(1024)}, u32[]{:S(2)}) copy-start(s32[1024]{0:T(1024)} %param.32) | copy-start | bytes 12292
  9.5 45.3 %copy-start.1 = (bf16[16,128,128]{2,1,0:T(8,128)(2,1)}, bf16[16,128,128]{2,1,0:T(8,128)(2,1)S(1)}, u32[]{:S(2)}) copy-start(bf16[16,128,128]{2,1,0:T(8,128)(2,1)S(1)} %shard_map.259.refs_5_) | copy-start | bytes 1572868
  9.5 14.9 %collective-permute-start.6 = (bf16[16,128,128]{2,1,0:T(8,128)(2,1)S(1)}, bf16[16,128,128]{2,1,0:T(8,128)(2,1)S(1)}, u32[]{:S(2)}, u32[]{:S(2)}) collective-permute-start(bf16[16,128,128]{2,1,0:T(8,128)(2,1)S(1)} %shard_map.259.refs_5_), channel_id=1, source_target_pairs={{0,8},{4,12},{8,0},{12,4},{1,9},{5,13},{9,1},{13,5},{2,10},{6,14},... | collective-permute-start | bytes 1572872 | tf_op jit(solution)/shard_map/ppermute | solution.py:323
  12.5 42.3 %collective-permute-start.5 = (bf16[16,128,128]{2,1,0:T(8,128)(2,1)S(1)}, bf16[16,128,128]{2,1,0:T(8,128)(2,1)S(1)}, u32[]{:S(2)}, u32[]{:S(2)}) collective-permute-start(bf16[16,128,128]{2,1,0:T(8,128)(2,1)S(1)} %shard_map.259.refs_5_), channel_id=1, source_target_pairs={{0,4},{4,0},{8,12},{12,8},{1,5},{5,1},{9,13},{13,9},{2,6},{6,2},{1... | collective-permute-start | bytes 1572872 | tf_op jit(solution)/shard_map/ppermute | solution.py:323
  24.4 30.4 %copy-start.25 = (bf16[16,128,128]{2,1,0:T(8,128)(2,1)}, bf16[16,128,128]{2,1,0:T(8,128)(2,1)S(1)}, u32[]{:S(2)}) copy-start(bf16[16,128,128]{2,1,0:T(8,128)(2,1)S(1)} %collective-permute-done.6.refs_7_) | copy-start | bytes 1572868
  24.4 30.4 %collective-permute-start.7 = (bf16[16,128,128]{2,1,0:T(8,128)(2,1)S(1)}, bf16[16,128,128]{2,1,0:T(8,128)(2,1)}, u32[]{:S(2)}, u32[]{:S(2)}) collective-permute-start(bf16[16,128,128]{2,1,0:T(8,128)(2,1)S(1)} %collective-permute-done.6.refs_7_), channel_id=1, source_target_pairs={{0,4},{4,0},{8,12},{12,8},{1,5},{5,1},{9,13},{13,9},{2,6},{6,2},{1... | collective-permute-start | bytes 1572872 | tf_op jit(solution)/shard_map/ppermute | solution.py:323
  24.4 5.4 %collective-permute-start.1 = (bf16[96,128]{1,0:T(8,128)(2,1)S(1)}, bf16[96,128]{1,0:T(8,128)(2,1)S(1)}, u32[]{:S(2)}, u32[]{:S(2)}) collective-permute-start(bf16[96,128]{1,0:T(8,128)(2,1)S(1)} %get-tuple-element.22), channel_id=1, source_target_pairs={{1,0},{2,1},{3,2},{0,3},{5,4},{6,5},{7,6},{4,7},{9,8},{10,9},{11,1... | collective-permute-start | bytes 73736 | tf_op jit(solution)/shard_map/ppermute | solution.py:310
  28.3 5.6 %collective-permute-start = (bf16[96,128]{1,0:T(8,128)(2,1)S(1)}, bf16[96,128]{1,0:T(8,128)(2,1)S(1)}, u32[]{:S(2)}, u32[]{:S(2)}) collective-permute-start(bf16[96,128]{1,0:T(8,128)(2,1)S(1)} %get-tuple-element.23), channel_id=1, source_target_pairs={{0,1},{1,2},{2,3},{3,0},{4,5},{5,6},{6,7},{7,4},{8,9},{9,10},{10,1... | collective-permute-start | bytes 73736 | tf_op jit(solution)/shard_map/ppermute | solution.py:309
  28.4 26.4 %copy-start.16 = (s32[3]{0:T(128)}, s32[3]{0:T(128)S(1)}, u32[]{:S(2)}) copy-start(s32[3]{0:T(128)S(1)} %pad_add_fusion.place_ref.refs_0_) | copy-start | bytes 40
  39.0 15.8 %copy-start.9 = (bf16[128,768]{1,0:T(8,128)(2,1)}, bf16[128,768]{1,0:T(8,128)(2,1)S(1)}, u32[]{:S(2)}) copy-start(bf16[128,768]{1,0:T(8,128)(2,1)S(1)} %get-tuple-element.12.refs_1_) | copy-start | bytes 589828
  39.0 9.3 %collective-permute-start.3 = (bf16[128,768]{1,0:T(8,128)(2,1)S(1)}, bf16[128,768]{1,0:T(8,128)(2,1)S(1)}, u32[]{:S(2)}, u32[]{:S(2)}) collective-permute-start(bf16[128,768]{1,0:T(8,128)(2,1)S(1)} %get-tuple-element.12.refs_1_), channel_id=1, source_target_pairs={{0,2},{1,3},{2,0},{3,1},{4,6},{5,7},{6,4},{7,5},{8,10},{9,11},{10,... | collective-permute-start | bytes 589832 | tf_op jit(solution)/shard_map/ppermute | solution.py:323
  39.0 10.0 %collective-permute-start.2 = (bf16[128,768]{1,0:T(8,128)(2,1)S(1)}, bf16[128,768]{1,0:T(8,128)(2,1)S(1)}, u32[]{:S(2)}, u32[]{:S(2)}) collective-permute-start(bf16[128,768]{1,0:T(8,128)(2,1)S(1)} %get-tuple-element.12.refs_1_), channel_id=1, source_target_pairs={{0,1},{1,0},{2,3},{3,2},{4,5},{5,4},{6,7},{7,6},{8,9},{9,8},{10,11... | collective-permute-start | bytes 589832 | tf_op jit(solution)/shard_map/ppermute | solution.py:323
  48.3 6.5 %copy-start.27 = (bf16[128,768]{1,0:T(8,128)(2,1)}, bf16[128,768]{1,0:T(8,128)(2,1)S(1)}, u32[]{:S(2)}) copy-start(bf16[128,768]{1,0:T(8,128)(2,1)S(1)} %collective-permute-done.3.refs_3_) | copy-start | bytes 589828
  48.4 6.4 %collective-permute-start.4 = (bf16[128,768]{1,0:T(8,128)(2,1)S(1)}, bf16[128,768]{1,0:T(8,128)(2,1)S(1)}, u32[]{:S(2)}, u32[]{:S(2)}) collective-permute-start(bf16[128,768]{1,0:T(8,128)(2,1)S(1)} %collective-permute-done.3.refs_3_), channel_id=1, source_target_pairs={{0,1},{1,0},{2,3},{3,2},{4,5},{5,4},{6,7},{7,6},{8,9},{9,8},{10,11... | collective-permute-start | bytes 589832 | tf_op jit(solution)/shard_map/ppermute | solution.py:323
  55.7 20.4 %copy-start.13 = (s32[4096]{0:T(1024)S(1)}, s32[4096]{0:T(1024)}, u32[]{:S(2)}) copy-start(s32[4096]{0:T(1024)} %param.34) | copy-start | bytes 49156
  55.7 20.4 %copy-start.22 = (bf16[3,128]{1,0:T(4,128)(2,1)S(1)}, bf16[3,128]{1,0:T(4,128)(2,1)}, u32[]{:S(2)}) copy-start(bf16[3,128]{1,0:T(4,128)(2,1)} %coord_out_ref.1) | copy-start | bytes 2308
  55.7 20.4 %copy-start.24 = (f32[128]{0:T(128)S(1)}, f32[128]{0:T(128)}, u32[]{:S(2)}) copy-start(f32[128]{0:T(128)} %param.50) | copy-start | bytes 1540
  69.1 3.9 %collective-permute-start.9 = (bf16[96,128]{1,0:T(8,128)(2,1)S(1)}, bf16[96,128]{1,0:T(8,128)(2,1)S(1)}, u32[]{:S(2)}, u32[]{:S(2)}) collective-permute-start(bf16[96,128]{1,0:T(8,128)(2,1)S(1)} %get-tuple-element.20), channel_id=1, source_target_pairs={{1,0},{2,1},{3,2},{0,3},{5,4},{6,5},{7,6},{4,7},{9,8},{10,9},{11,1... | collective-permute-start | bytes 73736 | tf_op jit(solution)/shard_map/ppermute | solution.py:310
  70.4 5.6 %collective-permute-start.8 = (bf16[96,128]{1,0:T(8,128)(2,1)S(1)}, bf16[96,128]{1,0:T(8,128)(2,1)S(1)}, u32[]{:S(2)}, u32[]{:S(2)}) collective-permute-start(bf16[96,128]{1,0:T(8,128)(2,1)S(1)} %get-tuple-element.21), channel_id=1, source_target_pairs={{0,1},{1,2},{2,3},{3,0},{4,5},{5,6},{6,7},{7,4},{8,9},{9,10},{10,1... | collective-permute-start | bytes 73736 | tf_op jit(solution)/shard_map/ppermute | solution.py:309
  (11 other events, 15.1 us)

commit v2 on v1

v2 whole, which is shorter than its diff:
```python
import functools
import math

import jax
import jax.numpy as jnp
from jax import lax
from jax.experimental import pallas as pl
from jax.experimental.pallas import tpu as pltpu
from jax.sharding import PartitionSpec as P

HEADS = 16
AHEADS = 4
WQ = 32
WK = 128
HALO = 96
LANES = 128
PRIVATE = 62

sigma_data = 16.0
gamma_boost = 0.8
norm_eps = 1e-05
masked_score = -1e30
LOG2E = math.log2(math.e)
F32 = jnp.float32
BF16 = jnp.bfloat16
NT = (((1,), (1,)), ((), ()))
TN = (((0,), (0,)), ((), ()))


def vmem(mib):
    return pltpu.CompilerParams(vmem_limit_bytes=mib * 1024 * 1024)


def cost(micros):
    return pl.CostEstimate(flops=int(micros * 1e9), transcendentals=0, bytes_accessed=int(micros * 3e6))


def hbm(count):
    return [pl.BlockSpec(memory_space=pltpu.HBM)] * count


def fetch(sources, targets, sems):
    copies = [pltpu.make_async_copy(a, b, sems.at[i]) for i, (a, b) in enumerate(zip(sources, targets))]
    for copy in copies:
        copy.start()
    return copies


def whole(count):
    return [pl.BlockSpec(memory_space=pltpu.VMEM)] * count


def dot(a, b, dims=(((1,), (0,)), ((), ()))):
    return lax.dot_general(a, b, dims, preferred_element_type=F32)


def norm_rows(values, gain):
    average = jnp.mean(values, axis=-1, keepdims=True)
    centred = values - average
    variance = jnp.mean(centred * centred, axis=-1, keepdims=True)
    return centred * lax.rsqrt(variance + norm_eps) * gain


def noisy_of(level, coords, kicks):
    level_hat = (1.0 + gamma_boost) * level
    noisy = coords + jnp.sqrt(level_hat * level_hat - level * level) * kicks
    return level_hat, noisy


def column_of(row):
    size = row.shape[1]
    down = lax.broadcasted_iota(jnp.int32, (size, size), 0)
    across = lax.broadcasted_iota(jnp.int32, (size, size), 1)
    spread = jnp.where(down == across, jnp.broadcast_to(row, (size, size)), 0.0)
    return dot(spread.astype(BF16), jnp.ones((size, LANES), BF16))


def rows_of(ref):
    return jnp.concatenate([ref[k] for k in range(ref.shape[0])], axis=0)


def write_edges(normed, low_edge_ref, high_edge_ref):
    low_edge_ref[...] = normed[:HALO]
    high_edge_ref[...] = normed[normed.shape[0] - HALO :]


def prepare_kernel(
    level_ref, coords_hbm, kicks_hbm, single_hbm, coord_in_hbm, gain_hbm, state_ref, normed_ref, low_edge_ref, high_edge_ref,
    coords_ref, kicks_ref, single_ref, coord_in_ref, gain_ref, sems
):
    copies = fetch(
        [coords_hbm, kicks_hbm, single_hbm, coord_in_hbm, gain_hbm],
        [coords_ref, kicks_ref, single_ref, coord_in_ref, gain_ref], sems,
    )
    for copy in copies:
        copy.wait()
    level_hat, noisy = noisy_of(level_ref[...], rows_of(coords_ref), rows_of(kicks_ref))
    scaled = noisy / jnp.sqrt(level_hat * level_hat + sigma_data * sigma_data)
    embedded = lax.dot_general(
        scaled, coord_in_ref[...], TN, precision=lax.Precision.HIGHEST, preferred_element_type=F32
    )
    state = single_ref[...].astype(F32) + embedded
    state_ref[...] = state
    normed = norm_rows(state, gain_ref[0:1]).astype(BF16)
    normed_ref[...] = normed
    write_edges(normed, low_edge_ref, high_edge_ref)


def pair_kernel(step_rows, tile_hbm, gain_hbm, heads_hbm, bias_ref, tile_ref, gain_ref, heads_ref, tile_sems, sems):
    keys, channels = tile_ref.shape[1:]
    head_count = heads_ref.shape[0]
    steps = tile_ref.shape[0] // step_rows
    small = fetch([gain_hbm, heads_hbm], [gain_ref, heads_ref], sems)
    spans = [pl.ds(step * step_rows, step_rows) for step in range(steps)]
    tiles = fetch([tile_hbm.at[span] for span in spans], [tile_ref.at[span] for span in spans], tile_sems)
    for copy in small:
        copy.wait()
    weights = heads_ref[...].astype(F32) * gain_ref[...]
    high = weights.astype(BF16)
    low = (weights - high.astype(F32)).astype(BF16)
    total = jnp.sum(high.astype(F32) + low.astype(F32), axis=1, keepdims=True)
    ones = jnp.ones((head_count, channels), BF16)
    left = jnp.concatenate([high, low, ones], axis=0)
    for step in range(steps):
        tiles[step].wait()
        begin = step * step_rows
        tile = tile_ref[begin : begin + step_rows].reshape(step_rows * keys, channels)
        wide = tile.astype(F32)
        square = wide * wide
        square_high = square.astype(BF16)
        square_low = (square - square_high.astype(F32)).astype(BF16)
        sums = dot(left, tile, NT)
        squares = dot(ones, square_high, NT) + dot(ones, square_low, NT)
        average = sums[2 * head_count :] / channels
        variance = jnp.maximum(squares / channels - average * average, 0.0)
        raw = sums[:head_count] + sums[head_count : 2 * head_count]
        result = (raw - average * total) * lax.rsqrt(variance + norm_eps)
        pieces = [result[:, i * keys : (i + 1) * keys] for i in range(step_rows)]
        bias_ref[:, begin : begin + step_rows, :] = jnp.stack(pieces, axis=1).astype(BF16)


def live_bias(mask_ref, chunk, outside):
    final = mask_ref.shape[0] - 1
    row = mask_ref[pl.ds(jnp.clip(chunk, 0, final), 1), :].astype(F32)
    column = column_of(row)
    column = jnp.where(outside, 0.0, column)
    return (column - 1.0) * -masked_score


def attend(queries, blocks, parts, lives, w_kv, offsets_ref, scratch):
    key_scr, value_scr, live_scr, score_scr, prob_scr, out_scr = scratch
    row_count, width = queries.shape
    block_count = len(blocks)
    head_size = width // AHEADS
    at = 0
    for part in parts:
        projected = dot(part, w_kv).astype(BF16).astype(F32)
        key_scr[at : at + part.shape[0], :] = projected[:, :width]
        value_scr[at : at + part.shape[0], :] = projected[:, width:]
        at += part.shape[0]
    at = 0
    for live in lives:
        live_scr[at : at + live.shape[0], :] = live
        at += live.shape[0]

    stacked_rows = AHEADS * WQ
    lane = lax.broadcasted_iota(jnp.int32, (stacked_rows, width), 1)
    line = lax.broadcasted_iota(jnp.int32, (stacked_rows, width), 0)
    own_head = lane // head_size == line // WQ
    pick = jnp.where(lane == 0, 1.0, 0.0).astype(BF16)
    ones = jnp.ones((WK, width), BF16)
    begins = []
    for b, (block, shift) in enumerate(blocks):
        begin = block * WQ + shift + offsets_ref[block]
        begins.append(begin)
        keys = key_scr[pl.ds(begin, WK), :].astype(BF16)
        live = live_scr[pl.ds(begin, WK), :].astype(BF16)
        query = queries[b * WQ : (b + 1) * WQ]
        query = jnp.concatenate([query] * AHEADS, axis=0)
        query = jnp.where(own_head, query, jnp.zeros_like(query))
        score_scr[b * stacked_rows : (b + 1) * stacked_rows, :] = dot(
            jnp.concatenate([query, pick], axis=1), jnp.concatenate([keys, live], axis=1), NT
        )
    factor = LOG2E / math.sqrt(head_size)
    step = 4 * stacked_rows
    for begin in range(0, block_count * stacked_rows, step):
        scores = score_scr[begin : begin + step, :]
        largest = jnp.max(scores, axis=-1, keepdims=True)
        prob_scr[begin : begin + step, :] = jnp.exp2((scores - largest) * factor).astype(BF16)
    for b in range(block_count):
        values = value_scr[pl.ds(begins[b], WK), :].astype(BF16)
        probs = prob_scr[b * stacked_rows : (b + 1) * stacked_rows, :]
        both = dot(probs, jnp.concatenate([values, ones], axis=1))
        mixed = jnp.where(own_head, both[:, :width], 0.0)
        weight = jnp.where(own_head, both[:, width:], 0.0)
        mixed = sum(mixed[h * WQ : (h + 1) * WQ] for h in range(AHEADS))
        weight = sum(weight[h * WQ : (h + 1) * WQ] for h in range(AHEADS))
        out_scr[b * WQ : (b + 1) * WQ, :] = (mixed / weight).astype(BF16)
    return out_scr[0:row_count, :]


def window_scratch(extended, row_count, width):
    scores = row_count * AHEADS
    return [
        pltpu.VMEM((extended, width), F32),
        pltpu.VMEM((extended, width), F32),
        pltpu.VMEM((extended, LANES), F32),
        pltpu.VMEM((scores, WK), F32),
        pltpu.VMEM((scores, WK), BF16),
        pltpu.VMEM((row_count, width), BF16),
    ]


def member_of(token_ref, mask_ref, first_chunk, base, tok_rows):
    chunk_count = token_ref.shape[0]
    tokens = lax.broadcasted_iota(jnp.int32, (tok_rows, LANES), 0)
    pieces = []
    for chunk in range(chunk_count):
        local = token_ref[chunk : chunk + 1, :] - base
        valid = mask_ref[pl.ds(first_chunk + chunk, 1), :]
        local = jnp.where(valid > 0, local, -1)
        pieces.append(jnp.where(local == tokens, 1.0, 0.0).astype(BF16))
    return jnp.concatenate(pieces, axis=1)


def encoder_kernel(
    place_ref, offsets_ref, level_ref, state_ref, low_ref, mid_ref, high_ref, mask_ref, token_ref, w_qkv_ref, w_out_ref,
    lift_hbm, single_hbm, embed_ref, gain_ref, encoded_ref, token_state_ref, normed_ref, member_ref, lift_ref, single_ref, sems,
    *scratch
):
    late = fetch([lift_hbm, single_hbm], [lift_ref, single_ref], sems)
    row, count = place_ref[0], place_ref[1]
    first, last = row == 0, row == count - 1
    tok_rows = single_ref.shape[0]
    chunks = token_ref.shape[0]
    width = state_ref.shape[1]
    begin = row * chunks
    low = jnp.where(first, jnp.zeros_like(low_ref[...]), low_ref[...])
    high = jnp.where(last, jnp.zeros_like(high_ref[...]), high_ref[...])
    mid = mid_ref[...]
    lives = [live_bias(mask_ref, begin - 1, first)[LANES - HALO :]]
    lives += [live_bias(mask_ref, begin + chunk, False) for chunk in range(chunks)]
    lives += [live_bias(mask_ref, begin + chunks, last)[:HALO]]
    w_qkv = w_qkv_ref[0]
    queries = dot(mid, w_qkv[:, :width]).astype(BF16)
    mixed = attend(
        queries, [(b, HALO) for b in range(mid.shape[0] // WQ)], [low, mid, high], lives, w_qkv[:, width:], offsets_ref, scratch
    )
    state = state_ref[...] + dot(mixed, w_out_ref[0])
    encoded_ref[...] = state
    for copy in late:
        copy.wait()
    lifted = jnp.maximum(dot(state.astype(BF16), lift_ref[...]), 0.0).astype(BF16)
    member = member_of(token_ref, mask_ref, begin, row * tok_rows, tok_rows)
    member_ref[...] = member
    counts = jnp.maximum(dot(member, jnp.ones((member.shape[1], LANES), BF16)), 1.0)
    pooled = dot(member, lifted) / counts[:, 0:1]
    level_hat = (1.0 + gamma_boost) * level_ref[...]
    token_state = (
        pooled + single_ref[...].astype(F32) + jnp.log(level_hat / sigma_data) / 4.0 * embed_ref[...]
    )
    token_state_ref[...] = token_state
    normed_ref[...] = norm_rows(token_state, gain_ref[0:1]).astype(BF16)


def head_spans(head_size):
    spans = []
    for h in range(HEADS):
        begin = h * head_size // LANES * LANES
        end = -(-(h + 1) * head_size // LANES) * LANES
        spans.append((begin, end))
    return spans


def inside_head(h, head_size, shape, begin):
    lane = lax.broadcasted_iota(jnp.int32, shape, 1) + begin
    return (lane >= h * head_size) & (lane < (h + 1) * head_size)


def token_scores(query_of, kv_scr, bias_of, key_mask_ref, row, near, count, per_block, spans, scale, score_scr):
    piece = key_mask_ref.shape[1]

    def one(at):
        other = (row ^ (near + at // per_block)) * per_block + at % per_block
        live = key_mask_ref[pl.ds(other, 1), :] > 0
        rows = pl.ds(at * piece if isinstance(at, int) else pl.multiple_of(at * piece, piece), piece)
        for h in range(HEADS):
            begin, end = spans[h]
            scores = dot(query_of(h), kv_scr[rows, begin:end], NT) * scale
            scores = scores + bias_of(at, other, h).astype(F32)
            score_scr[at, h] = jnp.where(live, scores, masked_score)

    if count <= 4:
        for at in range(count):
            one(at)
    else:
        lax.fori_loop(0, count, lambda at, carry: (one(at), carry)[1], 0)


def attend_first_kernel(near_count, row_count, smp_count, *refs):
    place_ref = refs[0]
    normed_refs = refs[1 : 1 + near_count]
    bias_refs = refs[1 + near_count : 1 + near_count + smp_count]
    (
        key_mask_ref, w_qkv_ref, query_ref, mixed_ref, stat_ref, far_bias_ref, kv_scr, score_scr, bias_scr,
    ) = refs[1 + near_count + smp_count :]
    row, smp = place_ref[0], place_ref[2]
    tok_rows, width = query_ref.shape
    head_size = width // HEADS
    piece = key_mask_ref.shape[1]
    per_block = tok_rows // piece
    for d in range(smp_count):
        bias_scr[smp ^ d] = bias_refs[d][...]
    for d in range(near_count, row_count):
        for e in range(per_block):
            far_bias_ref[(d - near_count) * per_block + e] = bias_scr[(row ^ d) * per_block + e]
    queries = dot(normed_refs[0][...], w_qkv_ref[:, :width]).astype(BF16)
    query_ref[...] = queries
    for d in range(near_count):
        kv_scr[d * tok_rows : (d + 1) * tok_rows, :] = dot(normed_refs[d][...], w_qkv_ref[:, width:]).astype(BF16)
    spans = head_spans(head_size)

    def query_of(h):
        begin, end = spans[h]
        query = queries[:, begin:end]
        return jnp.where(inside_head(h, head_size, query.shape, begin), query, jnp.zeros_like(query))

    count = near_count * per_block
    token_scores(
        query_of, kv_scr, lambda at, other, h: bias_scr[other, h], key_mask_ref, row, 0, count, per_block, spans,
        1.0 / math.sqrt(head_size), score_scr,
    )
    mixed_ref[...] = jnp.zeros_like(mixed_ref)
    lane = lax.broadcasted_iota(jnp.int32, (tok_rows, LANES), 1)
    stats = jnp.zeros((tok_rows, LANES), F32)
    for h in range(HEADS):
        begin, end = spans[h]
        scores = [score_scr[at, h] for at in range(count)]
        largest = jnp.max(functools.reduce(jnp.maximum, scores), axis=-1, keepdims=True)
        exponents = [jnp.exp2((part - largest) * LOG2E) for part in scores]
        total = jnp.sum(functools.reduce(jnp.add, exponents), axis=-1, keepdims=True)
        mixed = functools.reduce(
            jnp.add,
            [
                dot(exponents[at].astype(BF16), kv_scr[at * piece : (at + 1) * piece, width + begin : width + end])
                for at in range(count)
            ],
        )
        mixed_ref[:, begin:end] += jnp.where(inside_head(h, head_size, mixed.shape, begin), mixed, 0.0)
        stats = jnp.where(lane == h, largest, jnp.where(lane == HEADS + h, total, stats))
    stat_ref[...] = stats


def token_kernel(near_count, row_count, *refs):
    far_count = row_count - near_count
    place_ref = refs[0]
    normed_refs = refs[1 : 1 + far_count]
    (
        query_ref, carried_ref, stat_ref, bias_ref, state_ref, key_mask_ref, w_qkv_ref, w_proj_ref, gain_ref, ffn_in_ref,
        ffn_out_ref, spread_ref, encoded_ref, member_ref, atom_gain_ref, out_ref, joined_ref, atom_normed_ref,
        low_edge_ref, high_edge_ref, kv_scr, score_scr, mixed_scr,
    ) = refs[1 + far_count :]
    row = place_ref[0]
    tok_rows, width = state_ref.shape
    head_size = width // HEADS
    piece = key_mask_ref.shape[1]
    per_block = tok_rows // piece
    for d in range(far_count):
        kv_scr[d * tok_rows : (d + 1) * tok_rows, :] = dot(normed_refs[d][...], w_qkv_ref[:, width:]).astype(BF16)
    spans = head_spans(head_size)
    queries = query_ref[...]

    def query_of(h):
        begin, end = spans[h]
        query = queries[:, begin:end]
        return jnp.where(inside_head(h, head_size, query.shape, begin), query, jnp.zeros_like(query))

    count = far_count * per_block
    token_scores(
        query_of, kv_scr, lambda at, other, h: bias_ref[at, h], key_mask_ref, row, near_count, count, per_block, spans,
        1.0 / math.sqrt(head_size), score_scr,
    )
    mixed_scr[...] = jnp.zeros_like(mixed_scr)
    for h in range(HEADS):
        begin, end = spans[h]
        scores = [score_scr[at, h] for at in range(count)]
        before = stat_ref[:, h : h + 1]
        largest = jnp.max(functools.reduce(jnp.maximum, scores), axis=-1, keepdims=True)
        largest = jnp.maximum(largest, before)
        exponents = [jnp.exp2((part - largest) * LOG2E) for part in scores]
        shrink = jnp.exp2((before - largest) * LOG2E)
        total = jnp.sum(functools.reduce(jnp.add, exponents), axis=-1, keepdims=True)
        total = total + shrink * stat_ref[:, HEADS + h : HEADS + h + 1]
        mixed = functools.reduce(
            jnp.add,
            [
                dot(exponents[at].astype(BF16), kv_scr[at * piece : (at + 1) * piece, width + begin : width + end])
                for at in range(count)
            ],
        )
        mixed = (mixed + shrink * carried_ref[:, begin:end]) / total
        mixed_scr[:, begin:end] += jnp.where(inside_head(h, head_size, mixed.shape, begin), mixed, 0.0)
    state = state_ref[...] + dot(mixed_scr[...].astype(BF16), w_proj_ref[...])
    normed = norm_rows(state, gain_ref[1:2]).astype(BF16)
    hidden = dot(normed, ffn_in_ref[...])
    half = hidden.shape[1] // 2
    gate, up = hidden[:, :half], hidden[:, half:]
    active = (gate / (1.0 + jnp.exp(-gate)) * up).astype(BF16)
    state = state + dot(active, ffn_out_ref[...])
    result = state.astype(BF16)
    out_ref[0] = result
    spread = dot(result, spread_ref[...]).astype(BF16)
    joined = encoded_ref[...] + dot(member_ref[...], spread, TN)
    joined_ref[...] = joined
    normed = norm_rows(joined, atom_gain_ref[1:2]).astype(BF16)
    atom_normed_ref[...] = normed
    write_edges(normed, low_edge_ref, high_edge_ref)


def directions(state, level_ref, coords_ref, kicks_ref, gain_ref, coord_out_ref, direction_ref, begin):
    rows = state.shape[0]
    normed = norm_rows(state, gain_ref[...]).astype(BF16)
    update = dot(coord_out_ref[...], normed, NT)
    for k in range(coords_ref.shape[0]):
        level_hat, noisy = noisy_of(
            level_ref[...], coords_ref[k, :, begin : begin + rows], kicks_ref[k, :, begin : begin + rows]
        )
        base_square = sigma_data * sigma_data + level_hat * level_hat
        skip_scale = sigma_data * sigma_data / base_square
        out_scale = level_hat * sigma_data / jnp.sqrt(base_square)
        denoised = skip_scale * noisy + out_scale * update[k : k + 1]
        direction_ref[k, :, begin : begin + rows] = (noisy - denoised) / level_hat


def inner_kernel(
    place_ref, offsets_ref, level_ref, coords_ref, kicks_ref, state_ref, mid_ref, mask_ref, w_qkv_ref, w_out_ref, gain_ref,
    coord_out_ref, direction_ref, *scratch
):
    atoms, width = state_ref.shape
    chunks = atoms // LANES
    begin = place_ref[0] * chunks
    edge = LANES
    skip = edge - HALO
    lives = [live_bias(mask_ref, begin, False)[skip:]]
    lives += [live_bias(mask_ref, begin + chunk, False) for chunk in range(1, chunks)]
    w_qkv = w_qkv_ref[1]
    queries = dot(mid_ref[edge : atoms - edge, :], w_qkv[:, :width]).astype(BF16)
    blocks = [(b, -skip) for b in range(edge // WQ, (atoms - edge) // WQ)]
    mixed = attend(queries, blocks, [mid_ref[skip:, :]], lives, w_qkv[:, width:], offsets_ref, scratch)
    state = state_ref[edge : atoms - edge, :] + dot(mixed, w_out_ref[1])
    for k in range(direction_ref.shape[0]):
        direction_ref[k, :, 0:edge] = jnp.zeros((1, edge), F32)
        direction_ref[k, :, atoms - edge :] = jnp.zeros((1, edge), F32)
    directions(state, level_ref, coords_ref, kicks_ref, gain_ref, coord_out_ref, direction_ref, edge)


def edge_kernel(
    place_ref, offsets_ref, level_ref, coords_ref, kicks_ref, state_ref, low_ref, mid_ref, high_ref, mask_ref, w_qkv_ref,
    w_out_ref, gain_ref, coord_out_ref, inner_ref, direction_ref, *scratch
):
    row, count = place_ref[0], place_ref[1]
    first, last = row == 0, row == count - 1
    atoms, width = state_ref.shape
    chunks = atoms // LANES
    begin = row * chunks
    edge = LANES
    reach = edge + HALO
    w_qkv = w_qkv_ref[1]
    w_out = w_out_ref[1]
    for k in range(direction_ref.shape[0]):
        direction_ref[k, :, edge : atoms - edge] = inner_ref[k, :, edge : atoms - edge]
    low = jnp.where(first, jnp.zeros_like(low_ref[...]), low_ref[...])
    high = jnp.where(last, jnp.zeros_like(high_ref[...]), high_ref[...])
    lives = [
        live_bias(mask_ref, begin - 1, first)[LANES - HALO :],
        live_bias(mask_ref, begin, False),
        live_bias(mask_ref, begin + 1, False)[:HALO],
        live_bias(mask_ref, begin + chunks - 2, False)[LANES - HALO :],
        live_bias(mask_ref, begin + chunks - 1, False),
        live_bias(mask_ref, begin + chunks, last)[:HALO],
    ]
    own = jnp.concatenate([mid_ref[0:edge, :], mid_ref[atoms - edge :, :]], axis=0)
    queries = dot(own, w_qkv[:, :width]).astype(BF16)
    span = edge + 2 * HALO
    blocks = [(b, HALO) for b in range(edge // WQ)]
    blocks += [(b, span + reach - atoms) for b in range((atoms - edge) // WQ, atoms // WQ)]
    mixed = attend(
        queries, blocks, [low, mid_ref[0:reach, :], mid_ref[atoms - reach :, :], high], lives, w_qkv[:, width:], offsets_ref,
        scratch,
    )
    shift = dot(mixed, w_out)
    lower = state_ref[0:edge, :] + shift[:edge]
    upper = state_ref[atoms - edge :, :] + shift[edge:]
    directions(lower, level_ref, coords_ref, kicks_ref, gain_ref, coord_out_ref, direction_ref, 0)
    directions(upper, level_ref, coords_ref, kicks_ref, gain_ref, coord_out_ref, direction_ref, atoms - edge)


def halos_of(low_edge, high_edge):
    count = lax.axis_size("row")
    up = [(i, (i + 1) % count) for i in range(count)]
    down = [((i + 1) % count, i) for i in range(count)]
    low = lax.ppermute(high_edge, "row", up)
    high = lax.ppermute(low_edge, "row", down)
    return low, high


def spread_over(block, axis, after=None):
    count = lax.axis_size(axis)
    have = {0: block}
    bit = count // 2
    while bit:
        pairs = [(i, i ^ bit) for i in range(count)]
        for d in list(have):
            sent = have[d]
            if d and after is not None:
                sent, _ = lax.optimization_barrier((sent, after))
            have[d | bit] = lax.ppermute(sent, axis, pairs)
        bit //= 2
    return [have[d] for d in range(count)]


def per_device(
    positions,
    noise_draw,
    noise_level,
    atom_single,
    token_single,
    pair_cond,
    atom_to_token,
    window_offsets,
    atom_mask,
    token_mask,
    coord_in,
    atom_gain,
    atom_qkv,
    atom_proj,
    gather_in,
    noise_embed,
    pair_gain,
    pair_heads,
    token_gain,
    token_qkv,
    token_proj,
    ffn_in,
    ffn_out,
    scatter_out,
    out_gain,
    coord_out,
):
    row_count, smp_count = lax.axis_size("row"), lax.axis_size("smp")
    atoms, width = atom_single.shape
    tok_rows, token_width = token_single.shape
    heads = pair_heads.shape[1]
    keys = pair_cond.shape[1]
    place = jnp.stack(
        [lax.axis_index("row"), jnp.int32(row_count), lax.axis_index("smp")]
    ).astype(jnp.int32)
    level = noise_level.reshape(1, 1)
    coords = positions.transpose(1, 0, 2)
    kicks = noise_draw.transpose(1, 0, 2)
    mask = atom_mask.reshape(-1, LANES)
    tokens = atom_to_token.reshape(-1, LANES)
    smem = pl.BlockSpec(memory_space=pltpu.SMEM)
    shape = jax.ShapeDtypeStruct
    state_like = shape((atoms, width), F32)
    normed_like = shape((atoms, width), BF16)
    edge_like = shape((HALO, width), BF16)

    state, normed, low_edge, high_edge = pl.pallas_call(
        prepare_kernel,
        out_shape=(state_like, normed_like, edge_like, edge_like),
        in_specs=whole(1) + hbm(5),
        out_specs=tuple(whole(4)),
        scratch_shapes=[pltpu.VMEM(a.shape, a.dtype) for a in (coords, kicks, atom_single, coord_in, atom_gain)]
        + [pltpu.SemaphoreType.DMA((5,))],
        compiler_params=vmem(PRIVATE),
        cost_estimate=cost(1.5),
    )(level, coords, kicks, atom_single, coord_in, atom_gain)
    low, high = halos_of(low_edge, high_edge)

    pair_rows, _, channels = pair_cond.shape
    step_rows = 16
    gain_row, _ = lax.optimization_barrier((pair_gain, low_edge))
    bias = pl.pallas_call(
        functools.partial(pair_kernel, step_rows),
        out_shape=shape((heads, pair_rows, keys), BF16),
        in_specs=hbm(3),
        out_specs=whole(1)[0],
        scratch_shapes=[
            pltpu.VMEM(pair_cond.shape, BF16),
            pltpu.VMEM((1, channels), F32),
            pltpu.VMEM((heads, channels), BF16),
            pltpu.SemaphoreType.DMA((pair_rows // step_rows,)),
            pltpu.SemaphoreType.DMA((2,)),
        ],
        compiler_params=vmem(PRIVATE),
        cost_estimate=cost(5),
    )(pair_cond, gain_row.reshape(1, -1), pair_heads.T)

    encoded, token_state, token_normed, member = pl.pallas_call(
        encoder_kernel,
        out_shape=(
            state_like,
            shape((tok_rows, token_width), F32),
            shape((tok_rows, token_width), BF16),
            shape((tok_rows, atoms), BF16),
        ),
        in_specs=[smem, smem] + whole(9) + hbm(2) + whole(2),
        out_specs=tuple(whole(4)),
        scratch_shapes=[
            pltpu.VMEM(gather_in.shape, BF16),
            pltpu.VMEM(token_single.shape, BF16),
            pltpu.SemaphoreType.DMA((2,)),
        ]
        + window_scratch(atoms + 2 * HALO, atoms, width),
        compiler_params=vmem(16),
        cost_estimate=cost(3.4),
    )(
        place, window_offsets, level, state, low, normed, high, mask, tokens, atom_qkv, atom_proj, gather_in,
        token_single, noise_embed.reshape(1, -1), token_gain,
    )
    gathered = spread_over(token_normed, "row")
    biases = spread_over(bias, "smp", gathered[1 : row_count // 2 + 1])

    key_mask = token_mask.reshape(-1, keys)
    near_count = row_count - row_count // 4
    far_count = row_count - near_count
    pieces = tok_rows // keys

    def need(count):
        tile = tok_rows * max(keys, LANES)
        return (count * (keys * token_width * 4 + heads * tile * 4) + smp_count * heads * tile * 2) // 2**20 + 1

    queries, carried, stats, far_bias = pl.pallas_call(
        functools.partial(attend_first_kernel, near_count, row_count, smp_count),
        out_shape=(
            shape((tok_rows, token_width), BF16),
            shape((tok_rows, token_width), F32),
            shape((tok_rows, LANES), F32),
            shape((far_count * pieces, heads, tok_rows, keys), BF16),
        ),
        in_specs=[smem] + whole(near_count + smp_count + 2),
        out_specs=tuple(whole(4)),
        scratch_shapes=[
            pltpu.VMEM((near_count * tok_rows, 2 * token_width), BF16),
            pltpu.VMEM((near_count * pieces, heads, tok_rows, keys), F32),
            pltpu.VMEM((smp_count, heads, tok_rows, keys), BF16),
        ],
        compiler_params=vmem(8 + 2 * need(near_count * pieces)),
        cost_estimate=cost(4),
    )(place, *gathered[:near_count], *biases, key_mask, token_qkv)
    token_result, joined, atom_normed, low_edge, high_edge = pl.pallas_call(
        functools.partial(token_kernel, near_count, row_count),
        out_shape=(
            shape((1, tok_rows, token_width), BF16),
            state_like,
            normed_like,
            edge_like,
            edge_like,
        ),
        in_specs=[smem] + whole(far_count + 15),
        out_specs=tuple(whole(5)),
        scratch_shapes=[
            pltpu.VMEM((far_count * tok_rows, 2 * token_width), BF16),
            pltpu.VMEM((far_count * pieces, heads, tok_rows, keys), F32),
            pltpu.VMEM((tok_rows, token_width), F32),
        ],
        compiler_params=vmem(20 + need(far_count * pieces)),
        cost_estimate=cost(6),
    )(
        place, *gathered[near_count:], queries, carried, stats, far_bias, token_state, key_mask, token_qkv, token_proj,
        token_gain, ffn_in, ffn_out, scatter_out, encoded, member, atom_gain,
    )
    low, high = halos_of(low_edge, high_edge)

    edge = LANES
    direction_like = shape(coords.shape, F32)
    out_row = out_gain.reshape(1, -1)
    inner = pl.pallas_call(
        inner_kernel,
        out_shape=direction_like,
        in_specs=[smem, smem] + whole(10),
        out_specs=whole(1)[0],
        scratch_shapes=window_scratch(atoms - edge + HALO, atoms - 2 * edge, width),
        compiler_params=vmem(16),
        cost_estimate=cost(2.7),
    )(
        place, window_offsets, level, coords, kicks, joined, atom_normed, mask, atom_qkv, atom_proj, out_row, coord_out
    )
    direction = pl.pallas_call(
        edge_kernel,
        out_shape=direction_like,
        in_specs=[smem, smem] + whole(13),
        out_specs=whole(1)[0],
        scratch_shapes=window_scratch(2 * (edge + 2 * HALO), 2 * edge, width),
        compiler_params=vmem(12),
        cost_estimate=cost(2),
    )(
        place, window_offsets, level, coords, kicks, joined, low, atom_normed, high, mask, atom_qkv, atom_proj, out_row,
        coord_out, inner,
    )
    return (token_result, direction.transpose(1, 0, 2))


def solution(mesh):
    in_specs = (
        P(("grp", "smp"), None, "row"),
        P(("grp", "smp"), None, "row"),
        P(("grp", "smp")),
        P(("grp", "row"), None),
        P(("grp", "row"), None),
        P(("grp", "row"), "smp", None),
        P(("grp", "row")),
        P(("grp", "row")),
        P("grp"),
        P("grp"),
        P(),
        P(),
        P(),
        P(),
        P(),
        P(),
        P(),
        P(),
        P(),
        P(),
        P(),
        P(),
        P(),
        P(),
        P(),
        P(),
    )
    out_specs = (P(("grp", "smp"), "row", None), P(("grp", "smp"), None, "row"))
    return jax.shard_map(
        per_device, mesh=mesh, in_specs=in_specs, out_specs=out_specs, check_vma=False
    )
```

time: 82.6 us -> 59 us (0.71)
  waiting for transfers between devices: 35.9 us -> 10.2 us
  local copies, waits for them, and re-layouts: 10 us -> 0.14 us
  Pallas kernels: 25.1 us -> 31.8 us
  starting transfers between devices: 9.52 us -> 14.9 us
    ppermute x10, waiting for transfers between devices: 35.9 us -> 10.2 us  [the longest x6 10.2 us: spread_over(): have[d | bit] = lax.ppermute(sent, axis, pairs)]
    unnamed x69 -> x48, local copies, waits for them, and re-layouts: 9.28 us -> 0.13 us
    pallas_call x5 -> x7, Pallas kernels: 25.1 us -> 31.8 us  [the longest x1 7.97 us: per_device(): pl.pallas_call(functools.partial(pair_kernel, step_rows), out_shape=shape...]
    ppermute x10, starting transfers between devices: 9.52 us -> 14.9 us  [the longest x2 8.64 us: halos_of(): high = lax.ppermute(low_edge, 'row', down)]
  transfers between devices with their start and end apart: 10 -> 10, of which waited for: 8 -> 4; matrix products, arithmetic and copies ran while one was open for 0% -> 0% of each run, Pallas kernels for 5% -> 32%
where the time goes in v2:
time: 59 us; the launch traced here: 58.8 us
  Pallas kernels  31.8 us (54%)
  starting transfers between devices  14.9 us (25%)
  waiting for transfers between devices  10.2 us (17%)
  between operations  1.65 us (3%)
    ppermute x6, waiting for transfers between devices, spread_over(): have[d | bit] = lax.ppermute(sent, axis, pairs)  10.2 us
    ppermute x2, starting transfers between devices, halos_of(): high = lax.ppermute(low_edge, 'row', down)  8.64 us
    pallas_call x1, Pallas kernels, per_device(): pl.pallas_call(functools.partial(pair_kernel, step_rows), out_shape=shape...  7.97 us
    pallas_call x1, Pallas kernels, per_device(): pl.pallas_call(functools.partial(token_kernel, near_count, row_count), ou...  7.59 us
    ppermute x6, starting transfers between devices, spread_over(): have[d | bit] = lax.ppermute(sent, axis, pairs)  6.02 us
    pallas_call x1, Pallas kernels, per_device(): pl.pallas_call(encoder_kernel, out_shape=(state_like, shape((tok_rows, to...  4.36 us
    pallas_call x1, Pallas kernels, per_device(): pl.pallas_call(functools.partial(attend_first_kernel, near_count, row_cou...  4.06 us
    pallas_call x1, Pallas kernels, per_device(): pl.pallas_call(prepare_kernel, out_shape=(state_like, normed_like, edge_l...  2.68 us
  transfers between devices with their start and end apart: 10, of which 4 were waited for; matrix products, arithmetic and copies ran while one was open for 0% of the time, Pallas kernels for 32%

profile of v2, /device:TPU:0, one launch (start us, length us, event | category | flops | bytes accessed | tf_op | source)
XLA Modules:
  0.0 58.8 jit_solution(9008842740620549480)
XLA Ops:
  1.3 2.7 %shard_map.257 = (f32[1024,128]{1,0:T(8,128)}, bf16[1024,128]{1,0:T(8,128)(2,1)}, bf16[96,128]{1,0:T(8,128)(2,1)}, bf16[96,128]{1,0:T(8,128)(2,1)}) custom-call(f32[1,1]{1,0:T(1,128)} %bitcast.12.level_ref, f32[3,1,1024]{2,1,0:T(1,128)} %bitcast.21, f32[3,1,1024]{2,1,0:T(1,128)} %bitcast.24, bf16[1024,128]{1,0:T(8,128)(2,1)} %single_hbm.2, ...), custom_call_target="tpu_custom_call" | custom-call | flops 1500000000 | bytes 4500000 | tf_op jit(solution)/shard_map/pallas_call | solution.py:569
  4.0 5.1 %collective-permute-start.1 = (bf16[96,128]{1,0:T(8,128)(2,1)}, bf16[96,128]{1,0:T(8,128)(2,1)S(1)}, u32[]{:S(2)}, u32[]{:S(2)}) collective-permute-start(bf16[96,128]{1,0:T(8,128)(2,1)} %get-tuple-element.24), channel_id=1, source_target_pairs={{1,0},{2,1},{3,2},{0,3},{5,4},{6,5},{7,6},{4,7},{9,8},{10,9},{11,1... | collective-permute-start | bytes 73736 | tf_op jit(solution)/shard_map/ppermute | solution.py:503
  9.1 0.0 copy-start.7
  9.1 0.0 copy-start.8
  9.1 0.0 copy-start.9
  9.1 0.0 copy-start.12
  9.1 0.0 copy-start.13
  9.1 0.0 copy-start.17
  9.2 8.0 %shard_map.259.refs_4_ = bf16[16,128,128]{2,1,0:T(8,128)(2,1)} custom-call(bf16[128,128,128]{2,1,0:T(8,128)(2,1)} %tile_hbm.1, f32[1,128]{1,0:T(1,128)} %bitcast.33, bf16[16,128]{1,0:T(8,128)(2,1)} %bitcast.32), custom_call_target="tpu_custom_call" | custom-call | flops 5000000000 | bytes 15000000 | tf_op jit(solution)/shard_map/pallas_call | solution.py:584
  17.1 1.6 %collective-permute-start.6 = (bf16[16,128,128]{2,1,0:T(8,128)(2,1)}, bf16[16,128,128]{2,1,0:T(8,128)(2,1)S(1)}, u32[]{:S(2)}, u32[]{:S(2)}) collective-permute-start(bf16[16,128,128]{2,1,0:T(8,128)(2,1)} %shard_map.259.refs_4_), channel_id=1, source_target_pairs={{0,8},{4,12},{8,0},{12,4},{1,9},{5,13},{9,1},{13,5},{2,10},{6,14},... | collective-permute-start | bytes 1572872 | tf_op jit(solution)/shard_map/ppermute | solution.py:517
  18.7 0.1 pad_add_fusion.place_ref.refs_0_
  18.9 0.0 copy-start
  18.9 0.0 copy-start.14
  18.9 0.0 slice-start
  19.0 4.4 %shard_map.258 = (f32[1024,128]{1,0:T(8,128)S(1)}, f32[128,768]{1,0:T(8,128)S(1)}, bf16[128,768]{1,0:T(8,128)(2,1)S(1)}, bf16[128,1024]{1,0:T(8,128)(2,1)S(1)}) custom-call(s32[3]{0:T(128)S(1)} %pad_add_fusion.place_ref.refs_0_, s32[32]{0:T(128)S(1)} %copy-done.17, f32[1,1]{1,0:T(1,128)} %bitcast.13.level_ref, f32[1024,128]{1,0:T(8,128)S(1)} %copy-done.19, ...), custom_call_target="tpu_custom_call" | custom-call | flops 3400000000 | bytes 10200000 | tf_op jit(solution)/shard_map/pallas_call | solution.py:600
  23.3 1.0 %collective-permute-start.2 = (bf16[128,768]{1,0:T(8,128)(2,1)S(1)}, bf16[128,768]{1,0:T(8,128)(2,1)S(1)}, u32[]{:S(2)}, u32[]{:S(2)}) collective-permute-start(bf16[128,768]{1,0:T(8,128)(2,1)S(1)} %get-tuple-element.25.refs_1_), channel_id=1, source_target_pairs={{0,2},{1,3},{2,0},{3,1},{4,6},{5,7},{6,4},{7,5},{8,10},{9,11},{10,... | collective-permute-start | bytes 589832 | tf_op jit(solution)/shard_map/ppermute | solution.py:517
  24.3 3.4 %collective-permute-start.4 = (bf16[128,768]{1,0:T(8,128)(2,1)S(1)}, bf16[128,768]{1,0:T(8,128)(2,1)S(1)}, u32[]{:S(2)}, u32[]{:S(2)}) collective-permute-start(bf16[128,768]{1,0:T(8,128)(2,1)S(1)} %get-tuple-element.25.refs_1_), channel_id=1, source_target_pairs={{0,1},{1,0},{2,3},{3,2},{4,5},{5,4},{6,7},{7,6},{8,9},{9,8},{10,11... | collective-permute-start | bytes 589832 | tf_op jit(solution)/shard_map/ppermute | solution.py:517
  27.7 6.9 %collective-permute-done.2.refs_3_ = bf16[128,768]{1,0:T(8,128)(2,1)S(1)} collective-permute-done((bf16[128,768]{1,0:T(8,128)(2,1)S(1)}, bf16[128,768]{1,0:T(8,128)(2,1)S(1)}, u32[]{:S(2)}, u32[]{:S(2)}) %collective-permute-start.2) | collective-permute-done | bytes 196640 | tf_op jit(solution)/shard_map/ppermute | solution.py:517
  34.7 0.1 collective-permute-done.4.refs_2_
  34.8 0.0 collective-permute-start.3
  34.8 1.9 %collective-permute-done.7.refs_7_ = bf16[16,128,128]{2,1,0:T(8,128)(2,1)S(1)} collective-permute-done((bf16[16,128,128]{2,1,0:T(8,128)(2,1)S(1)}, bf16[16,128,128]{2,1,0:T(8,128)(2,1)S(1)}, u32[]{:S(2)}, u32[]{:S(2)}) %collective-permute-start.7) | collective-permute-done | bytes 524320 | tf_op jit(solution)/shard_map/ppermute | solution.py:517
  36.7 0.0 copy-start.2
  36.7 0.0 copy-start.6
  36.7 4.1 %shard_map.260 = (bf16[128,768]{1,0:T(8,128)(2,1)S(1)}, f32[128,768]{1,0:T(8,128)S(1)}, f32[128,128]{1,0:T(8,128)S(1)}, bf16[1,16,128,128]{3,2,1,0:T(8,128)(2,1)S(1)}) custom-call(s32[3]{0:T(128)S(1)} %pad_add_fusion.place_ref.refs_0_, bf16[128,768]{1,0:T(8,128)(2,1)S(1)} %get-tuple-element.25.refs_1_, bf16[128,768]{1,0:T(8,128)(2,1)S(1)} %collective-permute-done.4.refs_2_, ...), custom_call_target="tpu_custom_call" | custom-call | flops 4000000000 | bytes 12000000 | tf_op jit(solution)/shard_map/pallas_call | solution.py:634
  40.8 1.3 %collective-permute-done.3.refs_1_ = bf16[128,768]{1,0:T(8,128)(2,1)S(1)} collective-permute-done((bf16[128,768]{1,0:T(8,128)(2,1)S(1)}, bf16[128,768]{1,0:T(8,128)(2,1)S(1)}, u32[]{:S(2)}, u32[]{:S(2)}) %collective-permute-start.3) | collective-permute-done | bytes 196640 | tf_op jit(solution)/shard_map/ppermute | solution.py:517
  42.2 0.0 copy-start.11
  42.2 0.0 copy-start.16
  42.2 7.6 %shard_map.261 = (bf16[1,128,768]{2,1,0:T(8,128)(2,1)}, f32[1024,128]{1,0:T(8,128)S(1)}, bf16[1024,128]{1,0:T(8,128)(2,1)S(1)}, bf16[96,128]{1,0:T(8,128)(2,1)S(1)}, bf16[96,128]{1,0:T(8,128)(2,1)S(1)}) custom-call(s32[3]{0:T(128)S(1)} %pad_add_fusion.place_ref.refs_0_, bf16[128,768]{1,0:T(8,128)(2,1)S(1)} %collective-permute-done.3.refs_1_, ...), custom_call_target="tpu_custom_call" | custom-call | flops 6000000000 | bytes 18000000 | tf_op jit(solution)/shard_map/pallas_call | solution.py:652
  49.8 0.3 collective-permute-start.8
  50.1 3.5 %collective-permute-start.9 = (bf16[96,128]{1,0:T(8,128)(2,1)S(1)}, bf16[96,128]{1,0:T(8,128)(2,1)S(1)}, u32[]{:S(2)}, u32[]{:S(2)}) collective-permute-start(bf16[96,128]{1,0:T(8,128)(2,1)S(1)} %get-tuple-element.39), channel_id=1, source_target_pairs={{1,0},{2,1},{3,2},{0,3},{5,4},{6,5},{7,6},{4,7},{9,8},{10,9},{11,1... | collective-permute-start | bytes 73736 | tf_op jit(solution)/shard_map/ppermute | solution.py:503
  53.6 2.6 %shard_map.262.inner_ref = f32[3,1,1024]{2,1,0:T(1,128)S(1)} custom-call(s32[3]{0:T(128)S(1)} %pad_add_fusion.place_ref.refs_0_, s32[32]{0:T(128)S(1)} %copy-done.17, f32[1,1]{1,0:T(1,128)} %bitcast.14.level_ref, f32[3,1,1024]{2,1,0:T(1,128)S(1)} %bitcast.22, f32[3,1,1024]{2,1,0:T(1,128)S(1)} %bitcast.25, f32[1024,128]{1,0:T(8,128)S(1)} %get-tuple-element.36.state_ref, ...), custom_call_target="tpu_custom_call" | custom-call | flops 2700000000 | bytes 8100000 | tf_op jit(solution)/shard_map/pallas_call | solution.py:679
  56.3 2.5 %shard_map.263 = f32[3,1,1024]{2,1,0:T(1,128)} custom-call(s32[3]{0:T(128)S(1)} %pad_add_fusion.place_ref.refs_0_, s32[32]{0:T(128)S(1)} %copy-done.17, f32[1,1]{1,0:T(1,128)} %bitcast.15.level_ref, f32[3,1,1024]{2,1,0:T(1,128)S(1)} %bitcast.23, f32[3,1,1024]{2,1,0:T(1,128)S(1)} %bitcast.26, f32[1024,128]{1,0:T(8,128)S(1)} %get-tuple-element.36.state_ref, ...), custom_call_target="tpu_custom_call" | custom-call | flops 2000000000 | bytes 6000000 | tf_op jit(solution)/shard_map/pallas_call | solution.py:690
  (46 shorter events, 0.1 us)
Async XLA Ops:
  4.0 14.8 %collective-permute-start.1 = (bf16[96,128]{1,0:T(8,128)(2,1)}, bf16[96,128]{1,0:T(8,128)(2,1)S(1)}, u32[]{:S(2)}, u32[]{:S(2)}) collective-permute-start(bf16[96,128]{1,0:T(8,128)(2,1)} %get-tuple-element.24), channel_id=1, source_target_pairs={{1,0},{2,1},{3,2},{0,3},{5,4},{6,5},{7,6},{4,7},{9,8},{10,9},{11,1... | collective-permute-start | bytes 73736 | tf_op jit(solution)/shard_map/ppermute | solution.py:503
  9.1 9.7 %collective-permute-start = (bf16[96,128]{1,0:T(8,128)(2,1)}, bf16[96,128]{1,0:T(8,128)(2,1)S(1)}, u32[]{:S(2)}, u32[]{:S(2)}) collective-permute-start(bf16[96,128]{1,0:T(8,128)(2,1)} %get-tuple-element.22), channel_id=1, source_target_pairs={{0,1},{1,2},{2,3},{3,0},{4,5},{5,6},{6,7},{7,4},{8,9},{9,10},{10,1... | collective-permute-start | bytes 73736 | tf_op jit(solution)/shard_map/ppermute | solution.py:502
  9.1 9.7 %copy-start.21 = (f32[768]{0:T(1024)S(1)}, f32[768]{0:T(1024)}, u32[]{:S(2)}) copy-start(f32[768]{0:T(1024)} %param.41) | copy-start | bytes 9220
  9.1 9.7 %copy-start.4 = (bf16[128,768]{1,0:T(8,128)(2,1)S(1)}, bf16[128,768]{1,0:T(8,128)(2,1)}, u32[]{:S(2)}) copy-start(bf16[128,768]{1,0:T(8,128)(2,1)} %lift_hbm.1) | copy-start | bytes 589828
  9.1 9.8 %copy-start.5 = (bf16[128,768]{1,0:T(8,128)(2,1)S(1)}, bf16[128,768]{1,0:T(8,128)(2,1)}, u32[]{:S(2)}) copy-start(bf16[128,768]{1,0:T(8,128)(2,1)} %single_hbm.3) | copy-start | bytes 589828
  9.1 9.8 %copy-start.7 = (bf16[2,128,384]{2,1,0:T(8,128)(2,1)S(1)}, bf16[2,128,384]{2,1,0:T(8,128)(2,1)}, u32[]{:S(2)}) copy-start(bf16[2,128,384]{2,1,0:T(8,128)(2,1)} %w_qkv_ref.5) | copy-start | bytes 589828
  9.1 9.8 %copy-start.8 = (bf16[2,128,128]{2,1,0:T(8,128)(2,1)S(1)}, bf16[2,128,128]{2,1,0:T(8,128)(2,1)}, u32[]{:S(2)}) copy-start(bf16[2,128,128]{2,1,0:T(8,128)(2,1)} %w_out_ref.5) | copy-start | bytes 196612
  9.1 9.8 %copy-start.9 = (s32[4096]{0:T(1024)S(1)}, s32[4096]{0:T(1024)}, u32[]{:S(2)}) copy-start(s32[4096]{0:T(1024)} %param.34) | copy-start | bytes 49156
  9.1 9.7 %copy-start.12 = (f32[2,768]{1,0:T(2,128)S(1)}, f32[2,768]{1,0:T(2,128)}, u32[]{:S(2)}) copy-start(f32[2,768]{1,0:T(2,128)} %refs_10_.1) | copy-start | bytes 18436
  9.1 9.7 %copy-start.13 = (s32[1024]{0:T(1024)S(1)}, s32[1024]{0:T(1024)}, u32[]{:S(2)}) copy-start(s32[1024]{0:T(1024)} %param.32) | copy-start | bytes 12292
  9.1 9.7 %copy-start.17 = (s32[32]{0:T(128)S(1)}, s32[32]{0:T(128)}, u32[]{:S(2)}) copy-start(s32[32]{0:T(128)} %offsets_ref.5) | copy-start | bytes 388
  9.2 9.7 %copy-start.19 = (f32[1024,128]{1,0:T(8,128)S(1)}, f32[1024,128]{1,0:T(8,128)}, u32[]{:S(2)}) copy-start(f32[1024,128]{1,0:T(8,128)} %get-tuple-element.21.state_ref) | copy-start | bytes 1572868
  9.2 9.7 %copy-start.20 = (bf16[1024,128]{1,0:T(8,128)(2,1)S(1)}, bf16[1024,128]{1,0:T(8,128)(2,1)}, u32[]{:S(2)}) copy-start(bf16[1024,128]{1,0:T(8,128)(2,1)} %get-tuple-element.23.mid_ref) | copy-start | bytes 786436
  17.1 17.6 %collective-permute-start.6 = (bf16[16,128,128]{2,1,0:T(8,128)(2,1)}, bf16[16,128,128]{2,1,0:T(8,128)(2,1)S(1)}, u32[]{:S(2)}, u32[]{:S(2)}) collective-permute-start(bf16[16,128,128]{2,1,0:T(8,128)(2,1)} %shard_map.259.refs_4_), channel_id=1, source_target_pairs={{0,8},{4,12},{8,0},{12,4},{1,9},{5,13},{9,1},{13,5},{2,10},{6,14},... | collective-permute-start | bytes 1572872 | tf_op jit(solution)/shard_map/ppermute | solution.py:517
  18.9 8.8 %copy-start.3 = (bf16[16,128,128]{2,1,0:T(8,128)(2,1)S(1)}, bf16[16,128,128]{2,1,0:T(8,128)(2,1)}, u32[]{:S(2)}) copy-start(bf16[16,128,128]{2,1,0:T(8,128)(2,1)} %shard_map.259.refs_4_) | copy-start | bytes 1572868
  18.9 17.8 %copy-start = (bf16[768,2304]{1,0:T(8,128)(2,1)S(1)}, bf16[768,2304]{1,0:T(8,128)(2,1)}, u32[]{:S(2)}) copy-start(bf16[768,2304]{1,0:T(8,128)(2,1)} %refs_8_.1) | copy-start | bytes 10616836
  18.9 17.8 %copy-start.14 = (s32[512]{0:T(512)S(1)}, s32[512]{0:T(512)}, u32[]{:S(2)}) copy-start(s32[512]{0:T(512)} %param.35) | copy-start | bytes 6148
  18.9 23.1 %slice-start = ((s8[4718592]{0:T(1024)(128)(4,1)}), s8[4194304]{0:T(1024)(128)(4,1)S(1)}, s32[]{:S(2)}) async-start(s8[4718592]{0:T(1024)(128)(4,1)} %bitcast.16), calls=%async_computation | async-start | bytes 8388608
  23.3 11.4 %collective-permute-start.2 = (bf16[128,768]{1,0:T(8,128)(2,1)S(1)}, bf16[128,768]{1,0:T(8,128)(2,1)S(1)}, u32[]{:S(2)}, u32[]{:S(2)}) collective-permute-start(bf16[128,768]{1,0:T(8,128)(2,1)S(1)} %get-tuple-element.25.refs_1_), channel_id=1, source_target_pairs={{0,2},{1,3},{2,0},{3,1},{4,6},{5,7},{6,4},{7,5},{8,10},{9,11},{10,... | collective-permute-start | bytes 589832 | tf_op jit(solution)/shard_map/ppermute | solution.py:517
  24.3 10.4 %collective-permute-start.4 = (bf16[128,768]{1,0:T(8,128)(2,1)S(1)}, bf16[128,768]{1,0:T(8,128)(2,1)S(1)}, u32[]{:S(2)}, u32[]{:S(2)}) collective-permute-start(bf16[128,768]{1,0:T(8,128)(2,1)S(1)} %get-tuple-element.25.refs_1_), channel_id=1, source_target_pairs={{0,1},{1,0},{2,3},{3,2},{4,5},{5,4},{6,7},{7,6},{8,9},{9,8},{10,11... | collective-permute-start | bytes 589832 | tf_op jit(solution)/shard_map/ppermute | solution.py:517
  27.7 7.1 %collective-permute-start.5 = (bf16[16,128,128]{2,1,0:T(8,128)(2,1)S(1)}, bf16[16,128,128]{2,1,0:T(8,128)(2,1)S(1)}, u32[]{:S(2)}, u32[]{:S(2)}) collective-permute-start(bf16[16,128,128]{2,1,0:T(8,128)(2,1)S(1)} %copy-done.3), channel_id=1, source_target_pairs={{0,4},{4,0},{8,12},{12,8},{1,5},{5,1},{9,13},{13,9},{2,6},{6,2},{1... | collective-permute-start | bytes 1572872 | tf_op jit(solution)/shard_map/ppermute | solution.py:517
  34.8 1.9 %collective-permute-start.7 = (bf16[16,128,128]{2,1,0:T(8,128)(2,1)S(1)}, bf16[16,128,128]{2,1,0:T(8,128)(2,1)S(1)}, u32[]{:S(2)}, u32[]{:S(2)}) collective-permute-start(bf16[16,128,128]{2,1,0:T(8,128)(2,1)S(1)} %collective-permute-done.6.refs_6_), channel_id=1, source_target_pairs={{0,4},{4,0},{8,12},{12,8},{1,5},{5,1},{9,13},{13,9},{2,6},{6,2},{1... | collective-permute-start | bytes 1572872 | tf_op jit(solution)/shard_map/ppermute | solution.py:517
  34.8 7.3 %collective-permute-start.3 = (bf16[128,768]{1,0:T(8,128)(2,1)S(1)}, bf16[128,768]{1,0:T(8,128)(2,1)S(1)}, u32[]{:S(2)}, u32[]{:S(2)}) collective-permute-start(bf16[128,768]{1,0:T(8,128)(2,1)S(1)} %collective-permute-done.2.refs_3_), channel_id=1, source_target_pairs={{0,1},{1,0},{2,3},{3,2},{4,5},{5,4},{6,7},{7,6},{8,9},{9,8},{10,11... | collective-permute-start | bytes 589832 | tf_op jit(solution)/shard_map/ppermute | solution.py:517
  36.7 5.4 %slice-start.1 = ((s8[4718592]{0:T(1024)(128)(4,1)}), s8[524288]{0:T(1024)(128)(4,1)S(1)}, s32[]{:S(2)}) async-start(s8[4718592]{0:T(1024)(128)(4,1)} %bitcast.16), calls=%async_computation.1 | async-start | bytes 1048576
  36.7 5.4 %copy-start.1 = (bf16[1536,768]{1,0:T(8,128)(2,1)S(1)}, bf16[1536,768]{1,0:T(8,128)(2,1)}, u32[]{:S(2)}) copy-start(bf16[1536,768]{1,0:T(8,128)(2,1)} %refs_12_.1) | copy-start | bytes 7077892
  36.7 5.4 %copy-start.2 = (bf16[768,768]{1,0:T(8,128)(2,1)S(1)}, bf16[768,768]{1,0:T(8,128)(2,1)}, u32[]{:S(2)}) copy-start(bf16[768,768]{1,0:T(8,128)(2,1)} %refs_9_.3) | copy-start | bytes 3538948
  42.1 11.5 %copy-start.10 = (f32[1,3,1024]{2,0,1:T(1,128)S(1)}, f32[1,3,1024]{2,0,1:T(1,128)}, u32[]{:S(2)}) copy-start(f32[1,3,1024]{2,0,1:T(1,128)} %param.26) | copy-start | bytes 36868
  42.2 11.5 %copy-start.11 = (f32[1,3,1024]{2,0,1:T(1,128)S(1)}, f32[1,3,1024]{2,0,1:T(1,128)}, u32[]{:S(2)}) copy-start(f32[1,3,1024]{2,0,1:T(1,128)} %param.27) | copy-start | bytes 36868
  42.2 11.4 %copy-start.16 = (bf16[3,128]{1,0:T(4,128)(2,1)S(1)}, bf16[3,128]{1,0:T(4,128)(2,1)}, u32[]{:S(2)}) copy-start(bf16[3,128]{1,0:T(4,128)(2,1)} %coord_out_ref.3) | copy-start | bytes 2308
  42.2 11.4 %copy-start.18 = (f32[128]{0:T(128)S(1)}, f32[128]{0:T(128)}, u32[]{:S(2)}) copy-start(f32[128]{0:T(128)} %param.50) | copy-start | bytes 1540
  49.8 6.5 %collective-permute-start.8 = (bf16[96,128]{1,0:T(8,128)(2,1)S(1)}, bf16[96,128]{1,0:T(8,128)(2,1)S(1)}, u32[]{:S(2)}, u32[]{:S(2)}) collective-permute-start(bf16[96,128]{1,0:T(8,128)(2,1)S(1)} %get-tuple-element.37), channel_id=1, source_target_pairs={{0,1},{1,2},{2,3},{3,0},{4,5},{5,6},{6,7},{7,4},{8,9},{9,10},{10,1... | collective-permute-start | bytes 73736 | tf_op jit(solution)/shard_map/ppermute | solution.py:502
  50.1 6.2 %collective-permute-start.9 = (bf16[96,128]{1,0:T(8,128)(2,1)S(1)}, bf16[96,128]{1,0:T(8,128)(2,1)S(1)}, u32[]{:S(2)}, u32[]{:S(2)}) collective-permute-start(bf16[96,128]{1,0:T(8,128)(2,1)S(1)} %get-tuple-element.39), channel_id=1, source_target_pairs={{1,0},{2,1},{3,2},{0,3},{5,4},{6,5},{7,6},{4,7},{9,8},{10,9},{11,1... | collective-permute-start | bytes 73736 | tf_op jit(solution)/shard_map/ppermute | solution.py:503
  (2 other events, 10.8 us)

commit v3 on v2

--- a/solution.py
+++ b/solution.py
@@ -119,24 +119,20 @@
     high = weights.astype(BF16)
     low = (weights - high.astype(F32)).astype(BF16)
     total = jnp.sum(high.astype(F32) + low.astype(F32), axis=1, keepdims=True)
-    ones = jnp.ones((head_count, channels), BF16)
-    left = jnp.concatenate([high, low, ones], axis=0)
+    left = jnp.concatenate([high, low], axis=0)
     for step in range(steps):
         tiles[step].wait()
         begin = step * step_rows
-        tile = tile_ref[begin : begin + step_rows].reshape(step_rows * keys, channels)
+        tile = tile_ref[begin : begin + step_rows].reshape(step_rows * keys, channels).T
         wide = tile.astype(F32)
-        square = wide * wide
-        square_high = square.astype(BF16)
-        square_low = (square - square_high.astype(F32)).astype(BF16)
-        sums = dot(left, tile, NT)
-        squares = dot(ones, square_high, NT) + dot(ones, square_low, NT)
-        average = sums[2 * head_count :] / channels
-        variance = jnp.maximum(squares / channels - average * average, 0.0)
-        raw = sums[:head_count] + sums[head_count : 2 * head_count]
+        average = jnp.mean(wide, axis=0, keepdims=True)
+        centred = wide - average
+        variance = jnp.mean(centred * centred, axis=0, keepdims=True)
+        sums = dot(left, tile)
+        raw = sums[:head_count] + sums[head_count:]
         result = (raw - average * total) * lax.rsqrt(variance + norm_eps)
         pieces = [result[:, i * keys : (i + 1) * keys] for i in range(step_rows)]
-        bias_ref[:, begin : begin + step_rows, :] = jnp.stack(pieces, axis=1).astype(BF16)
+        bias_ref[:, begin : begin + step_rows, :] = jnp.swapaxes(jnp.stack(pieces, axis=0), 0, 1).astype(BF16)
 
 
 def live_bias(mask_ref, chunk, outside):
@@ -277,6 +273,34 @@
     return (lane >= h * head_size) & (lane < (h + 1) * head_size)
 
 
+class Tiles:
+    def __init__(self, rows, width):
+        self.rows = rows
+        self.tiles = [None] * (width // LANES)
+
+    def add(self, h, head_size, begin, values):
+        for at in range(0, values.shape[1], LANES):
+            tile = (begin + at) // LANES
+            inside = inside_head(h, head_size, (self.rows, LANES), begin + at)
+            kept = self.tiles[tile]
+            part = values[:, at : at + LANES]
+            self.tiles[tile] = jnp.where(inside, part, 0.0 if kept is None else kept)
+
+    def join(self):
+        return jnp.concatenate(self.tiles, axis=1)
+
+
+def weighted_values(prob_scr, kv_scr, h, count, piece, begin, end):
+    ones = jnp.ones((piece, LANES), BF16)
+    return functools.reduce(
+        jnp.add,
+        [
+            dot(prob_scr[at, h], jnp.concatenate([kv_scr[at * piece : (at + 1) * piece, begin:end], ones], axis=1))
+            for at in range(count)
+        ],
+    )
+
+
 def token_scores(query_of, kv_scr, bias_of, key_mask_ref, row, near, count, per_block, spans, scale, score_scr):
     piece = key_mask_ref.shape[1]
 
@@ -302,7 +326,8 @@
     normed_refs = refs[1 : 1 + near_count]
     bias_refs = refs[1 + near_count : 1 + near_count + smp_count]
     (
-        key_mask_ref, w_qkv_ref, query_ref, mixed_ref, stat_ref, far_bias_ref, kv_scr, score_scr, bias_scr,
+        key_mask_ref, w_qkv_ref, query_ref, mixed_ref, largest_ref, total_ref, far_bias_ref, kv_scr, score_scr, prob_scr,
+        bias_scr,
     ) = refs[1 + near_count + smp_count :]
     row, smp = place_ref[0], place_ref[2]
     tok_rows, width = query_ref.shape
@@ -330,25 +355,21 @@
         query_of, kv_scr, lambda at, other, h: bias_scr[other, h], key_mask_ref, row, 0, count, per_block, spans,
         1.0 / math.sqrt(head_size), score_scr,
     )
-    mixed_ref[...] = jnp.zeros_like(mixed_ref)
-    lane = lax.broadcasted_iota(jnp.int32, (tok_rows, LANES), 1)
-    stats = jnp.zeros((tok_rows, LANES), F32)
+    step = 4
+    for begin in range(0, HEADS, step):
+        heads = slice(begin, begin + step)
+        scores = [score_scr[at, heads] for at in range(count)]
+        largest = jnp.max(functools.reduce(jnp.maximum, scores), axis=-1, keepdims=True)
+        largest_ref[heads] = jnp.broadcast_to(largest, largest_ref[heads].shape)
+        for at in range(count):
+            prob_scr[at, heads] = jnp.exp2((scores[at] - largest) * LOG2E).astype(BF16)
+    mixed = Tiles(tok_rows, width)
     for h in range(HEADS):
         begin, end = spans[h]
-        scores = [score_scr[at, h] for at in range(count)]
-        largest = jnp.max(functools.reduce(jnp.maximum, scores), axis=-1, keepdims=True)
-        exponents = [jnp.exp2((part - largest) * LOG2E) for part in scores]
-        total = jnp.sum(functools.reduce(jnp.add, exponents), axis=-1, keepdims=True)
-        mixed = functools.reduce(
-            jnp.add,
-            [
-                dot(exponents[at].astype(BF16), kv_scr[at * piece : (at + 1) * piece, width + begin : width + end])
-                for at in range(count)
-            ],
-        )
-        mixed_ref[:, begin:end] += jnp.where(inside_head(h, head_size, mixed.shape, begin), mixed, 0.0)
-        stats = jnp.where(lane == h, largest, jnp.where(lane == HEADS + h, total, stats))
-    stat_ref[...] = stats
+        both = weighted_values(prob_scr, kv_scr, h, count, piece, width + begin, width + end)
+        mixed.add(h, head_size, begin, both[:, : end - begin])
+        total_ref[h] = both[:, end - begin :]
+    mixed_ref[...] = mixed.join()
 
 
 def token_kernel(near_count, row_count, *refs):
@@ -356,9 +377,9 @@
     place_ref = refs[0]
     normed_refs = refs[1 : 1 + far_count]
     (
-        query_ref, carried_ref, stat_ref, bias_ref, state_ref, key_mask_ref, w_qkv_ref, w_proj_ref, gain_ref, ffn_in_ref,
+        query_ref, carried_ref, largest_ref, total_ref, bias_ref, state_ref, key_mask_ref, w_qkv_ref, w_proj_ref, gain_ref, ffn_in_ref,
         ffn_out_ref, spread_ref, encoded_ref, member_ref, atom_gain_ref, out_ref, joined_ref, atom_normed_ref,
-        low_edge_ref, high_edge_ref, kv_scr, score_scr, mixed_scr,
+        low_edge_ref, high_edge_ref, kv_scr, score_scr, prob_scr, shrink_scr,
     ) = refs[1 + far_count :]
     row = place_ref[0]
     tok_rows, width = state_ref.shape
@@ -380,27 +401,28 @@
         query_of, kv_scr, lambda at, other, h: bias_ref[at, h], key_mask_ref, row, near_count, count, per_block, spans,
         1.0 / math.sqrt(head_size), score_scr,
     )
-    mixed_scr[...] = jnp.zeros_like(mixed_scr)
+    step = 4
+    for begin in range(0, HEADS, step):
+        heads = slice(begin, begin + step)
+        scores = [score_scr[at, heads] for at in range(count)]
+        before = largest_ref[heads]
+        largest = jnp.max(functools.reduce(jnp.maximum, scores), axis=-1, keepdims=True)
+        largest = jnp.maximum(jnp.broadcast_to(largest, before.shape), before)
+        shrink_scr[heads] = jnp.exp2((before - largest) * LOG2E)
+        for at in range(count):
+            prob_scr[at, heads] = jnp.exp2((scores[at] - largest[:, :, :piece]) * LOG2E).astype(BF16)
+    mixed, total = Tiles(tok_rows, width), Tiles(tok_rows, width)
     for h in range(HEADS):
         begin, end = spans[h]
-        scores = [score_scr[at, h] for at in range(count)]
-        before = stat_ref[:, h : h + 1]
-        largest = jnp.max(functools.reduce(jnp.maximum, scores), axis=-1, keepdims=True)
-        largest = jnp.maximum(largest, before)
-        exponents = [jnp.exp2((part - largest) * LOG2E) for part in scores]
-        shrink = jnp.exp2((before - largest) * LOG2E)
-        total = jnp.sum(functools.reduce(jnp.add, exponents), axis=-1, keepdims=True)
-        total = total + shrink * stat_ref[:, HEADS + h : HEADS + h + 1]
-        mixed = functools.reduce(
-            jnp.add,
-            [
-                dot(exponents[at].astype(BF16), kv_scr[at * piece : (at + 1) * piece, width + begin : width + end])
-                for at in range(count)
-            ],
-        )
-        mixed = (mixed + shrink * carried_ref[:, begin:end]) / total
-        mixed_scr[:, begin:end] += jnp.where(inside_head(h, head_size, mixed.shape, begin), mixed, 0.0)
-    state = state_ref[...] + dot(mixed_scr[...].astype(BF16), w_proj_ref[...])
+        both = weighted_values(prob_scr, kv_scr, h, count, piece, width + begin, width + end)
+        shrink = shrink_scr[h]
+        weight = both[:, end - begin :] + shrink * total_ref[h]
+        for at in range(begin, end, LANES):
+            part = both[:, at - begin : at - begin + LANES] + shrink * carried_ref[:, at : at + LANES]
+            mixed.add(h, head_size, at, part)
+            total.add(h, head_size, at, weight)
+    attended = (mixed.join() / total.join()).astype(BF16)
+    state = state_ref[...] + dot(attended, w_proj_ref[...])
     normed = norm_rows(state, gain_ref[1:2]).astype(BF16)
     hidden = dot(normed, ffn_in_ref[...])
     half = hidden.shape[1] // 2
@@ -579,7 +601,7 @@
     low, high = halos_of(low_edge, high_edge)
 
     pair_rows, _, channels = pair_cond.shape
-    step_rows = 16
+    step_rows = 32
     gain_row, _ = lax.optimization_barrier((pair_gain, low_edge))
     bias = pl.pallas_call(
         functools.partial(pair_kernel, step_rows),
@@ -629,24 +651,26 @@
 
     def need(count):
         tile = tok_rows * max(keys, LANES)
-        return (count * (keys * token_width * 4 + heads * tile * 4) + smp_count * heads * tile * 2) // 2**20 + 1
-
-    queries, carried, stats, far_bias = pl.pallas_call(
+        return (count * (keys * token_width * 4 + heads * tile * 6) + smp_count * heads * tile * 2) // 2**20 + 1
+
+    queries, carried, largest, total, far_bias = pl.pallas_call(
         functools.partial(attend_first_kernel, near_count, row_count, smp_count),
         out_shape=(
             shape((tok_rows, token_width), BF16),
             shape((tok_rows, token_width), F32),
-            shape((tok_rows, LANES), F32),
+            shape((heads, tok_rows, LANES), F32),
+            shape((heads, tok_rows, LANES), F32),
             shape((far_count * pieces, heads, tok_rows, keys), BF16),
         ),
         in_specs=[smem] + whole(near_count + smp_count + 2),
-        out_specs=tuple(whole(4)),
+        out_specs=tuple(whole(5)),
         scratch_shapes=[
             pltpu.VMEM((near_count * tok_rows, 2 * token_width), BF16),
             pltpu.VMEM((near_count * pieces, heads, tok_rows, keys), F32),
+            pltpu.VMEM((near_count * pieces, heads, tok_rows, keys), BF16),
             pltpu.VMEM((smp_count, heads, tok_rows, keys), BF16),
         ],
-        compiler_params=vmem(8 + 2 * need(near_count * pieces)),
+        compiler_params=vmem(14 + need(near_count * pieces) * 3 // 2),
         cost_estimate=cost(4),
     )(place, *gathered[:near_count], *biases, key_mask, token_qkv)
     token_result, joined, atom_normed, low_edge, high_edge = pl.pallas_call(
@@ -658,17 +682,18 @@
             edge_like,
             edge_like,
         ),
-        in_specs=[smem] + whole(far_count + 15),
+        in_specs=[smem] + whole(far_count + 16),
         out_specs=tuple(whole(5)),
         scratch_shapes=[
             pltpu.VMEM((far_count * tok_rows, 2 * token_width), BF16),
             pltpu.VMEM((far_count * pieces, heads, tok_rows, keys), F32),
-            pltpu.VMEM((tok_rows, token_width), F32),
+            pltpu.VMEM((far_count * pieces, heads, tok_rows, keys), BF16),
+            pltpu.VMEM((heads, tok_rows, LANES), F32),
         ],
         compiler_params=vmem(20 + need(far_count * pieces)),
         cost_estimate=cost(6),
     )(
-        place, *gathered[near_count:], queries, carried, stats, far_bias, token_state, key_mask, token_qkv, token_proj,
+        place, *gathered[near_count:], queries, carried, largest, total, far_bias, token_state, key_mask, token_qkv, token_proj,
         token_gain, ffn_in, ffn_out, scatter_out, encoded, member, atom_gain,
     )
     low, high = halos_of(low_edge, high_edge)

time: 59 us -> 54 us (0.915)
  Pallas kernels: 31.8 us -> 27 us
    pallas_call x1, Pallas kernels: 7.59 us -> 4.98 us  [per_device(): pl.pallas_call(functools.partial(token_kernel, near_count, row_count), ou...]
    pallas_call x1, Pallas kernels: 7.97 us -> 5.57 us  [per_device(): pl.pallas_call(functools.partial(pair_kernel, step_rows), out_shape=shape...]
  transfers between devices with their start and end apart: 10 -> 10, of which waited for: 4 -> 4; matrix products, arithmetic and copies ran while one was open for 0% -> 0% of each run, Pallas kernels for 32% -> 31%
where the time goes in v3:
time: 54 us; the launch traced here: 53.7 us
  Pallas kernels  27 us (50%)
  starting transfers between devices  14.9 us (28%)
  waiting for transfers between devices  9.93 us (18%)
  between operations  1.64 us (3%)
    ppermute x6, waiting for transfers between devices, spread_over(): have[d | bit] = lax.ppermute(sent, axis, pairs)  9.92 us
    ppermute x2, starting transfers between devices, halos_of(): high = lax.ppermute(low_edge, 'row', down)  8.65 us
    ppermute x6, starting transfers between devices, spread_over(): have[d | bit] = lax.ppermute(sent, axis, pairs)  6.01 us
    pallas_call x1, Pallas kernels, per_device(): pl.pallas_call(functools.partial(pair_kernel, step_rows), out_shape=shape...  5.57 us
    pallas_call x1, Pallas kernels, per_device(): pl.pallas_call(functools.partial(token_kernel, near_count, row_count), ou...  4.98 us
    pallas_call x1, Pallas kernels, per_device(): pl.pallas_call(encoder_kernel, out_shape=(state_like, shape((tok_rows, to...  4.36 us
    pallas_call x1, Pallas kernels, per_device(): pl.pallas_call(functools.partial(attend_first_kernel, near_count, row_cou...  4.31 us
    pallas_call x1, Pallas kernels, per_device(): pl.pallas_call(prepare_kernel, out_shape=(state_like, normed_like, edge_l...  2.68 us
  transfers between devices with their start and end apart: 10, of which 4 were waited for; matrix products, arithmetic and copies ran while one was open for 0% of the time, Pallas kernels for 31%

profile of v3, /device:TPU:0, one launch (start us, length us, event | category | flops | bytes accessed | tf_op | source)
XLA Modules:
  0.0 53.7 jit_solution(10874249290056085302)
XLA Ops:
  1.3 2.7 %shard_map.257 = (f32[1024,128]{1,0:T(8,128)}, bf16[1024,128]{1,0:T(8,128)(2,1)}, bf16[96,128]{1,0:T(8,128)(2,1)}, bf16[96,128]{1,0:T(8,128)(2,1)}) custom-call(f32[1,1]{1,0:T(1,128)} %bitcast.12.level_ref, f32[3,1,1024]{2,1,0:T(1,128)} %bitcast.21, f32[3,1,1024]{2,1,0:T(1,128)} %bitcast.24, bf16[1024,128]{1,0:T(8,128)(2,1)} %single_hbm.2, ...), custom_call_target="tpu_custom_call" | custom-call | flops 1500000000 | bytes 4500000 | tf_op jit(solution)/shard_map/pallas_call | solution.py:591
  4.0 5.1 %collective-permute-start.1 = (bf16[96,128]{1,0:T(8,128)(2,1)}, bf16[96,128]{1,0:T(8,128)(2,1)S(1)}, u32[]{:S(2)}, u32[]{:S(2)}) collective-permute-start(bf16[96,128]{1,0:T(8,128)(2,1)} %get-tuple-element.25), channel_id=1, source_target_pairs={{1,0},{2,1},{3,2},{0,3},{5,4},{6,5},{7,6},{4,7},{9,8},{10,9},{11,1... | collective-permute-start | bytes 73736 | tf_op jit(solution)/shard_map/ppermute | solution.py:525
  9.1 0.0 copy-start.7
  9.1 0.0 copy-start.8
  9.1 0.0 copy-start.9
  9.1 0.0 copy-start.12
  9.1 0.0 copy-start.13
  9.1 0.0 copy-start.17
  9.2 5.6 %shard_map.259.refs_4_ = bf16[16,128,128]{2,1,0:T(8,128)(2,1)} custom-call(bf16[128,128,128]{2,1,0:T(8,128)(2,1)} %tile_hbm.1, f32[1,128]{1,0:T(1,128)} %bitcast.33, bf16[16,128]{1,0:T(8,128)(2,1)} %bitcast.32), custom_call_target="tpu_custom_call" | custom-call | flops 5000000000 | bytes 15000000 | tf_op jit(solution)/shard_map/pallas_call | solution.py:606
  14.7 1.6 %collective-permute-start.6 = (bf16[16,128,128]{2,1,0:T(8,128)(2,1)}, bf16[16,128,128]{2,1,0:T(8,128)(2,1)S(1)}, u32[]{:S(2)}, u32[]{:S(2)}) collective-permute-start(bf16[16,128,128]{2,1,0:T(8,128)(2,1)} %shard_map.259.refs_4_), channel_id=1, source_target_pairs={{0,8},{4,12},{8,0},{12,4},{1,9},{5,13},{9,1},{13,5},{2,10},{6,14},... | collective-permute-start | bytes 1572872 | tf_op jit(solution)/shard_map/ppermute | solution.py:539
  16.3 0.1 pad_add_fusion.place_ref.refs_0_
  16.5 0.0 copy-start
  16.5 0.0 copy-start.14
  16.5 0.0 slice-start
  16.6 4.4 %shard_map.258 = (f32[1024,128]{1,0:T(8,128)S(1)}, f32[128,768]{1,0:T(8,128)S(1)}, bf16[128,768]{1,0:T(8,128)(2,1)S(1)}, bf16[128,1024]{1,0:T(8,128)(2,1)S(1)}) custom-call(s32[3]{0:T(128)S(1)} %pad_add_fusion.place_ref.refs_0_, s32[32]{0:T(128)S(1)} %copy-done.17, f32[1,1]{1,0:T(1,128)} %bitcast.13.level_ref, f32[1024,128]{1,0:T(8,128)S(1)} %copy-done.19, ...), custom_call_target="tpu_custom_call" | custom-call | flops 3400000000 | bytes 10200000 | tf_op jit(solution)/shard_map/pallas_call | solution.py:622
  20.9 1.0 %collective-permute-start.2 = (bf16[128,768]{1,0:T(8,128)(2,1)S(1)}, bf16[128,768]{1,0:T(8,128)(2,1)S(1)}, u32[]{:S(2)}, u32[]{:S(2)}) collective-permute-start(bf16[128,768]{1,0:T(8,128)(2,1)S(1)} %get-tuple-element.26.refs_1_), channel_id=1, source_target_pairs={{0,2},{1,3},{2,0},{3,1},{4,6},{5,7},{6,4},{7,5},{8,10},{9,11},{10,... | collective-permute-start | bytes 589832 | tf_op jit(solution)/shard_map/ppermute | solution.py:539
  22.0 3.4 %collective-permute-start.4 = (bf16[128,768]{1,0:T(8,128)(2,1)S(1)}, bf16[128,768]{1,0:T(8,128)(2,1)S(1)}, u32[]{:S(2)}, u32[]{:S(2)}) collective-permute-start(bf16[128,768]{1,0:T(8,128)(2,1)S(1)} %get-tuple-element.26.refs_1_), channel_id=1, source_target_pairs={{0,1},{1,0},{2,3},{3,2},{4,5},{5,4},{6,7},{7,6},{8,9},{9,8},{10,11... | collective-permute-start | bytes 589832 | tf_op jit(solution)/shard_map/ppermute | solution.py:539
  25.3 6.9 %collective-permute-done.2.refs_3_ = bf16[128,768]{1,0:T(8,128)(2,1)S(1)} collective-permute-done((bf16[128,768]{1,0:T(8,128)(2,1)S(1)}, bf16[128,768]{1,0:T(8,128)(2,1)S(1)}, u32[]{:S(2)}, u32[]{:S(2)}) %collective-permute-start.2) | collective-permute-done | bytes 196640 | tf_op jit(solution)/shard_map/ppermute | solution.py:539
  32.3 0.1 collective-permute-done.4.refs_2_
  32.4 0.0 collective-permute-start.3
  32.4 1.9 %collective-permute-done.7.refs_7_ = bf16[16,128,128]{2,1,0:T(8,128)(2,1)S(1)} collective-permute-done((bf16[16,128,128]{2,1,0:T(8,128)(2,1)S(1)}, bf16[16,128,128]{2,1,0:T(8,128)(2,1)S(1)}, u32[]{:S(2)}, u32[]{:S(2)}) %collective-permute-start.7) | collective-permute-done | bytes 524320 | tf_op jit(solution)/shard_map/ppermute | solution.py:539
  34.3 0.0 copy-start.2
  34.3 0.0 copy-start.6
  34.3 4.3 %shard_map.260 = (bf16[128,768]{1,0:T(8,128)(2,1)S(1)}, f32[128,768]{1,0:T(8,128)S(1)}, f32[16,128,128]{2,1,0:T(8,128)S(1)}, f32[16,128,128]{2,1,0:T(8,128)S(1)}, bf16[1,16,128,128]{3,2,1,0:T(8,128)(2,1)S(1)}) custom-call(s32[3]{0:T(128)S(1)} %pad_add_fusion.place_ref.refs_0_, bf16[128,768]{1,0:T(8,128)(2,1)S(1)} %get-tuple-element.26.refs_1_, ...), custom_call_target="tpu_custom_call" | custom-call | flops 4000000000 | bytes 12000000 | tf_op jit(solution)/shard_map/pallas_call | solution.py:656
  38.6 1.0 %collective-permute-done.3.refs_1_ = bf16[128,768]{1,0:T(8,128)(2,1)S(1)} collective-permute-done((bf16[128,768]{1,0:T(8,128)(2,1)S(1)}, bf16[128,768]{1,0:T(8,128)(2,1)S(1)}, u32[]{:S(2)}, u32[]{:S(2)}) %collective-permute-start.3) | collective-permute-done | bytes 196640 | tf_op jit(solution)/shard_map/ppermute | solution.py:539
  39.7 0.0 copy-start.11
  39.8 0.0 copy-start.16
  39.8 5.0 %shard_map.261 = (bf16[1,128,768]{2,1,0:T(8,128)(2,1)}, f32[1024,128]{1,0:T(8,128)S(1)}, bf16[1024,128]{1,0:T(8,128)(2,1)S(1)}, bf16[96,128]{1,0:T(8,128)(2,1)S(1)}, bf16[96,128]{1,0:T(8,128)(2,1)S(1)}) custom-call(s32[3]{0:T(128)S(1)} %pad_add_fusion.place_ref.refs_0_, bf16[128,768]{1,0:T(8,128)(2,1)S(1)} %collective-permute-done.3.refs_1_, ...), custom_call_target="tpu_custom_call" | custom-call | flops 6000000000 | bytes 18000000 | tf_op jit(solution)/shard_map/pallas_call | solution.py:676
  44.8 0.3 collective-permute-start.8
  45.0 3.5 %collective-permute-start.9 = (bf16[96,128]{1,0:T(8,128)(2,1)S(1)}, bf16[96,128]{1,0:T(8,128)(2,1)S(1)}, u32[]{:S(2)}, u32[]{:S(2)}) collective-permute-start(bf16[96,128]{1,0:T(8,128)(2,1)S(1)} %get-tuple-element.41), channel_id=1, source_target_pairs={{1,0},{2,1},{3,2},{0,3},{5,4},{6,5},{7,6},{4,7},{9,8},{10,9},{11,1... | collective-permute-start | bytes 73736 | tf_op jit(solution)/shard_map/ppermute | solution.py:525
  48.6 2.6 %shard_map.262.inner_ref = f32[3,1,1024]{2,1,0:T(1,128)S(1)} custom-call(s32[3]{0:T(128)S(1)} %pad_add_fusion.place_ref.refs_0_, s32[32]{0:T(128)S(1)} %copy-done.17, f32[1,1]{1,0:T(1,128)} %bitcast.14.level_ref, f32[3,1,1024]{2,1,0:T(1,128)S(1)} %bitcast.22, f32[3,1,1024]{2,1,0:T(1,128)S(1)} %bitcast.25, f32[1024,128]{1,0:T(8,128)S(1)} %get-tuple-element.38.state_ref, ...), custom_call_target="tpu_custom_call" | custom-call | flops 2700000000 | bytes 8100000 | tf_op jit(solution)/shard_map/pallas_call | solution.py:704
  51.2 2.5 %shard_map.263 = f32[3,1,1024]{2,1,0:T(1,128)} custom-call(s32[3]{0:T(128)S(1)} %pad_add_fusion.place_ref.refs_0_, s32[32]{0:T(128)S(1)} %copy-done.17, f32[1,1]{1,0:T(1,128)} %bitcast.15.level_ref, f32[3,1,1024]{2,1,0:T(1,128)S(1)} %bitcast.23, f32[3,1,1024]{2,1,0:T(1,128)S(1)} %bitcast.26, f32[1024,128]{1,0:T(8,128)S(1)} %get-tuple-element.38.state_ref, ...), custom_call_target="tpu_custom_call" | custom-call | flops 2000000000 | bytes 6000000 | tf_op jit(solution)/shard_map/pallas_call | solution.py:715
  (46 shorter events, 0.1 us)
Async XLA Ops:
  4.0 12.4 %collective-permute-start.1 = (bf16[96,128]{1,0:T(8,128)(2,1)}, bf16[96,128]{1,0:T(8,128)(2,1)S(1)}, u32[]{:S(2)}, u32[]{:S(2)}) collective-permute-start(bf16[96,128]{1,0:T(8,128)(2,1)} %get-tuple-element.25), channel_id=1, source_target_pairs={{1,0},{2,1},{3,2},{0,3},{5,4},{6,5},{7,6},{4,7},{9,8},{10,9},{11,1... | collective-permute-start | bytes 73736 | tf_op jit(solution)/shard_map/ppermute | solution.py:525
  9.1 7.3 %collective-permute-start = (bf16[96,128]{1,0:T(8,128)(2,1)}, bf16[96,128]{1,0:T(8,128)(2,1)S(1)}, u32[]{:S(2)}, u32[]{:S(2)}) collective-permute-start(bf16[96,128]{1,0:T(8,128)(2,1)} %get-tuple-element.23), channel_id=1, source_target_pairs={{0,1},{1,2},{2,3},{3,0},{4,5},{5,6},{6,7},{7,4},{8,9},{9,10},{10,1... | collective-permute-start | bytes 73736 | tf_op jit(solution)/shard_map/ppermute | solution.py:524
  9.1 7.3 %copy-start.21 = (f32[768]{0:T(1024)S(1)}, f32[768]{0:T(1024)}, u32[]{:S(2)}) copy-start(f32[768]{0:T(1024)} %param.41) | copy-start | bytes 9220
  9.1 7.3 %copy-start.4 = (bf16[128,768]{1,0:T(8,128)(2,1)S(1)}, bf16[128,768]{1,0:T(8,128)(2,1)}, u32[]{:S(2)}) copy-start(bf16[128,768]{1,0:T(8,128)(2,1)} %lift_hbm.1) | copy-start | bytes 589828
  9.1 7.3 %copy-start.5 = (bf16[128,768]{1,0:T(8,128)(2,1)S(1)}, bf16[128,768]{1,0:T(8,128)(2,1)}, u32[]{:S(2)}) copy-start(bf16[128,768]{1,0:T(8,128)(2,1)} %single_hbm.3) | copy-start | bytes 589828
  9.1 7.3 %copy-start.7 = (bf16[2,128,384]{2,1,0:T(8,128)(2,1)S(1)}, bf16[2,128,384]{2,1,0:T(8,128)(2,1)}, u32[]{:S(2)}) copy-start(bf16[2,128,384]{2,1,0:T(8,128)(2,1)} %w_qkv_ref.5) | copy-start | bytes 589828
  9.1 7.3 %copy-start.8 = (bf16[2,128,128]{2,1,0:T(8,128)(2,1)S(1)}, bf16[2,128,128]{2,1,0:T(8,128)(2,1)}, u32[]{:S(2)}) copy-start(bf16[2,128,128]{2,1,0:T(8,128)(2,1)} %w_out_ref.5) | copy-start | bytes 196612
  9.1 7.3 %copy-start.9 = (s32[4096]{0:T(1024)S(1)}, s32[4096]{0:T(1024)}, u32[]{:S(2)}) copy-start(s32[4096]{0:T(1024)} %param.34) | copy-start | bytes 49156
  9.1 7.3 %copy-start.12 = (f32[2,768]{1,0:T(2,128)S(1)}, f32[2,768]{1,0:T(2,128)}, u32[]{:S(2)}) copy-start(f32[2,768]{1,0:T(2,128)} %refs_11_.1) | copy-start | bytes 18436
  9.1 7.3 %copy-start.13 = (s32[1024]{0:T(1024)S(1)}, s32[1024]{0:T(1024)}, u32[]{:S(2)}) copy-start(s32[1024]{0:T(1024)} %param.32) | copy-start | bytes 12292
  9.1 7.3 %copy-start.17 = (s32[32]{0:T(128)S(1)}, s32[32]{0:T(128)}, u32[]{:S(2)}) copy-start(s32[32]{0:T(128)} %offsets_ref.5) | copy-start | bytes 388
  9.2 7.3 %copy-start.19 = (f32[1024,128]{1,0:T(8,128)S(1)}, f32[1024,128]{1,0:T(8,128)}, u32[]{:S(2)}) copy-start(f32[1024,128]{1,0:T(8,128)} %get-tuple-element.22.state_ref) | copy-start | bytes 1572868
  9.2 7.3 %copy-start.20 = (bf16[1024,128]{1,0:T(8,128)(2,1)S(1)}, bf16[1024,128]{1,0:T(8,128)(2,1)}, u32[]{:S(2)}) copy-start(bf16[1024,128]{1,0:T(8,128)(2,1)} %get-tuple-element.24.mid_ref) | copy-start | bytes 786436
  14.7 17.6 %collective-permute-start.6 = (bf16[16,128,128]{2,1,0:T(8,128)(2,1)}, bf16[16,128,128]{2,1,0:T(8,128)(2,1)S(1)}, u32[]{:S(2)}, u32[]{:S(2)}) collective-permute-start(bf16[16,128,128]{2,1,0:T(8,128)(2,1)} %shard_map.259.refs_4_), channel_id=1, source_target_pairs={{0,8},{4,12},{8,0},{12,4},{1,9},{5,13},{9,1},{13,5},{2,10},{6,14},... | collective-permute-start | bytes 1572872 | tf_op jit(solution)/shard_map/ppermute | solution.py:539
  16.5 8.8 %copy-start.3 = (bf16[16,128,128]{2,1,0:T(8,128)(2,1)S(1)}, bf16[16,128,128]{2,1,0:T(8,128)(2,1)}, u32[]{:S(2)}) copy-start(bf16[16,128,128]{2,1,0:T(8,128)(2,1)} %shard_map.259.refs_4_) | copy-start | bytes 1572868
  16.5 17.8 %copy-start = (bf16[768,2304]{1,0:T(8,128)(2,1)S(1)}, bf16[768,2304]{1,0:T(8,128)(2,1)}, u32[]{:S(2)}) copy-start(bf16[768,2304]{1,0:T(8,128)(2,1)} %refs_9_.3) | copy-start | bytes 10616836
  16.5 17.8 %copy-start.14 = (s32[512]{0:T(512)S(1)}, s32[512]{0:T(512)}, u32[]{:S(2)}) copy-start(s32[512]{0:T(512)} %param.35) | copy-start | bytes 6148
  16.5 23.1 %slice-start = ((s8[4718592]{0:T(1024)(128)(4,1)}), s8[4194304]{0:T(1024)(128)(4,1)S(1)}, s32[]{:S(2)}) async-start(s8[4718592]{0:T(1024)(128)(4,1)} %bitcast.16), calls=%async_computation | async-start | bytes 8388608
  20.9 11.4 %collective-permute-start.2 = (bf16[128,768]{1,0:T(8,128)(2,1)S(1)}, bf16[128,768]{1,0:T(8,128)(2,1)S(1)}, u32[]{:S(2)}, u32[]{:S(2)}) collective-permute-start(bf16[128,768]{1,0:T(8,128)(2,1)S(1)} %get-tuple-element.26.refs_1_), channel_id=1, source_target_pairs={{0,2},{1,3},{2,0},{3,1},{4,6},{5,7},{6,4},{7,5},{8,10},{9,11},{10,... | collective-permute-start | bytes 589832 | tf_op jit(solution)/shard_map/ppermute | solution.py:539
  22.0 10.4 %collective-permute-start.4 = (bf16[128,768]{1,0:T(8,128)(2,1)S(1)}, bf16[128,768]{1,0:T(8,128)(2,1)S(1)}, u32[]{:S(2)}, u32[]{:S(2)}) collective-permute-start(bf16[128,768]{1,0:T(8,128)(2,1)S(1)} %get-tuple-element.26.refs_1_), channel_id=1, source_target_pairs={{0,1},{1,0},{2,3},{3,2},{4,5},{5,4},{6,7},{7,6},{8,9},{9,8},{10,11... | collective-permute-start | bytes 589832 | tf_op jit(solution)/shard_map/ppermute | solution.py:539
  25.3 7.1 %collective-permute-start.5 = (bf16[16,128,128]{2,1,0:T(8,128)(2,1)S(1)}, bf16[16,128,128]{2,1,0:T(8,128)(2,1)S(1)}, u32[]{:S(2)}, u32[]{:S(2)}) collective-permute-start(bf16[16,128,128]{2,1,0:T(8,128)(2,1)S(1)} %copy-done.3), channel_id=1, source_target_pairs={{0,4},{4,0},{8,12},{12,8},{1,5},{5,1},{9,13},{13,9},{2,6},{6,2},{1... | collective-permute-start | bytes 1572872 | tf_op jit(solution)/shard_map/ppermute | solution.py:539
  32.4 1.9 %collective-permute-start.7 = (bf16[16,128,128]{2,1,0:T(8,128)(2,1)S(1)}, bf16[16,128,128]{2,1,0:T(8,128)(2,1)S(1)}, u32[]{:S(2)}, u32[]{:S(2)}) collective-permute-start(bf16[16,128,128]{2,1,0:T(8,128)(2,1)S(1)} %collective-permute-done.6.refs_6_), channel_id=1, source_target_pairs={{0,4},{4,0},{8,12},{12,8},{1,5},{5,1},{9,13},{13,9},{2,6},{6,2},{1... | collective-permute-start | bytes 1572872 | tf_op jit(solution)/shard_map/ppermute | solution.py:539
  32.4 7.3 %collective-permute-start.3 = (bf16[128,768]{1,0:T(8,128)(2,1)S(1)}, bf16[128,768]{1,0:T(8,128)(2,1)S(1)}, u32[]{:S(2)}, u32[]{:S(2)}) collective-permute-start(bf16[128,768]{1,0:T(8,128)(2,1)S(1)} %collective-permute-done.2.refs_3_), channel_id=1, source_target_pairs={{0,1},{1,0},{2,3},{3,2},{4,5},{5,4},{6,7},{7,6},{8,9},{9,8},{10,11... | collective-permute-start | bytes 589832 | tf_op jit(solution)/shard_map/ppermute | solution.py:539
  34.3 5.4 %slice-start.1 = ((s8[4718592]{0:T(1024)(128)(4,1)}), s8[524288]{0:T(1024)(128)(4,1)S(1)}, s32[]{:S(2)}) async-start(s8[4718592]{0:T(1024)(128)(4,1)} %bitcast.16), calls=%async_computation.1 | async-start | bytes 1048576
  34.3 5.4 %copy-start.1 = (bf16[1536,768]{1,0:T(8,128)(2,1)S(1)}, bf16[1536,768]{1,0:T(8,128)(2,1)}, u32[]{:S(2)}) copy-start(bf16[1536,768]{1,0:T(8,128)(2,1)} %refs_13_.1) | copy-start | bytes 7077892
  34.3 5.4 %copy-start.2 = (bf16[768,768]{1,0:T(8,128)(2,1)S(1)}, bf16[768,768]{1,0:T(8,128)(2,1)}, u32[]{:S(2)}) copy-start(bf16[768,768]{1,0:T(8,128)(2,1)} %refs_10_.1) | copy-start | bytes 3538948
  39.7 8.9 %copy-start.10 = (f32[1,3,1024]{2,0,1:T(1,128)S(1)}, f32[1,3,1024]{2,0,1:T(1,128)}, u32[]{:S(2)}) copy-start(f32[1,3,1024]{2,0,1:T(1,128)} %param.26) | copy-start | bytes 36868
  39.7 8.8 %copy-start.11 = (f32[1,3,1024]{2,0,1:T(1,128)S(1)}, f32[1,3,1024]{2,0,1:T(1,128)}, u32[]{:S(2)}) copy-start(f32[1,3,1024]{2,0,1:T(1,128)} %param.27) | copy-start | bytes 36868
  39.8 8.8 %copy-start.16 = (bf16[3,128]{1,0:T(4,128)(2,1)S(1)}, bf16[3,128]{1,0:T(4,128)(2,1)}, u32[]{:S(2)}) copy-start(bf16[3,128]{1,0:T(4,128)(2,1)} %coord_out_ref.3) | copy-start | bytes 2308
  39.8 8.8 %copy-start.18 = (f32[128]{0:T(128)S(1)}, f32[128]{0:T(128)}, u32[]{:S(2)}) copy-start(f32[128]{0:T(128)} %param.50) | copy-start | bytes 1540
  44.8 6.5 %collective-permute-start.8 = (bf16[96,128]{1,0:T(8,128)(2,1)S(1)}, bf16[96,128]{1,0:T(8,128)(2,1)S(1)}, u32[]{:S(2)}, u32[]{:S(2)}) collective-permute-start(bf16[96,128]{1,0:T(8,128)(2,1)S(1)} %get-tuple-element.39), channel_id=1, source_target_pairs={{0,1},{1,2},{2,3},{3,0},{4,5},{5,6},{6,7},{7,4},{8,9},{9,10},{10,1... | collective-permute-start | bytes 73736 | tf_op jit(solution)/shard_map/ppermute | solution.py:524
  45.0 6.2 %collective-permute-start.9 = (bf16[96,128]{1,0:T(8,128)(2,1)S(1)}, bf16[96,128]{1,0:T(8,128)(2,1)S(1)}, u32[]{:S(2)}, u32[]{:S(2)}) collective-permute-start(bf16[96,128]{1,0:T(8,128)(2,1)S(1)} %get-tuple-element.41), channel_id=1, source_target_pairs={{1,0},{2,1},{3,2},{0,3},{5,4},{6,5},{7,6},{4,7},{9,8},{10,9},{11,1... | collective-permute-start | bytes 73736 | tf_op jit(solution)/shard_map/ppermute | solution.py:525
  (2 other events, 10.8 us)

commit v4 on v3

--- a/solution.py
+++ b/solution.py
@@ -79,18 +79,29 @@
     return jnp.concatenate([ref[k] for k in range(ref.shape[0])], axis=0)
 
 
-def write_edges(normed, low_edge_ref, high_edge_ref):
-    low_edge_ref[...] = normed[:HALO]
-    high_edge_ref[...] = normed[normed.shape[0] - HALO :]
+def write_edges(normed, row, first_edge_ref, second_edge_ref):
+    even = row % 2 == 0
+    low, high = normed[:HALO], normed[normed.shape[0] - HALO :]
+    first_edge_ref[...] = jnp.where(even, high, low)
+    second_edge_ref[...] = jnp.where(even, low, high)
+
+
+def halo_rows(row, count, first_ref, second_ref):
+    even = row % 2 == 0
+    low = jnp.where(even, second_ref[...], first_ref[...])
+    high = jnp.where(even, first_ref[...], second_ref[...])
+    low = jnp.where(row == 0, jnp.zeros_like(low), low)
+    high = jnp.where(row == count - 1, jnp.zeros_like(high), high)
+    return low, high
 
 
 def prepare_kernel(
-    level_ref, coords_hbm, kicks_hbm, single_hbm, coord_in_hbm, gain_hbm, state_ref, normed_ref, low_edge_ref, high_edge_ref,
-    coords_ref, kicks_ref, single_ref, coord_in_ref, gain_ref, sems
+    level_hbm, coords_hbm, kicks_hbm, single_hbm, coord_in_hbm, gain_hbm, state_ref, normed_ref, second_edge_ref, first_edge_ref,
+    level_ref, coords_ref, kicks_ref, single_ref, coord_in_ref, gain_ref, sems
 ):
     copies = fetch(
-        [coords_hbm, kicks_hbm, single_hbm, coord_in_hbm, gain_hbm],
-        [coords_ref, kicks_ref, single_ref, coord_in_ref, gain_ref], sems,
+        [level_hbm, coords_hbm, kicks_hbm, single_hbm, coord_in_hbm, gain_hbm],
+        [level_ref, coords_ref, kicks_ref, single_ref, coord_in_ref, gain_ref], sems,
     )
     for copy in copies:
         copy.wait()
@@ -103,7 +114,7 @@
     state_ref[...] = state
     normed = norm_rows(state, gain_ref[0:1]).astype(BF16)
     normed_ref[...] = normed
-    write_edges(normed, low_edge_ref, high_edge_ref)
+    write_edges(normed, lax.axis_index("row"), first_edge_ref, second_edge_ref)
 
 
 def pair_kernel(step_rows, tile_hbm, gain_hbm, heads_hbm, bias_ref, tile_ref, gain_ref, heads_ref, tile_sems, sems):
@@ -145,6 +156,7 @@
 
 def attend(queries, blocks, parts, lives, w_kv, offsets_ref, scratch):
     key_scr, value_scr, live_scr, score_scr, prob_scr, out_scr = scratch
+    offsets = offsets_ref[...]
     row_count, width = queries.shape
     block_count = len(blocks)
     head_size = width // AHEADS
@@ -167,7 +179,7 @@
     ones = jnp.ones((WK, width), BF16)
     begins = []
     for b, (block, shift) in enumerate(blocks):
-        begin = block * WQ + shift + offsets_ref[block]
+        begin = block * WQ + shift + offsets[0, block]
         begins.append(begin)
         keys = key_scr[pl.ds(begin, WK), :].astype(BF16)
         live = live_scr[pl.ds(begin, WK), :].astype(BF16)
@@ -220,19 +232,16 @@
 
 
 def encoder_kernel(
-    place_ref, offsets_ref, level_ref, state_ref, low_ref, mid_ref, high_ref, mask_ref, token_ref, w_qkv_ref, w_out_ref,
-    lift_hbm, single_hbm, embed_ref, gain_ref, encoded_ref, token_state_ref, normed_ref, member_ref, lift_ref, single_ref, sems,
-    *scratch
+    offsets_ref, level_ref, state_ref, low_ref, mid_ref, high_ref, mask_ref, token_ref, w_qkv_ref, w_out_ref,
+    lift_ref, single_ref, embed_ref, gain_ref, encoded_ref, token_state_ref, normed_ref, member_ref, *scratch
 ):
-    late = fetch([lift_hbm, single_hbm], [lift_ref, single_ref], sems)
-    row, count = place_ref[0], place_ref[1]
+    row, count = lax.axis_index("row"), lax.axis_size("row")
     first, last = row == 0, row == count - 1
     tok_rows = single_ref.shape[0]
     chunks = token_ref.shape[0]
     width = state_ref.shape[1]
     begin = row * chunks
-    low = jnp.where(first, jnp.zeros_like(low_ref[...]), low_ref[...])
-    high = jnp.where(last, jnp.zeros_like(high_ref[...]), high_ref[...])
+    low, high = halo_rows(row, count, low_ref, high_ref)
     mid = mid_ref[...]
     lives = [live_bias(mask_ref, begin - 1, first)[LANES - HALO :]]
     lives += [live_bias(mask_ref, begin + chunk, False) for chunk in range(chunks)]
@@ -244,8 +253,6 @@
     )
     state = state_ref[...] + dot(mixed, w_out_ref[0])
     encoded_ref[...] = state
-    for copy in late:
-        copy.wait()
     lifted = jnp.maximum(dot(state.astype(BF16), lift_ref[...]), 0.0).astype(BF16)
     member = member_of(token_ref, mask_ref, begin, row * tok_rows, tok_rows)
     member_ref[...] = member
@@ -322,14 +329,13 @@
 
 
 def attend_first_kernel(near_count, row_count, smp_count, *refs):
-    place_ref = refs[0]
-    normed_refs = refs[1 : 1 + near_count]
-    bias_refs = refs[1 + near_count : 1 + near_count + smp_count]
+    normed_refs = refs[:near_count]
+    bias_refs = refs[near_count : near_count + smp_count]
     (
         key_mask_ref, w_qkv_ref, query_ref, mixed_ref, largest_ref, total_ref, far_bias_ref, kv_scr, score_scr, prob_scr,
         bias_scr,
-    ) = refs[1 + near_count + smp_count :]
-    row, smp = place_ref[0], place_ref[2]
+    ) = refs[near_count + smp_count :]
+    row, smp = lax.axis_index("row"), lax.axis_index("smp")
     tok_rows, width = query_ref.shape
     head_size = width // HEADS
     piece = key_mask_ref.shape[1]
@@ -374,14 +380,13 @@
 
 def token_kernel(near_count, row_count, *refs):
     far_count = row_count - near_count
-    place_ref = refs[0]
-    normed_refs = refs[1 : 1 + far_count]
+    normed_refs = refs[:far_count]
     (
         query_ref, carried_ref, largest_ref, total_ref, bias_ref, state_ref, key_mask_ref, w_qkv_ref, w_proj_ref, gain_ref, ffn_in_ref,
         ffn_out_ref, spread_ref, encoded_ref, member_ref, atom_gain_ref, out_ref, joined_ref, atom_normed_ref,
-        low_edge_ref, high_edge_ref, kv_scr, score_scr, prob_scr, shrink_scr,
-    ) = refs[1 + far_count :]
-    row = place_ref[0]
+        second_edge_ref, first_edge_ref, kv_scr, score_scr, prob_scr, shrink_scr,
+    ) = refs[far_count:]
+    row = lax.axis_index("row")
     tok_rows, width = state_ref.shape
     head_size = width // HEADS
     piece = key_mask_ref.shape[1]
@@ -436,7 +441,7 @@
     joined_ref[...] = joined
     normed = norm_rows(joined, atom_gain_ref[1:2]).astype(BF16)
     atom_normed_ref[...] = normed
-    write_edges(normed, low_edge_ref, high_edge_ref)
+    write_edges(normed, row, first_edge_ref, second_edge_ref)
 
 
 def directions(state, level_ref, coords_ref, kicks_ref, gain_ref, coord_out_ref, direction_ref, begin):
@@ -455,12 +460,12 @@
 
 
 def inner_kernel(
-    place_ref, offsets_ref, level_ref, coords_ref, kicks_ref, state_ref, mid_ref, mask_ref, w_qkv_ref, w_out_ref, gain_ref,
+    offsets_ref, level_ref, coords_ref, kicks_ref, state_ref, mid_ref, mask_ref, w_qkv_ref, w_out_ref, gain_ref,
     coord_out_ref, direction_ref, *scratch
 ):
     atoms, width = state_ref.shape
     chunks = atoms // LANES
-    begin = place_ref[0] * chunks
+    begin = lax.axis_index("row") * chunks
     edge = LANES
     skip = edge - HALO
     lives = [live_bias(mask_ref, begin, False)[skip:]]
@@ -477,10 +482,10 @@
 
 
 def edge_kernel(
-    place_ref, offsets_ref, level_ref, coords_ref, kicks_ref, state_ref, low_ref, mid_ref, high_ref, mask_ref, w_qkv_ref,
+    offsets_ref, level_ref, coords_ref, kicks_ref, state_ref, low_ref, mid_ref, high_ref, mask_ref, w_qkv_ref,
     w_out_ref, gain_ref, coord_out_ref, inner_ref, direction_ref, *scratch
 ):
-    row, count = place_ref[0], place_ref[1]
+    row, count = lax.axis_index("row"), lax.axis_size("row")
     first, last = row == 0, row == count - 1
     atoms, width = state_ref.shape
     chunks = atoms // LANES
@@ -491,8 +496,7 @@
     w_out = w_out_ref[1]
     for k in range(direction_ref.shape[0]):
         direction_ref[k, :, edge : atoms - edge] = inner_ref[k, :, edge : atoms - edge]
-    low = jnp.where(first, jnp.zeros_like(low_ref[...]), low_ref[...])
-    high = jnp.where(last, jnp.zeros_like(high_ref[...]), high_ref[...])
+    low, high = halo_rows(row, count, low_ref, high_ref)
     lives = [
         live_bias(mask_ref, begin - 1, first)[LANES - HALO :],
         live_bias(mask_ref, begin, False),
@@ -517,13 +521,12 @@
     directions(upper, level_ref, coords_ref, kicks_ref, gain_ref, coord_out_ref, direction_ref, atoms - edge)
 
 
-def halos_of(low_edge, high_edge):
+def halos_of(first_edge, second_edge):
     count = lax.axis_size("row")
-    up = [(i, (i + 1) % count) for i in range(count)]
-    down = [((i + 1) % count, i) for i in range(count)]
-    low = lax.ppermute(high_edge, "row", up)
-    high = lax.ppermute(low_edge, "row", down)
-    return low, high
+    second = [(0, 0), (count - 1, count - 1)]
+    second += [(i, i + 1 if i % 2 else i - 1) for i in range(1, count - 1)]
+    from_second = lax.ppermute(second_edge, "row", second)
+    return lax.ppermute(first_edge, "row", [(i, i ^ 1) for i in range(count)]), from_second
 
 
 def spread_over(block, axis, after=None):
@@ -574,35 +577,31 @@
     tok_rows, token_width = token_single.shape
     heads = pair_heads.shape[1]
     keys = pair_cond.shape[1]
-    place = jnp.stack(
-        [lax.axis_index("row"), jnp.int32(row_count), lax.axis_index("smp")]
-    ).astype(jnp.int32)
     level = noise_level.reshape(1, 1)
     coords = positions.transpose(1, 0, 2)
     kicks = noise_draw.transpose(1, 0, 2)
     mask = atom_mask.reshape(-1, LANES)
     tokens = atom_to_token.reshape(-1, LANES)
-    smem = pl.BlockSpec(memory_space=pltpu.SMEM)
     shape = jax.ShapeDtypeStruct
     state_like = shape((atoms, width), F32)
     normed_like = shape((atoms, width), BF16)
     edge_like = shape((HALO, width), BF16)
 
-    state, normed, low_edge, high_edge = pl.pallas_call(
+    state, normed, second_edge, first_edge = pl.pallas_call(
         prepare_kernel,
         out_shape=(state_like, normed_like, edge_like, edge_like),
-        in_specs=whole(1) + hbm(5),
+        in_specs=hbm(6),
         out_specs=tuple(whole(4)),
-        scratch_shapes=[pltpu.VMEM(a.shape, a.dtype) for a in (coords, kicks, atom_single, coord_in, atom_gain)]
-        + [pltpu.SemaphoreType.DMA((5,))],
+        scratch_shapes=[pltpu.VMEM(a.shape, a.dtype) for a in (level, coords, kicks, atom_single, coord_in, atom_gain)]
+        + [pltpu.SemaphoreType.DMA((6,))],
         compiler_params=vmem(PRIVATE),
         cost_estimate=cost(1.5),
     )(level, coords, kicks, atom_single, coord_in, atom_gain)
-    low, high = halos_of(low_edge, high_edge)
+    low, high = halos_of(first_edge, second_edge)
 
     pair_rows, _, channels = pair_cond.shape
     step_rows = 32
-    gain_row, _ = lax.optimization_barrier((pair_gain, low_edge))
+    gain_row, _ = lax.optimization_barrier((pair_gain, second_edge))
     bias = pl.pallas_call(
         functools.partial(pair_kernel, step_rows),
         out_shape=shape((heads, pair_rows, keys), BF16),
@@ -627,18 +626,13 @@
             shape((tok_rows, token_width), BF16),
             shape((tok_rows, atoms), BF16),
         ),
-        in_specs=[smem, smem] + whole(9) + hbm(2) + whole(2),
+        in_specs=whole(1) + whole(13),
         out_specs=tuple(whole(4)),
-        scratch_shapes=[
-            pltpu.VMEM(gather_in.shape, BF16),
-            pltpu.VMEM(token_single.shape, BF16),
-            pltpu.SemaphoreType.DMA((2,)),
-        ]
-        + window_scratch(atoms + 2 * HALO, atoms, width),
+        scratch_shapes=window_scratch(atoms + 2 * HALO, atoms, width),
         compiler_params=vmem(16),
         cost_estimate=cost(3.4),
     )(
-        place, window_offsets, level, state, low, normed, high, mask, tokens, atom_qkv, atom_proj, gather_in,
+        window_offsets.reshape(1, -1), level, state, low, normed, high, mask, tokens, atom_qkv, atom_proj, gather_in,
         token_single, noise_embed.reshape(1, -1), token_gain,
     )
     gathered = spread_over(token_normed, "row")
@@ -662,7 +656,7 @@
             shape((heads, tok_rows, LANES), F32),
             shape((far_count * pieces, heads, tok_rows, keys), BF16),
         ),
-        in_specs=[smem] + whole(near_count + smp_count + 2),
+        in_specs=whole(near_count + smp_count + 2),
         out_specs=tuple(whole(5)),
         scratch_shapes=[
             pltpu.VMEM((near_count * tok_rows, 2 * token_width), BF16),
@@ -672,8 +666,8 @@
         ],
         compiler_params=vmem(14 + need(near_count * pieces) * 3 // 2),
         cost_estimate=cost(4),
-    )(place, *gathered[:near_count], *biases, key_mask, token_qkv)
-    token_result, joined, atom_normed, low_edge, high_edge = pl.pallas_call(
+    )(*gathered[:near_count], *biases, key_mask, token_qkv)
+    token_result, joined, atom_normed, second_edge, first_edge = pl.pallas_call(
         functools.partial(token_kernel, near_count, row_count),
         out_shape=(
             shape((1, tok_rows, token_width), BF16),
@@ -682,7 +676,7 @@
             edge_like,
             edge_like,
         ),
-        in_specs=[smem] + whole(far_count + 16),
+        in_specs=whole(far_count + 16),
         out_specs=tuple(whole(5)),
         scratch_shapes=[
             pltpu.VMEM((far_count * tok_rows, 2 * token_width), BF16),
@@ -693,10 +687,10 @@
         compiler_params=vmem(20 + need(far_count * pieces)),
         cost_estimate=cost(6),
     )(
-        place, *gathered[near_count:], queries, carried, largest, total, far_bias, token_state, key_mask, token_qkv, token_proj,
+        *gathered[near_count:], queries, carried, largest, total, far_bias, token_state, key_mask, token_qkv, token_proj,
         token_gain, ffn_in, ffn_out, scatter_out, encoded, member, atom_gain,
     )
-    low, high = halos_of(low_edge, high_edge)
+    low, high = halos_of(first_edge, second_edge)
 
     edge = LANES
     direction_like = shape(coords.shape, F32)
@@ -704,24 +698,24 @@
     inner = pl.pallas_call(
         inner_kernel,
         out_shape=direction_like,
-        in_specs=[smem, smem] + whole(10),
+        in_specs=whole(1) + whole(10),
         out_specs=whole(1)[0],
         scratch_shapes=window_scratch(atoms - edge + HALO, atoms - 2 * edge, width),
         compiler_params=vmem(16),
         cost_estimate=cost(2.7),
     )(
-        place, window_offsets, level, coords, kicks, joined, atom_normed, mask, atom_qkv, atom_proj, out_row, coord_out
+        window_offsets.reshape(1, -1), level, coords, kicks, joined, atom_normed, mask, atom_qkv, atom_proj, out_row, coord_out
     )
     direction = pl.pallas_call(
         edge_kernel,
         out_shape=direction_like,
-        in_specs=[smem, smem] + whole(13),
+        in_specs=whole(1) + whole(13),
         out_specs=whole(1)[0],
         scratch_shapes=window_scratch(2 * (edge + 2 * HALO), 2 * edge, width),
         compiler_params=vmem(12),
         cost_estimate=cost(2),
     )(
-        place, window_offsets, level, coords, kicks, joined, low, atom_normed, high, mask, atom_qkv, atom_proj, out_row,
+        window_offsets.reshape(1, -1), level, coords, kicks, joined, low, atom_normed, high, mask, atom_qkv, atom_proj, out_row,
         coord_out, inner,
     )
     return (token_result, direction.transpose(1, 0, 2))

time: 54 us -> 50.5 us (0.935)
  the two profiles are of different devices: /device:TPU:0 before, /device:TPU:8 now
where the time goes in v4:
time: 50.5 us; the launch traced here: 50.3 us
  Pallas kernels  23.6 us (47%)
  starting transfers between devices  13.9 us (28%)
  waiting for transfers between devices  11 us (22%)
  between operations  1.71 us (3%)
    ppermute x6, waiting for transfers between devices, spread_over(): have[d | bit] = lax.ppermute(sent, axis, pairs)  9.95 us
    ppermute x6, starting transfers between devices, spread_over(): have[d | bit] = lax.ppermute(sent, axis, pairs)  6.03 us
    ppermute x2, starting transfers between devices, halos_of(): from_second = lax.ppermute(second_edge, 'row', second)  6.03 us
    pallas_call x1, Pallas kernels, per_device(): pl.pallas_call(functools.partial(pair_kernel, step_rows), out_shape=shape...  5.57 us
    pallas_call x1, Pallas kernels, per_device(): pl.pallas_call(functools.partial(token_kernel, near_count, row_count), ou...  4.5 us
    pallas_call x1, Pallas kernels, per_device(): pl.pallas_call(functools.partial(attend_first_kernel, near_count, row_cou...  3.78 us
    pallas_call x1, Pallas kernels, per_device(): pl.pallas_call(encoder_kernel, out_shape=(state_like, shape((tok_rows, to...  2.98 us
    pallas_call x1, Pallas kernels, per_device(): pl.pallas_call(prepare_kernel, out_shape=(state_like, normed_like, edge_l...  2.7 us
  transfers between devices with their start and end apart: 10, of which 4 were waited for; matrix products, arithmetic and copies ran while one was open for 0% of the time, Pallas kernels for 29%

profile of v4, /device:TPU:8, one launch (start us, length us, event | category | flops | bytes accessed | tf_op | source)
XLA Modules:
  0.0 50.3 jit_solution(11457556293604277520)
XLA Ops:
  1.3 2.7 %shard_map.257 = (f32[1024,128]{1,0:T(8,128)}, bf16[1024,128]{1,0:T(8,128)(2,1)}, bf16[96,128]{1,0:T(8,128)(2,1)}, bf16[96,128]{1,0:T(8,128)(2,1)}) custom-call(f32[1,1]{1,0:T(1,128)} %bitcast.11.level_hbm, f32[3,1,1024]{2,1,0:T(1,128)} %bitcast.20, f32[3,1,1024]{2,1,0:T(1,128)} %bitcast.23, bf16[1024,128]{1,0:T(8,128)(2,1)} %single_hbm.1, ...), custom_call_target="tpu_custom_call" | custom-call | flops 1500000000 | bytes 4500000 | tf_op jit(solution)/shard_map/pallas_call | solution.py:590
  4.0 3.5 %collective-permute-start.1 = (bf16[96,128]{1,0:T(8,128)(2,1)}, bf16[96,128]{1,0:T(8,128)(2,1)S(1)}, u32[]{:S(2)}, u32[]{:S(2)}) collective-permute-start(bf16[96,128]{1,0:T(8,128)(2,1)} %get-tuple-element.25), channel_id=1, source_target_pairs={{0,0},{3,3},{1,2},{2,1},{4,4},{7,7},{5,6},{6,5},{8,8},{11,11},{9,1... | collective-permute-start | bytes 73736 | tf_op jit(solution)/shard_map/ppermute | solution.py:528
  7.5 0.1 collective-permute-start
  7.6 0.0 copy-start.21
  7.6 0.0 copy-start.7
  7.6 0.0 copy-start.8
  7.6 0.0 copy-start.13
  7.7 0.0 copy-start.17
  7.7 5.6 %shard_map.259.refs_3_ = bf16[16,128,128]{2,1,0:T(8,128)(2,1)} custom-call(bf16[128,128,128]{2,1,0:T(8,128)(2,1)} %tile_hbm.1, f32[1,128]{1,0:T(1,128)} %bitcast.35, bf16[16,128]{1,0:T(8,128)(2,1)} %bitcast.34), custom_call_target="tpu_custom_call" | custom-call | flops 5000000000 | bytes 15000000 | tf_op jit(solution)/shard_map/pallas_call | solution.py:605
  13.3 1.6 %collective-permute-start.6 = (bf16[16,128,128]{2,1,0:T(8,128)(2,1)}, bf16[16,128,128]{2,1,0:T(8,128)(2,1)S(1)}, u32[]{:S(2)}, u32[]{:S(2)}) collective-permute-start(bf16[16,128,128]{2,1,0:T(8,128)(2,1)} %shard_map.259.refs_3_), channel_id=1, source_target_pairs={{0,8},{4,12},{8,0},{12,4},{1,9},{5,13},{9,1},{13,5},{2,10},{6,14},... | collective-permute-start | bytes 1572872 | tf_op jit(solution)/shard_map/ppermute | solution.py:542
  15.0 0.0 copy-start.14
  15.0 0.0 slice-start
  15.0 3.0 %shard_map.258 = (f32[1024,128]{1,0:T(8,128)S(1)}, f32[128,768]{1,0:T(8,128)S(1)}, bf16[128,768]{1,0:T(8,128)(2,1)S(1)}, bf16[128,1024]{1,0:T(8,128)(2,1)S(1)}) custom-call(s32[1,32]{1,0:T(1,128)S(1)} %bitcast.29, f32[1,1]{1,0:T(1,128)} %bitcast.12.level_ref, f32[1024,128]{1,0:T(8,128)S(1)} %copy-done.19, bf16[96,128]{1,0:T(8,128)(2,1)S(1)} %collective-permute-done.low_ref, ...), custom_call_target="tpu_custom_call" | custom-call | flops 3400000000 | bytes 10200000 | tf_op jit(solution)/shard_map/pallas_call | solution.py:621
  18.0 1.9 %collective-permute-start.2 = (bf16[128,768]{1,0:T(8,128)(2,1)S(1)}, bf16[128,768]{1,0:T(8,128)(2,1)S(1)}, u32[]{:S(2)}, u32[]{:S(2)}) collective-permute-start(bf16[128,768]{1,0:T(8,128)(2,1)S(1)} %get-tuple-element.26.refs_0_), channel_id=1, source_target_pairs={{0,2},{1,3},{2,0},{3,1},{4,6},{5,7},{6,4},{7,5},{8,10},{9,11},{10,... | collective-permute-start | bytes 589832 | tf_op jit(solution)/shard_map/ppermute | solution.py:542
  19.9 0.6 %collective-permute-start.4 = (bf16[128,768]{1,0:T(8,128)(2,1)S(1)}, bf16[128,768]{1,0:T(8,128)(2,1)S(1)}, u32[]{:S(2)}, u32[]{:S(2)}) collective-permute-start(bf16[128,768]{1,0:T(8,128)(2,1)S(1)} %get-tuple-element.26.refs_0_), channel_id=1, source_target_pairs={{0,1},{1,0},{2,3},{3,2},{4,5},{5,4},{6,7},{7,6},{8,9},{9,8},{10,11... | collective-permute-start | bytes 589832 | tf_op jit(solution)/shard_map/ppermute | solution.py:542
  20.4 7.0 %collective-permute-done.2.refs_2_ = bf16[128,768]{1,0:T(8,128)(2,1)S(1)} collective-permute-done((bf16[128,768]{1,0:T(8,128)(2,1)S(1)}, bf16[128,768]{1,0:T(8,128)(2,1)S(1)}, u32[]{:S(2)}, u32[]{:S(2)}) %collective-permute-start.2) | collective-permute-done | bytes 196640 | tf_op jit(solution)/shard_map/ppermute | solution.py:542
  27.4 1.4 %collective-permute-done.4.refs_1_ = bf16[128,768]{1,0:T(8,128)(2,1)S(1)} collective-permute-done((bf16[128,768]{1,0:T(8,128)(2,1)S(1)}, bf16[128,768]{1,0:T(8,128)(2,1)S(1)}, u32[]{:S(2)}, u32[]{:S(2)}) %collective-permute-start.4) | collective-permute-done | bytes 196640 | tf_op jit(solution)/shard_map/ppermute | solution.py:542
  28.8 2.0 %collective-permute-start.3 = (bf16[128,768]{1,0:T(8,128)(2,1)S(1)}, bf16[128,768]{1,0:T(8,128)(2,1)S(1)}, u32[]{:S(2)}, u32[]{:S(2)}) collective-permute-start(bf16[128,768]{1,0:T(8,128)(2,1)S(1)} %collective-permute-done.2.refs_2_), channel_id=1, source_target_pairs={{0,1},{1,0},{2,3},{3,2},{4,5},{5,4},{6,7},{7,6},{8,9},{9,8},{10,11... | collective-permute-start | bytes 589832 | tf_op jit(solution)/shard_map/ppermute | solution.py:542
  30.8 0.0 slice-start.1
  30.8 0.0 copy-start.1
  30.8 0.0 copy-start.2
  30.9 3.8 %shard_map.260 = (bf16[128,768]{1,0:T(8,128)(2,1)S(1)}, f32[128,768]{1,0:T(8,128)S(1)}, f32[16,128,128]{2,1,0:T(8,128)S(1)}, f32[16,128,128]{2,1,0:T(8,128)S(1)}, bf16[1,16,128,128]{3,2,1,0:T(8,128)(2,1)S(1)}) custom-call(bf16[128,768]{1,0:T(8,128)(2,1)S(1)} %get-tuple-element.26.refs_0_, bf16[128,768]{1,0:T(8,128)(2,1)S(1)} %collective-permute-done.4.refs_1_, ...), custom_call_target="tpu_custom_call" | custom-call | flops 4000000000 | bytes 12000000 | tf_op jit(solution)/shard_map/pallas_call | solution.py:650
  34.6 1.6 %collective-permute-done.3.refs_0_ = bf16[128,768]{1,0:T(8,128)(2,1)S(1)} collective-permute-done((bf16[128,768]{1,0:T(8,128)(2,1)S(1)}, bf16[128,768]{1,0:T(8,128)(2,1)S(1)}, u32[]{:S(2)}, u32[]{:S(2)}) %collective-permute-start.3) | collective-permute-done | bytes 196640 | tf_op jit(solution)/shard_map/ppermute | solution.py:542
  36.3 0.0 copy-start.10
  36.3 0.0 copy-start.11
  36.4 0.0 copy-start.18
  36.4 4.5 %shard_map.261 = (bf16[1,128,768]{2,1,0:T(8,128)(2,1)}, f32[1024,128]{1,0:T(8,128)S(1)}, bf16[1024,128]{1,0:T(8,128)(2,1)S(1)}, bf16[96,128]{1,0:T(8,128)(2,1)S(1)}, bf16[96,128]{1,0:T(8,128)(2,1)S(1)}) custom-call(bf16[128,768]{1,0:T(8,128)(2,1)S(1)} %collective-permute-done.3.refs_0_, bf16[128,768]{1,0:T(8,128)(2,1)S(1)} %get-tuple-element.29.refs_1_, ...), custom_call_target="tpu_custom_call" | custom-call | flops 6000000000 | bytes 18000000 | tf_op jit(solution)/shard_map/pallas_call | solution.py:670
  40.9 1.7 %collective-permute-start.8 = (bf16[96,128]{1,0:T(8,128)(2,1)S(1)}, bf16[96,128]{1,0:T(8,128)(2,1)S(1)}, u32[]{:S(2)}, u32[]{:S(2)}) collective-permute-start(bf16[96,128]{1,0:T(8,128)(2,1)S(1)} %get-tuple-element.39), channel_id=1, source_target_pairs={{0,1},{1,0},{2,3},{3,2},{4,5},{5,4},{6,7},{7,6},{8,9},{9,8},{10,11... | collective-permute-start | bytes 73736 | tf_op jit(solution)/shard_map/ppermute | solution.py:529
  42.6 2.5 %collective-permute-start.9 = (bf16[96,128]{1,0:T(8,128)(2,1)S(1)}, bf16[96,128]{1,0:T(8,128)(2,1)S(1)}, u32[]{:S(2)}, u32[]{:S(2)}) collective-permute-start(bf16[96,128]{1,0:T(8,128)(2,1)S(1)} %get-tuple-element.41), channel_id=1, source_target_pairs={{0,0},{3,3},{1,2},{2,1},{4,4},{7,7},{5,6},{6,5},{8,8},{11,11},{9,1... | collective-permute-start | bytes 73736 | tf_op jit(solution)/shard_map/ppermute | solution.py:528
  45.2 2.1 %shard_map.262.inner_ref = f32[3,1,1024]{2,1,0:T(1,128)S(1)} custom-call(s32[1,32]{1,0:T(1,128)S(1)} %bitcast.30, f32[1,1]{1,0:T(1,128)} %bitcast.13.level_ref, f32[3,1,1024]{2,1,0:T(1,128)S(1)} %bitcast.21, f32[3,1,1024]{2,1,0:T(1,128)S(1)} %bitcast.24, f32[1024,128]{1,0:T(8,128)S(1)} %get-tuple-element.38.state_ref, ...), custom_call_target="tpu_custom_call" | custom-call | flops 2700000000 | bytes 8100000 | tf_op jit(solution)/shard_map/pallas_call | solution.py:698
  47.3 1.0 %collective-permute-done.9.high_ref = bf16[96,128]{1,0:T(8,128)(2,1)S(1)} collective-permute-done((bf16[96,128]{1,0:T(8,128)(2,1)S(1)}, bf16[96,128]{1,0:T(8,128)(2,1)S(1)}, u32[]{:S(2)}, u32[]{:S(2)}) %collective-permute-start.9) | collective-permute-done | bytes 24608 | tf_op jit(solution)/shard_map/ppermute | solution.py:528
  48.3 1.9 %shard_map.263 = f32[3,1,1024]{2,1,0:T(1,128)} custom-call(s32[1,32]{1,0:T(1,128)S(1)} %bitcast.31, f32[1,1]{1,0:T(1,128)} %bitcast.14.level_ref, f32[3,1,1024]{2,1,0:T(1,128)S(1)} %bitcast.22, f32[3,1,1024]{2,1,0:T(1,128)S(1)} %bitcast.25, f32[1024,128]{1,0:T(8,128)S(1)} %get-tuple-element.38.state_ref, bf16[96,128]{1,0:T(8,128)(2,1)S(1)} %collective-permute-done.8.low_ref, ...), custom_call_target="tpu_custom_call" | custom-call | flops 2000000000 | bytes 6000000 | tf_op jit(solution)/shard_map/pallas_call | solution.py:709
  (45 shorter events, 0.1 us)
Async XLA Ops:
  4.0 10.8 %collective-permute-start.1 = (bf16[96,128]{1,0:T(8,128)(2,1)}, bf16[96,128]{1,0:T(8,128)(2,1)S(1)}, u32[]{:S(2)}, u32[]{:S(2)}) collective-permute-start(bf16[96,128]{1,0:T(8,128)(2,1)} %get-tuple-element.25), channel_id=1, source_target_pairs={{0,0},{3,3},{1,2},{2,1},{4,4},{7,7},{5,6},{6,5},{8,8},{11,11},{9,1... | collective-permute-start | bytes 73736 | tf_op jit(solution)/shard_map/ppermute | solution.py:528
  7.5 7.4 %collective-permute-start = (bf16[96,128]{1,0:T(8,128)(2,1)}, bf16[96,128]{1,0:T(8,128)(2,1)S(1)}, u32[]{:S(2)}, u32[]{:S(2)}) collective-permute-start(bf16[96,128]{1,0:T(8,128)(2,1)} %get-tuple-element.23), channel_id=1, source_target_pairs={{0,1},{1,0},{2,3},{3,2},{4,5},{5,4},{6,7},{7,6},{8,9},{9,8},{10,11... | collective-permute-start | bytes 73736 | tf_op jit(solution)/shard_map/ppermute | solution.py:529
  7.6 7.3 %copy-start.21 = (f32[768]{0:T(1024)S(1)}, f32[768]{0:T(1024)}, u32[]{:S(2)}) copy-start(f32[768]{0:T(1024)} %param.41) | copy-start | bytes 9220
  7.6 7.3 %copy-start.4 = (bf16[128,768]{1,0:T(8,128)(2,1)S(1)}, bf16[128,768]{1,0:T(8,128)(2,1)}, u32[]{:S(2)}) copy-start(bf16[128,768]{1,0:T(8,128)(2,1)} %lift_ref.1) | copy-start | bytes 589828
  7.6 7.3 %copy-start.5 = (bf16[128,768]{1,0:T(8,128)(2,1)S(1)}, bf16[128,768]{1,0:T(8,128)(2,1)}, u32[]{:S(2)}) copy-start(bf16[128,768]{1,0:T(8,128)(2,1)} %single_ref.1) | copy-start | bytes 589828
  7.6 7.3 %copy-start.7 = (bf16[2,128,384]{2,1,0:T(8,128)(2,1)S(1)}, bf16[2,128,384]{2,1,0:T(8,128)(2,1)}, u32[]{:S(2)}) copy-start(bf16[2,128,384]{2,1,0:T(8,128)(2,1)} %w_qkv_ref.5) | copy-start | bytes 589828
  7.6 7.3 %copy-start.8 = (bf16[2,128,128]{2,1,0:T(8,128)(2,1)S(1)}, bf16[2,128,128]{2,1,0:T(8,128)(2,1)}, u32[]{:S(2)}) copy-start(bf16[2,128,128]{2,1,0:T(8,128)(2,1)} %w_out_ref.5) | copy-start | bytes 196612
  7.6 7.3 %copy-start.9 = (s32[4096]{0:T(1024)S(1)}, s32[4096]{0:T(1024)}, u32[]{:S(2)}) copy-start(s32[4096]{0:T(1024)} %param.34) | copy-start | bytes 49156
  7.6 7.3 %copy-start.12 = (f32[2,768]{1,0:T(2,128)S(1)}, f32[2,768]{1,0:T(2,128)}, u32[]{:S(2)}) copy-start(f32[2,768]{1,0:T(2,128)} %refs_10_.1) | copy-start | bytes 18436
  7.6 7.3 %copy-start.13 = (s32[1024]{0:T(1024)S(1)}, s32[1024]{0:T(1024)}, u32[]{:S(2)}) copy-start(s32[1024]{0:T(1024)} %param.32) | copy-start | bytes 12292
  7.7 7.3 %copy-start.17 = (s32[32]{0:T(128)S(1)}, s32[32]{0:T(128)}, u32[]{:S(2)}) copy-start(s32[32]{0:T(128)} %param.33) | copy-start | bytes 388
  7.7 7.3 %copy-start.19 = (f32[1024,128]{1,0:T(8,128)S(1)}, f32[1024,128]{1,0:T(8,128)}, u32[]{:S(2)}) copy-start(f32[1024,128]{1,0:T(8,128)} %get-tuple-element.22.state_ref) | copy-start | bytes 1572868
  7.7 7.3 %copy-start.20 = (bf16[1024,128]{1,0:T(8,128)(2,1)S(1)}, bf16[1024,128]{1,0:T(8,128)(2,1)}, u32[]{:S(2)}) copy-start(bf16[1024,128]{1,0:T(8,128)(2,1)} %get-tuple-element.24.mid_ref) | copy-start | bytes 786436
  13.3 15.5 %collective-permute-start.6 = (bf16[16,128,128]{2,1,0:T(8,128)(2,1)}, bf16[16,128,128]{2,1,0:T(8,128)(2,1)S(1)}, u32[]{:S(2)}, u32[]{:S(2)}) collective-permute-start(bf16[16,128,128]{2,1,0:T(8,128)(2,1)} %shard_map.259.refs_3_), channel_id=1, source_target_pairs={{0,8},{4,12},{8,0},{12,4},{1,9},{5,13},{9,1},{13,5},{2,10},{6,14},... | collective-permute-start | bytes 1572872 | tf_op jit(solution)/shard_map/ppermute | solution.py:542
  14.9 5.5 %copy-start.3 = (bf16[16,128,128]{2,1,0:T(8,128)(2,1)S(1)}, bf16[16,128,128]{2,1,0:T(8,128)(2,1)}, u32[]{:S(2)}) copy-start(bf16[16,128,128]{2,1,0:T(8,128)(2,1)} %shard_map.259.refs_3_) | copy-start | bytes 1572868
  15.0 15.8 %copy-start = (bf16[768,2304]{1,0:T(8,128)(2,1)S(1)}, bf16[768,2304]{1,0:T(8,128)(2,1)}, u32[]{:S(2)}) copy-start(bf16[768,2304]{1,0:T(8,128)(2,1)} %refs_8_.3) | copy-start | bytes 10616836
  15.0 15.8 %copy-start.14 = (s32[512]{0:T(512)S(1)}, s32[512]{0:T(512)}, u32[]{:S(2)}) copy-start(s32[512]{0:T(512)} %param.35) | copy-start | bytes 6148
  15.0 21.3 %slice-start = ((s8[4718592]{0:T(1024)(128)(4,1)}), s8[4194304]{0:T(1024)(128)(4,1)S(1)}, s32[]{:S(2)}) async-start(s8[4718592]{0:T(1024)(128)(4,1)} %bitcast.15), calls=%async_computation | async-start | bytes 8388608
  18.0 9.4 %collective-permute-start.2 = (bf16[128,768]{1,0:T(8,128)(2,1)S(1)}, bf16[128,768]{1,0:T(8,128)(2,1)S(1)}, u32[]{:S(2)}, u32[]{:S(2)}) collective-permute-start(bf16[128,768]{1,0:T(8,128)(2,1)S(1)} %get-tuple-element.26.refs_0_), channel_id=1, source_target_pairs={{0,2},{1,3},{2,0},{3,1},{4,6},{5,7},{6,4},{7,5},{8,10},{9,11},{10,... | collective-permute-start | bytes 589832 | tf_op jit(solution)/shard_map/ppermute | solution.py:542
  19.9 8.9 %collective-permute-start.4 = (bf16[128,768]{1,0:T(8,128)(2,1)S(1)}, bf16[128,768]{1,0:T(8,128)(2,1)S(1)}, u32[]{:S(2)}, u32[]{:S(2)}) collective-permute-start(bf16[128,768]{1,0:T(8,128)(2,1)S(1)} %get-tuple-element.26.refs_0_), channel_id=1, source_target_pairs={{0,1},{1,0},{2,3},{3,2},{4,5},{5,4},{6,7},{7,6},{8,9},{9,8},{10,11... | collective-permute-start | bytes 589832 | tf_op jit(solution)/shard_map/ppermute | solution.py:542
  20.4 10.3 %collective-permute-start.5 = (bf16[16,128,128]{2,1,0:T(8,128)(2,1)S(1)}, bf16[16,128,128]{2,1,0:T(8,128)(2,1)S(1)}, u32[]{:S(2)}, u32[]{:S(2)}) collective-permute-start(bf16[16,128,128]{2,1,0:T(8,128)(2,1)S(1)} %copy-done.3), channel_id=1, source_target_pairs={{0,4},{4,0},{8,12},{12,8},{1,5},{5,1},{9,13},{13,9},{2,6},{6,2},{1... | collective-permute-start | bytes 1572872 | tf_op jit(solution)/shard_map/ppermute | solution.py:542
  28.7 2.0 %collective-permute-start.7 = (bf16[16,128,128]{2,1,0:T(8,128)(2,1)S(1)}, bf16[16,128,128]{2,1,0:T(8,128)(2,1)S(1)}, u32[]{:S(2)}, u32[]{:S(2)}) collective-permute-start(bf16[16,128,128]{2,1,0:T(8,128)(2,1)S(1)} %collective-permute-done.6.refs_5_), channel_id=1, source_target_pairs={{0,4},{4,0},{8,12},{12,8},{1,5},{5,1},{9,13},{13,9},{2,6},{6,2},{1... | collective-permute-start | bytes 1572872 | tf_op jit(solution)/shard_map/ppermute | solution.py:542
  28.8 7.5 %collective-permute-start.3 = (bf16[128,768]{1,0:T(8,128)(2,1)S(1)}, bf16[128,768]{1,0:T(8,128)(2,1)S(1)}, u32[]{:S(2)}, u32[]{:S(2)}) collective-permute-start(bf16[128,768]{1,0:T(8,128)(2,1)S(1)} %collective-permute-done.2.refs_2_), channel_id=1, source_target_pairs={{0,1},{1,0},{2,3},{3,2},{4,5},{5,4},{6,7},{7,6},{8,9},{9,8},{10,11... | collective-permute-start | bytes 589832 | tf_op jit(solution)/shard_map/ppermute | solution.py:542
  30.8 5.5 %slice-start.1 = ((s8[4718592]{0:T(1024)(128)(4,1)}), s8[524288]{0:T(1024)(128)(4,1)S(1)}, s32[]{:S(2)}) async-start(s8[4718592]{0:T(1024)(128)(4,1)} %bitcast.15), calls=%async_computation.1 | async-start | bytes 1048576
  30.8 5.5 %copy-start.1 = (bf16[1536,768]{1,0:T(8,128)(2,1)S(1)}, bf16[1536,768]{1,0:T(8,128)(2,1)}, u32[]{:S(2)}) copy-start(bf16[1536,768]{1,0:T(8,128)(2,1)} %refs_12_.1) | copy-start | bytes 7077892
  30.8 5.5 %copy-start.2 = (bf16[768,768]{1,0:T(8,128)(2,1)S(1)}, bf16[768,768]{1,0:T(8,128)(2,1)}, u32[]{:S(2)}) copy-start(bf16[768,768]{1,0:T(8,128)(2,1)} %refs_9_.1) | copy-start | bytes 3538948
  36.3 8.8 %copy-start.10 = (f32[1,3,1024]{2,0,1:T(1,128)S(1)}, f32[1,3,1024]{2,0,1:T(1,128)}, u32[]{:S(2)}) copy-start(f32[1,3,1024]{2,0,1:T(1,128)} %param.26) | copy-start | bytes 36868
  36.3 8.8 %copy-start.11 = (f32[1,3,1024]{2,0,1:T(1,128)S(1)}, f32[1,3,1024]{2,0,1:T(1,128)}, u32[]{:S(2)}) copy-start(f32[1,3,1024]{2,0,1:T(1,128)} %param.27) | copy-start | bytes 36868
  36.4 8.8 %copy-start.16 = (bf16[3,128]{1,0:T(4,128)(2,1)S(1)}, bf16[3,128]{1,0:T(4,128)(2,1)}, u32[]{:S(2)}) copy-start(bf16[3,128]{1,0:T(4,128)(2,1)} %coord_out_ref.3) | copy-start | bytes 2308
  36.4 8.8 %copy-start.18 = (f32[128]{0:T(128)S(1)}, f32[128]{0:T(128)}, u32[]{:S(2)}) copy-start(f32[128]{0:T(128)} %param.50) | copy-start | bytes 1540
  40.9 6.4 %collective-permute-start.8 = (bf16[96,128]{1,0:T(8,128)(2,1)S(1)}, bf16[96,128]{1,0:T(8,128)(2,1)S(1)}, u32[]{:S(2)}, u32[]{:S(2)}) collective-permute-start(bf16[96,128]{1,0:T(8,128)(2,1)S(1)} %get-tuple-element.39), channel_id=1, source_target_pairs={{0,1},{1,0},{2,3},{3,2},{4,5},{5,4},{6,7},{7,6},{8,9},{9,8},{10,11... | collective-permute-start | bytes 73736 | tf_op jit(solution)/shard_map/ppermute | solution.py:529
  42.6 5.7 %collective-permute-start.9 = (bf16[96,128]{1,0:T(8,128)(2,1)S(1)}, bf16[96,128]{1,0:T(8,128)(2,1)S(1)}, u32[]{:S(2)}, u32[]{:S(2)}) collective-permute-start(bf16[96,128]{1,0:T(8,128)(2,1)S(1)} %get-tuple-element.41), channel_id=1, source_target_pairs={{0,0},{3,3},{1,2},{2,1},{4,4},{7,7},{5,6},{6,5},{8,8},{11,11},{9,1... | collective-permute-start | bytes 73736 | tf_op jit(solution)/shard_map/ppermute | solution.py:528
  (2 other events, 10.9 us)

commit v5 on v4

--- a/solution.py
+++ b/solution.py
@@ -117,12 +117,13 @@
     write_edges(normed, lax.axis_index("row"), first_edge_ref, second_edge_ref)
 
 
-def pair_kernel(step_rows, tile_hbm, gain_hbm, heads_hbm, bias_ref, tile_ref, gain_ref, heads_ref, tile_sems, sems):
+def pair_kernel(
+    steps, tile_hbm, gain_hbm, heads_hbm, bias_hbm, tile_ref, gain_ref, heads_ref, bias_ref, tile_sems, bias_sems, sems
+):
     keys, channels = tile_ref.shape[1:]
     head_count = heads_ref.shape[0]
-    steps = tile_ref.shape[0] // step_rows
     small = fetch([gain_hbm, heads_hbm], [gain_ref, heads_ref], sems)
-    spans = [pl.ds(step * step_rows, step_rows) for step in range(steps)]
+    spans = [pl.ds(begin, step_rows) for begin, step_rows in steps]
     tiles = fetch([tile_hbm.at[span] for span in spans], [tile_ref.at[span] for span in spans], tile_sems)
     for copy in small:
         copy.wait()
@@ -131,9 +132,9 @@
     low = (weights - high.astype(F32)).astype(BF16)
     total = jnp.sum(high.astype(F32) + low.astype(F32), axis=1, keepdims=True)
     left = jnp.concatenate([high, low], axis=0)
-    for step in range(steps):
+    sent = []
+    for step, (begin, step_rows) in enumerate(steps):
         tiles[step].wait()
-        begin = step * step_rows
         tile = tile_ref[begin : begin + step_rows].reshape(step_rows * keys, channels).T
         wide = tile.astype(F32)
         average = jnp.mean(wide, axis=0, keepdims=True)
@@ -144,6 +145,13 @@
         result = (raw - average * total) * lax.rsqrt(variance + norm_eps)
         pieces = [result[:, i * keys : (i + 1) * keys] for i in range(step_rows)]
         bias_ref[:, begin : begin + step_rows, :] = jnp.swapaxes(jnp.stack(pieces, axis=0), 0, 1).astype(BF16)
+        copy = pltpu.make_async_copy(
+            bias_ref.at[:, spans[step], :], bias_hbm.at[:, spans[step], :], bias_sems.at[step]
+        )
+        copy.start()
+        sent.append(copy)
+    for copy in sent:
+        copy.wait()
 
 
 def live_bias(mask_ref, chunk, outside):
@@ -601,17 +609,21 @@
 
     pair_rows, _, channels = pair_cond.shape
     step_rows = 32
+    half = pair_rows // 2
+    steps = [(0, step_rows), (step_rows, half - step_rows), (half, pair_rows - half)]
     gain_row, _ = lax.optimization_barrier((pair_gain, second_edge))
     bias = pl.pallas_call(
-        functools.partial(pair_kernel, step_rows),
+        functools.partial(pair_kernel, steps),
         out_shape=shape((heads, pair_rows, keys), BF16),
         in_specs=hbm(3),
-        out_specs=whole(1)[0],
+        out_specs=hbm(1)[0],
         scratch_shapes=[
             pltpu.VMEM(pair_cond.shape, BF16),
             pltpu.VMEM((1, channels), F32),
             pltpu.VMEM((heads, channels), BF16),
-            pltpu.SemaphoreType.DMA((pair_rows // step_rows,)),
+            pltpu.VMEM((heads, pair_rows, keys), BF16),
+            pltpu.SemaphoreType.DMA((len(steps),)),
+            pltpu.SemaphoreType.DMA((len(steps),)),
             pltpu.SemaphoreType.DMA((2,)),
         ],
         compiler_params=vmem(PRIVATE),

time: 50.5 us -> 50 us (0.990)
  the two profiles are of different devices: /device:TPU:8 before, /device:TPU:12 now
where the time goes in v5:
time: 50 us; the launch traced here: 49.7 us
  Pallas kernels  23 us (46%)
  starting transfers between devices  13.9 us (28%)
  waiting for transfers between devices  11 us (22%)
  between operations  1.71 us (3%)
    ppermute x6, waiting for transfers between devices, spread_over(): have[d | bit] = lax.ppermute(sent, axis, pairs)  9.96 us
    ppermute x2, starting transfers between devices, halos_of(): from_second = lax.ppermute(second_edge, 'row', second)  6.06 us
    ppermute x6, starting transfers between devices, spread_over(): have[d | bit] = lax.ppermute(sent, axis, pairs)  6.03 us
    pallas_call x1, Pallas kernels, per_device(): pl.pallas_call(functools.partial(pair_kernel, steps), out_shape=shape((he...  5.01 us
    pallas_call x1, Pallas kernels, per_device(): pl.pallas_call(functools.partial(token_kernel, near_count, row_count), ou...  4.53 us
    pallas_call x1, Pallas kernels, per_device(): pl.pallas_call(functools.partial(attend_first_kernel, near_count, row_cou...  3.77 us
    pallas_call x1, Pallas kernels, per_device(): pl.pallas_call(encoder_kernel, out_shape=(state_like, shape((tok_rows, to...  2.95 us
    pallas_call x1, Pallas kernels, per_device(): pl.pallas_call(prepare_kernel, out_shape=(state_like, normed_like, edge_l...  2.7 us
  transfers between devices with their start and end apart: 10, of which 4 were waited for; matrix products, arithmetic and copies ran while one was open for 0% of the time, Pallas kernels for 28%

profile of v5, /device:TPU:12, one launch (start us, length us, event | category | flops | bytes accessed | tf_op | source)
XLA Modules:
  0.0 49.7 jit_solution(607611822031926616)
XLA Ops:
  1.3 2.7 %shard_map.257 = (f32[1024,128]{1,0:T(8,128)}, bf16[1024,128]{1,0:T(8,128)(2,1)}, bf16[96,128]{1,0:T(8,128)(2,1)}, bf16[96,128]{1,0:T(8,128)(2,1)}) custom-call(f32[1,1]{1,0:T(1,128)} %bitcast.11.level_hbm, f32[3,1,1024]{2,1,0:T(1,128)} %bitcast.20, f32[3,1,1024]{2,1,0:T(1,128)} %bitcast.23, bf16[1024,128]{1,0:T(8,128)(2,1)} %single_hbm.1, ...), custom_call_target="tpu_custom_call" | custom-call | flops 1500000000 | bytes 4500000 | tf_op jit(solution)/shard_map/pallas_call | solution.py:598
  4.0 3.5 %collective-permute-start.1 = (bf16[96,128]{1,0:T(8,128)(2,1)}, bf16[96,128]{1,0:T(8,128)(2,1)S(1)}, u32[]{:S(2)}, u32[]{:S(2)}) collective-permute-start(bf16[96,128]{1,0:T(8,128)(2,1)} %get-tuple-element.25), channel_id=1, source_target_pairs={{0,0},{3,3},{1,2},{2,1},{4,4},{7,7},{5,6},{6,5},{8,8},{11,11},{9,1... | collective-permute-start | bytes 73736 | tf_op jit(solution)/shard_map/ppermute | solution.py:536
  7.5 0.1 collective-permute-start
  7.6 0.0 copy-start.21
  7.6 0.0 copy-start.4
  7.6 0.0 copy-start.7
  7.6 0.0 copy-start.8
  7.6 0.0 copy-start.13
  7.7 0.0 copy-start.17
  7.7 5.0 %shard_map.259.refs_3_ = bf16[16,128,128]{2,1,0:T(8,128)(2,1)} custom-call(bf16[128,128,128]{2,1,0:T(8,128)(2,1)} %tile_hbm.1, f32[1,128]{1,0:T(1,128)} %bitcast.35, bf16[16,128]{1,0:T(8,128)(2,1)} %bitcast.34), custom_call_target="tpu_custom_call" | custom-call | flops 5000000000 | bytes 15000000 | tf_op jit(solution)/shard_map/pallas_call | solution.py:615
  12.7 1.6 %collective-permute-start.6 = (bf16[16,128,128]{2,1,0:T(8,128)(2,1)}, bf16[16,128,128]{2,1,0:T(8,128)(2,1)S(1)}, u32[]{:S(2)}, u32[]{:S(2)}) collective-permute-start(bf16[16,128,128]{2,1,0:T(8,128)(2,1)} %shard_map.259.refs_3_), channel_id=1, source_target_pairs={{0,8},{4,12},{8,0},{12,4},{1,9},{5,13},{9,1},{13,5},{2,10},{6,14},... | collective-permute-start | bytes 1572872 | tf_op jit(solution)/shard_map/ppermute | solution.py:550
  14.4 0.0 copy-start.14
  14.4 0.0 slice-start
  14.4 3.0 %shard_map.258 = (f32[1024,128]{1,0:T(8,128)S(1)}, f32[128,768]{1,0:T(8,128)S(1)}, bf16[128,768]{1,0:T(8,128)(2,1)S(1)}, bf16[128,1024]{1,0:T(8,128)(2,1)S(1)}) custom-call(s32[1,32]{1,0:T(1,128)S(1)} %bitcast.29, f32[1,1]{1,0:T(1,128)} %bitcast.12.level_ref, f32[1024,128]{1,0:T(8,128)S(1)} %copy-done.19, bf16[96,128]{1,0:T(8,128)(2,1)S(1)} %collective-permute-done.low_ref, ...), custom_call_target="tpu_custom_call" | custom-call | flops 3400000000 | bytes 10200000 | tf_op jit(solution)/shard_map/pallas_call | solution.py:633
  17.4 1.9 %collective-permute-start.2 = (bf16[128,768]{1,0:T(8,128)(2,1)S(1)}, bf16[128,768]{1,0:T(8,128)(2,1)S(1)}, u32[]{:S(2)}, u32[]{:S(2)}) collective-permute-start(bf16[128,768]{1,0:T(8,128)(2,1)S(1)} %get-tuple-element.26.refs_0_), channel_id=1, source_target_pairs={{0,2},{1,3},{2,0},{3,1},{4,6},{5,7},{6,4},{7,5},{8,10},{9,11},{10,... | collective-permute-start | bytes 589832 | tf_op jit(solution)/shard_map/ppermute | solution.py:550
  19.3 0.5 %collective-permute-start.4 = (bf16[128,768]{1,0:T(8,128)(2,1)S(1)}, bf16[128,768]{1,0:T(8,128)(2,1)S(1)}, u32[]{:S(2)}, u32[]{:S(2)}) collective-permute-start(bf16[128,768]{1,0:T(8,128)(2,1)S(1)} %get-tuple-element.26.refs_0_), channel_id=1, source_target_pairs={{0,1},{1,0},{2,3},{3,2},{4,5},{5,4},{6,7},{7,6},{8,9},{9,8},{10,11... | collective-permute-start | bytes 589832 | tf_op jit(solution)/shard_map/ppermute | solution.py:550
  19.8 7.0 %collective-permute-done.2.refs_2_ = bf16[128,768]{1,0:T(8,128)(2,1)S(1)} collective-permute-done((bf16[128,768]{1,0:T(8,128)(2,1)S(1)}, bf16[128,768]{1,0:T(8,128)(2,1)S(1)}, u32[]{:S(2)}, u32[]{:S(2)}) %collective-permute-start.2) | collective-permute-done | bytes 196640 | tf_op jit(solution)/shard_map/ppermute | solution.py:550
  26.8 1.3 %collective-permute-done.4.refs_1_ = bf16[128,768]{1,0:T(8,128)(2,1)S(1)} collective-permute-done((bf16[128,768]{1,0:T(8,128)(2,1)S(1)}, bf16[128,768]{1,0:T(8,128)(2,1)S(1)}, u32[]{:S(2)}, u32[]{:S(2)}) %collective-permute-start.4) | collective-permute-done | bytes 196640 | tf_op jit(solution)/shard_map/ppermute | solution.py:550
  28.2 2.0 %collective-permute-start.3 = (bf16[128,768]{1,0:T(8,128)(2,1)S(1)}, bf16[128,768]{1,0:T(8,128)(2,1)S(1)}, u32[]{:S(2)}, u32[]{:S(2)}) collective-permute-start(bf16[128,768]{1,0:T(8,128)(2,1)S(1)} %collective-permute-done.2.refs_2_), channel_id=1, source_target_pairs={{0,1},{1,0},{2,3},{3,2},{4,5},{5,4},{6,7},{7,6},{8,9},{9,8},{10,11... | collective-permute-start | bytes 589832 | tf_op jit(solution)/shard_map/ppermute | solution.py:550
  30.2 0.0 slice-start.1
  30.2 0.0 copy-start.2
  30.3 0.0 copy-start.6
  30.3 3.8 %shard_map.260 = (bf16[128,768]{1,0:T(8,128)(2,1)S(1)}, f32[128,768]{1,0:T(8,128)S(1)}, f32[16,128,128]{2,1,0:T(8,128)S(1)}, f32[16,128,128]{2,1,0:T(8,128)S(1)}, bf16[1,16,128,128]{3,2,1,0:T(8,128)(2,1)S(1)}) custom-call(bf16[128,768]{1,0:T(8,128)(2,1)S(1)} %get-tuple-element.26.refs_0_, bf16[128,768]{1,0:T(8,128)(2,1)S(1)} %collective-permute-done.4.refs_1_, ...), custom_call_target="tpu_custom_call" | custom-call | flops 4000000000 | bytes 12000000 | tf_op jit(solution)/shard_map/pallas_call | solution.py:662
  34.1 1.6 %collective-permute-done.3.refs_0_ = bf16[128,768]{1,0:T(8,128)(2,1)S(1)} collective-permute-done((bf16[128,768]{1,0:T(8,128)(2,1)S(1)}, bf16[128,768]{1,0:T(8,128)(2,1)S(1)}, u32[]{:S(2)}, u32[]{:S(2)}) %collective-permute-start.3) | collective-permute-done | bytes 196640 | tf_op jit(solution)/shard_map/ppermute | solution.py:550
  35.7 0.0 copy-start.10
  35.8 0.0 copy-start.11
  35.8 4.5 %shard_map.261 = (bf16[1,128,768]{2,1,0:T(8,128)(2,1)}, f32[1024,128]{1,0:T(8,128)S(1)}, bf16[1024,128]{1,0:T(8,128)(2,1)S(1)}, bf16[96,128]{1,0:T(8,128)(2,1)S(1)}, bf16[96,128]{1,0:T(8,128)(2,1)S(1)}) custom-call(bf16[128,768]{1,0:T(8,128)(2,1)S(1)} %collective-permute-done.3.refs_0_, bf16[128,768]{1,0:T(8,128)(2,1)S(1)} %get-tuple-element.29.refs_1_, ...), custom_call_target="tpu_custom_call" | custom-call | flops 6000000000 | bytes 18000000 | tf_op jit(solution)/shard_map/pallas_call | solution.py:682
  40.3 1.7 %collective-permute-start.8 = (bf16[96,128]{1,0:T(8,128)(2,1)S(1)}, bf16[96,128]{1,0:T(8,128)(2,1)S(1)}, u32[]{:S(2)}, u32[]{:S(2)}) collective-permute-start(bf16[96,128]{1,0:T(8,128)(2,1)S(1)} %get-tuple-element.39), channel_id=1, source_target_pairs={{0,1},{1,0},{2,3},{3,2},{4,5},{5,4},{6,7},{7,6},{8,9},{9,8},{10,11... | collective-permute-start | bytes 73736 | tf_op jit(solution)/shard_map/ppermute | solution.py:537
  42.1 2.6 %collective-permute-start.9 = (bf16[96,128]{1,0:T(8,128)(2,1)S(1)}, bf16[96,128]{1,0:T(8,128)(2,1)S(1)}, u32[]{:S(2)}, u32[]{:S(2)}) collective-permute-start(bf16[96,128]{1,0:T(8,128)(2,1)S(1)} %get-tuple-element.41), channel_id=1, source_target_pairs={{0,0},{3,3},{1,2},{2,1},{4,4},{7,7},{5,6},{6,5},{8,8},{11,11},{9,1... | collective-permute-start | bytes 73736 | tf_op jit(solution)/shard_map/ppermute | solution.py:536
  44.7 2.1 %shard_map.262.inner_ref = f32[3,1,1024]{2,1,0:T(1,128)S(1)} custom-call(s32[1,32]{1,0:T(1,128)S(1)} %bitcast.30, f32[1,1]{1,0:T(1,128)} %bitcast.13.level_ref, f32[3,1,1024]{2,1,0:T(1,128)S(1)} %bitcast.21, f32[3,1,1024]{2,1,0:T(1,128)S(1)} %bitcast.24, f32[1024,128]{1,0:T(8,128)S(1)} %get-tuple-element.38.state_ref, ...), custom_call_target="tpu_custom_call" | custom-call | flops 2700000000 | bytes 8100000 | tf_op jit(solution)/shard_map/pallas_call | solution.py:710
  46.8 1.0 %collective-permute-done.9.high_ref = bf16[96,128]{1,0:T(8,128)(2,1)S(1)} collective-permute-done((bf16[96,128]{1,0:T(8,128)(2,1)S(1)}, bf16[96,128]{1,0:T(8,128)(2,1)S(1)}, u32[]{:S(2)}, u32[]{:S(2)}) %collective-permute-start.9) | collective-permute-done | bytes 24608 | tf_op jit(solution)/shard_map/ppermute | solution.py:536
  47.8 1.9 %shard_map.263 = f32[3,1,1024]{2,1,0:T(1,128)} custom-call(s32[1,32]{1,0:T(1,128)S(1)} %bitcast.31, f32[1,1]{1,0:T(1,128)} %bitcast.14.level_ref, f32[3,1,1024]{2,1,0:T(1,128)S(1)} %bitcast.22, f32[3,1,1024]{2,1,0:T(1,128)S(1)} %bitcast.25, f32[1024,128]{1,0:T(8,128)S(1)} %get-tuple-element.38.state_ref, bf16[96,128]{1,0:T(8,128)(2,1)S(1)} %collective-permute-done.8.low_ref, ...), custom_call_target="tpu_custom_call" | custom-call | flops 2000000000 | bytes 6000000 | tf_op jit(solution)/shard_map/pallas_call | solution.py:721
  (45 shorter events, 0.1 us)
Async XLA Ops:
  4.0 10.3 %collective-permute-start.1 = (bf16[96,128]{1,0:T(8,128)(2,1)}, bf16[96,128]{1,0:T(8,128)(2,1)S(1)}, u32[]{:S(2)}, u32[]{:S(2)}) collective-permute-start(bf16[96,128]{1,0:T(8,128)(2,1)} %get-tuple-element.25), channel_id=1, source_target_pairs={{0,0},{3,3},{1,2},{2,1},{4,4},{7,7},{5,6},{6,5},{8,8},{11,11},{9,1... | collective-permute-start | bytes 73736 | tf_op jit(solution)/shard_map/ppermute | solution.py:536
  7.5 6.8 %collective-permute-start = (bf16[96,128]{1,0:T(8,128)(2,1)}, bf16[96,128]{1,0:T(8,128)(2,1)S(1)}, u32[]{:S(2)}, u32[]{:S(2)}) collective-permute-start(bf16[96,128]{1,0:T(8,128)(2,1)} %get-tuple-element.23), channel_id=1, source_target_pairs={{0,1},{1,0},{2,3},{3,2},{4,5},{5,4},{6,7},{7,6},{8,9},{9,8},{10,11... | collective-permute-start | bytes 73736 | tf_op jit(solution)/shard_map/ppermute | solution.py:537
  7.6 6.7 %copy-start.21 = (f32[768]{0:T(1024)S(1)}, f32[768]{0:T(1024)}, u32[]{:S(2)}) copy-start(f32[768]{0:T(1024)} %param.41) | copy-start | bytes 9220
  7.6 6.7 %copy-start.4 = (bf16[128,768]{1,0:T(8,128)(2,1)S(1)}, bf16[128,768]{1,0:T(8,128)(2,1)}, u32[]{:S(2)}) copy-start(bf16[128,768]{1,0:T(8,128)(2,1)} %lift_ref.1) | copy-start | bytes 589828
  7.6 6.7 %copy-start.5 = (bf16[128,768]{1,0:T(8,128)(2,1)S(1)}, bf16[128,768]{1,0:T(8,128)(2,1)}, u32[]{:S(2)}) copy-start(bf16[128,768]{1,0:T(8,128)(2,1)} %single_ref.1) | copy-start | bytes 589828
  7.6 6.7 %copy-start.7 = (bf16[2,128,384]{2,1,0:T(8,128)(2,1)S(1)}, bf16[2,128,384]{2,1,0:T(8,128)(2,1)}, u32[]{:S(2)}) copy-start(bf16[2,128,384]{2,1,0:T(8,128)(2,1)} %w_qkv_ref.5) | copy-start | bytes 589828
  7.6 6.7 %copy-start.8 = (bf16[2,128,128]{2,1,0:T(8,128)(2,1)S(1)}, bf16[2,128,128]{2,1,0:T(8,128)(2,1)}, u32[]{:S(2)}) copy-start(bf16[2,128,128]{2,1,0:T(8,128)(2,1)} %w_out_ref.5) | copy-start | bytes 196612
  7.6 6.7 %copy-start.9 = (s32[4096]{0:T(1024)S(1)}, s32[4096]{0:T(1024)}, u32[]{:S(2)}) copy-start(s32[4096]{0:T(1024)} %param.34) | copy-start | bytes 49156
  7.6 6.7 %copy-start.12 = (f32[2,768]{1,0:T(2,128)S(1)}, f32[2,768]{1,0:T(2,128)}, u32[]{:S(2)}) copy-start(f32[2,768]{1,0:T(2,128)} %refs_10_.1) | copy-start | bytes 18436
  7.6 6.7 %copy-start.13 = (s32[1024]{0:T(1024)S(1)}, s32[1024]{0:T(1024)}, u32[]{:S(2)}) copy-start(s32[1024]{0:T(1024)} %param.32) | copy-start | bytes 12292
  7.7 6.7 %copy-start.17 = (s32[32]{0:T(128)S(1)}, s32[32]{0:T(128)}, u32[]{:S(2)}) copy-start(s32[32]{0:T(128)} %param.33) | copy-start | bytes 388
  7.7 6.7 %copy-start.19 = (f32[1024,128]{1,0:T(8,128)S(1)}, f32[1024,128]{1,0:T(8,128)}, u32[]{:S(2)}) copy-start(f32[1024,128]{1,0:T(8,128)} %get-tuple-element.22.state_ref) | copy-start | bytes 1572868
  7.7 6.7 %copy-start.20 = (bf16[1024,128]{1,0:T(8,128)(2,1)S(1)}, bf16[1024,128]{1,0:T(8,128)(2,1)}, u32[]{:S(2)}) copy-start(bf16[1024,128]{1,0:T(8,128)(2,1)} %get-tuple-element.24.mid_ref) | copy-start | bytes 786436
  12.7 15.5 %collective-permute-start.6 = (bf16[16,128,128]{2,1,0:T(8,128)(2,1)}, bf16[16,128,128]{2,1,0:T(8,128)(2,1)S(1)}, u32[]{:S(2)}, u32[]{:S(2)}) collective-permute-start(bf16[16,128,128]{2,1,0:T(8,128)(2,1)} %shard_map.259.refs_3_), channel_id=1, source_target_pairs={{0,8},{4,12},{8,0},{12,4},{1,9},{5,13},{9,1},{13,5},{2,10},{6,14},... | collective-permute-start | bytes 1572872 | tf_op jit(solution)/shard_map/ppermute | solution.py:550
  14.4 15.8 %copy-start = (bf16[768,2304]{1,0:T(8,128)(2,1)S(1)}, bf16[768,2304]{1,0:T(8,128)(2,1)}, u32[]{:S(2)}) copy-start(bf16[768,2304]{1,0:T(8,128)(2,1)} %refs_8_.3) | copy-start | bytes 10616836
  14.4 15.8 %copy-start.14 = (s32[512]{0:T(512)S(1)}, s32[512]{0:T(512)}, u32[]{:S(2)}) copy-start(s32[512]{0:T(512)} %param.35) | copy-start | bytes 6148
  14.4 21.3 %slice-start = ((s8[4718592]{0:T(1024)(128)(4,1)}), s8[4194304]{0:T(1024)(128)(4,1)S(1)}, s32[]{:S(2)}) async-start(s8[4718592]{0:T(1024)(128)(4,1)} %bitcast.15), calls=%async_computation | async-start | bytes 8388608
  17.4 9.5 %collective-permute-start.2 = (bf16[128,768]{1,0:T(8,128)(2,1)S(1)}, bf16[128,768]{1,0:T(8,128)(2,1)S(1)}, u32[]{:S(2)}, u32[]{:S(2)}) collective-permute-start(bf16[128,768]{1,0:T(8,128)(2,1)S(1)} %get-tuple-element.26.refs_0_), channel_id=1, source_target_pairs={{0,2},{1,3},{2,0},{3,1},{4,6},{5,7},{6,4},{7,5},{8,10},{9,11},{10,... | collective-permute-start | bytes 589832 | tf_op jit(solution)/shard_map/ppermute | solution.py:550
  19.3 8.8 %collective-permute-start.4 = (bf16[128,768]{1,0:T(8,128)(2,1)S(1)}, bf16[128,768]{1,0:T(8,128)(2,1)S(1)}, u32[]{:S(2)}, u32[]{:S(2)}) collective-permute-start(bf16[128,768]{1,0:T(8,128)(2,1)S(1)} %get-tuple-element.26.refs_0_), channel_id=1, source_target_pairs={{0,1},{1,0},{2,3},{3,2},{4,5},{5,4},{6,7},{7,6},{8,9},{9,8},{10,11... | collective-permute-start | bytes 589832 | tf_op jit(solution)/shard_map/ppermute | solution.py:550
  19.8 10.4 %collective-permute-start.5 = (bf16[16,128,128]{2,1,0:T(8,128)(2,1)S(1)}, bf16[16,128,128]{2,1,0:T(8,128)(2,1)S(1)}, u32[]{:S(2)}, u32[]{:S(2)}) collective-permute-start(bf16[16,128,128]{2,1,0:T(8,128)(2,1)S(1)} %copy-done.3), channel_id=1, source_target_pairs={{0,4},{4,0},{8,12},{12,8},{1,5},{5,1},{9,13},{13,9},{2,6},{6,2},{1... | collective-permute-start | bytes 1572872 | tf_op jit(solution)/shard_map/ppermute | solution.py:550
  28.2 2.0 %collective-permute-start.7 = (bf16[16,128,128]{2,1,0:T(8,128)(2,1)S(1)}, bf16[16,128,128]{2,1,0:T(8,128)(2,1)S(1)}, u32[]{:S(2)}, u32[]{:S(2)}) collective-permute-start(bf16[16,128,128]{2,1,0:T(8,128)(2,1)S(1)} %collective-permute-done.6.refs_5_), channel_id=1, source_target_pairs={{0,4},{4,0},{8,12},{12,8},{1,5},{5,1},{9,13},{13,9},{2,6},{6,2},{1... | collective-permute-start | bytes 1572872 | tf_op jit(solution)/shard_map/ppermute | solution.py:550
  28.2 7.5 %collective-permute-start.3 = (bf16[128,768]{1,0:T(8,128)(2,1)S(1)}, bf16[128,768]{1,0:T(8,128)(2,1)S(1)}, u32[]{:S(2)}, u32[]{:S(2)}) collective-permute-start(bf16[128,768]{1,0:T(8,128)(2,1)S(1)} %collective-permute-done.2.refs_2_), channel_id=1, source_target_pairs={{0,1},{1,0},{2,3},{3,2},{4,5},{5,4},{6,7},{7,6},{8,9},{9,8},{10,11... | collective-permute-start | bytes 589832 | tf_op jit(solution)/shard_map/ppermute | solution.py:550
  30.2 5.5 %slice-start.1 = ((s8[4718592]{0:T(1024)(128)(4,1)}), s8[524288]{0:T(1024)(128)(4,1)S(1)}, s32[]{:S(2)}) async-start(s8[4718592]{0:T(1024)(128)(4,1)} %bitcast.15), calls=%async_computation.1 | async-start | bytes 1048576
  30.2 5.5 %copy-start.1 = (bf16[1536,768]{1,0:T(8,128)(2,1)S(1)}, bf16[1536,768]{1,0:T(8,128)(2,1)}, u32[]{:S(2)}) copy-start(bf16[1536,768]{1,0:T(8,128)(2,1)} %refs_12_.1) | copy-start | bytes 7077892
  30.2 5.5 %copy-start.2 = (bf16[768,768]{1,0:T(8,128)(2,1)S(1)}, bf16[768,768]{1,0:T(8,128)(2,1)}, u32[]{:S(2)}) copy-start(bf16[768,768]{1,0:T(8,128)(2,1)} %refs_9_.1) | copy-start | bytes 3538948
  30.3 5.5 %copy-start.6 = (bf16[768,128]{1,0:T(8,128)(2,1)S(1)}, bf16[768,128]{1,0:T(8,128)(2,1)}, u32[]{:S(2)}) copy-start(bf16[768,128]{1,0:T(8,128)(2,1)} %refs_13_.1) | copy-start | bytes 589828
  35.7 8.9 %copy-start.10 = (f32[1,3,1024]{2,0,1:T(1,128)S(1)}, f32[1,3,1024]{2,0,1:T(1,128)}, u32[]{:S(2)}) copy-start(f32[1,3,1024]{2,0,1:T(1,128)} %param.26) | copy-start | bytes 36868
  35.8 8.9 %copy-start.11 = (f32[1,3,1024]{2,0,1:T(1,128)S(1)}, f32[1,3,1024]{2,0,1:T(1,128)}, u32[]{:S(2)}) copy-start(f32[1,3,1024]{2,0,1:T(1,128)} %param.27) | copy-start | bytes 36868
  35.8 8.9 %copy-start.16 = (bf16[3,128]{1,0:T(4,128)(2,1)S(1)}, bf16[3,128]{1,0:T(4,128)(2,1)}, u32[]{:S(2)}) copy-start(bf16[3,128]{1,0:T(4,128)(2,1)} %coord_out_ref.3) | copy-start | bytes 2308
  35.8 8.9 %copy-start.18 = (f32[128]{0:T(128)S(1)}, f32[128]{0:T(128)}, u32[]{:S(2)}) copy-start(f32[128]{0:T(128)} %param.50) | copy-start | bytes 1540
  40.3 6.5 %collective-permute-start.8 = (bf16[96,128]{1,0:T(8,128)(2,1)S(1)}, bf16[96,128]{1,0:T(8,128)(2,1)S(1)}, u32[]{:S(2)}, u32[]{:S(2)}) collective-permute-start(bf16[96,128]{1,0:T(8,128)(2,1)S(1)} %get-tuple-element.39), channel_id=1, source_target_pairs={{0,1},{1,0},{2,3},{3,2},{4,5},{5,4},{6,7},{7,6},{8,9},{9,8},{10,11... | collective-permute-start | bytes 73736 | tf_op jit(solution)/shard_map/ppermute | solution.py:537
  42.1 5.7 %collective-permute-start.9 = (bf16[96,128]{1,0:T(8,128)(2,1)S(1)}, bf16[96,128]{1,0:T(8,128)(2,1)S(1)}, u32[]{:S(2)}, u32[]{:S(2)}) collective-permute-start(bf16[96,128]{1,0:T(8,128)(2,1)S(1)} %get-tuple-element.41), channel_id=1, source_target_pairs={{0,0},{3,3},{1,2},{2,1},{4,4},{7,7},{5,6},{6,5},{8,8},{11,11},{9,1... | collective-permute-start | bytes 73736 | tf_op jit(solution)/shard_map/ppermute | solution.py:536
  (2 other events, 10.9 us)

commit v6 on v5

--- a/solution.py
+++ b/solution.py
@@ -609,8 +609,7 @@
 
     pair_rows, _, channels = pair_cond.shape
     step_rows = 32
-    half = pair_rows // 2
-    steps = [(0, step_rows), (step_rows, half - step_rows), (half, pair_rows - half)]
+    steps = [(0, step_rows), (step_rows, pair_rows - step_rows)]
     gain_row, _ = lax.optimization_barrier((pair_gain, second_edge))
     bias = pl.pallas_call(
         functools.partial(pair_kernel, steps),

time: 50 us -> 50 us (level)
  no operation moved by 1% of the time
where the time goes in v6:
time: 50 us; the launch traced here: 49.7 us
  Pallas kernels  23 us (46%)
  starting transfers between devices  13.9 us (28%)
  waiting for transfers between devices  11 us (22%)
  between operations  1.71 us (3%)
    ppermute x6, waiting for transfers between devices, spread_over(): have[d | bit] = lax.ppermute(sent, axis, pairs)  9.95 us
    ppermute x6, starting transfers between devices, spread_over(): have[d | bit] = lax.ppermute(sent, axis, pairs)  6.05 us
    ppermute x2, starting transfers between devices, halos_of(): from_second = lax.ppermute(second_edge, 'row', second)  6.02 us
    pallas_call x1, Pallas kernels, per_device(): pl.pallas_call(functools.partial(pair_kernel, steps), out_shape=shape((he...  5.03 us
    pallas_call x1, Pallas kernels, per_device(): pl.pallas_call(functools.partial(token_kernel, near_count, row_count), ou...  4.51 us
    pallas_call x1, Pallas kernels, per_device(): pl.pallas_call(functools.partial(attend_first_kernel, near_count, row_cou...  3.78 us
    pallas_call x1, Pallas kernels, per_device(): pl.pallas_call(encoder_kernel, out_shape=(state_like, shape((tok_rows, to...  2.97 us
    pallas_call x1, Pallas kernels, per_device(): pl.pallas_call(prepare_kernel, out_shape=(state_like, normed_like, edge_l...  2.7 us
  transfers between devices with their start and end apart: 10, of which 4 were waited for; matrix products, arithmetic and copies ran while one was open for 0% of the time, Pallas kernels for 28%

profile of v6, /device:TPU:12, one launch (start us, length us, event | category | flops | bytes accessed | tf_op | source)
XLA Modules:
  0.0 49.7 jit_solution(9364110581006750340)
XLA Ops:
  1.3 2.7 %shard_map.257 = (f32[1024,128]{1,0:T(8,128)}, bf16[1024,128]{1,0:T(8,128)(2,1)}, bf16[96,128]{1,0:T(8,128)(2,1)}, bf16[96,128]{1,0:T(8,128)(2,1)}) custom-call(f32[1,1]{1,0:T(1,128)} %bitcast.11.level_hbm, f32[3,1,1024]{2,1,0:T(1,128)} %bitcast.20, f32[3,1,1024]{2,1,0:T(1,128)} %bitcast.23, bf16[1024,128]{1,0:T(8,128)(2,1)} %single_hbm.1, ...), custom_call_target="tpu_custom_call" | custom-call | flops 1500000000 | bytes 4500000 | tf_op jit(solution)/shard_map/pallas_call | solution.py:598
  4.0 3.5 %collective-permute-start.1 = (bf16[96,128]{1,0:T(8,128)(2,1)}, bf16[96,128]{1,0:T(8,128)(2,1)S(1)}, u32[]{:S(2)}, u32[]{:S(2)}) collective-permute-start(bf16[96,128]{1,0:T(8,128)(2,1)} %get-tuple-element.25), channel_id=1, source_target_pairs={{0,0},{3,3},{1,2},{2,1},{4,4},{7,7},{5,6},{6,5},{8,8},{11,11},{9,1... | collective-permute-start | bytes 73736 | tf_op jit(solution)/shard_map/ppermute | solution.py:536
  7.5 0.1 collective-permute-start
  7.6 0.0 copy-start.21
  7.6 0.0 copy-start.4
  7.6 0.0 copy-start.5
  7.6 0.0 copy-start.7
  7.6 0.0 copy-start.8
  7.6 0.0 copy-start.13
  7.7 0.0 copy-start.17
  7.7 5.0 %shard_map.259.refs_3_ = bf16[16,128,128]{2,1,0:T(8,128)(2,1)} custom-call(bf16[128,128,128]{2,1,0:T(8,128)(2,1)} %tile_hbm.1, f32[1,128]{1,0:T(1,128)} %bitcast.35, bf16[16,128]{1,0:T(8,128)(2,1)} %bitcast.34), custom_call_target="tpu_custom_call" | custom-call | flops 5000000000 | bytes 15000000 | tf_op jit(solution)/shard_map/pallas_call | solution.py:614
  12.7 1.6 %collective-permute-start.6 = (bf16[16,128,128]{2,1,0:T(8,128)(2,1)}, bf16[16,128,128]{2,1,0:T(8,128)(2,1)S(1)}, u32[]{:S(2)}, u32[]{:S(2)}) collective-permute-start(bf16[16,128,128]{2,1,0:T(8,128)(2,1)} %shard_map.259.refs_3_), channel_id=1, source_target_pairs={{0,8},{4,12},{8,0},{12,4},{1,9},{5,13},{9,1},{13,5},{2,10},{6,14},... | collective-permute-start | bytes 1572872 | tf_op jit(solution)/shard_map/ppermute | solution.py:550
  14.4 0.0 slice-start
  14.4 3.0 %shard_map.258 = (f32[1024,128]{1,0:T(8,128)S(1)}, f32[128,768]{1,0:T(8,128)S(1)}, bf16[128,768]{1,0:T(8,128)(2,1)S(1)}, bf16[128,1024]{1,0:T(8,128)(2,1)S(1)}) custom-call(s32[1,32]{1,0:T(1,128)S(1)} %bitcast.29, f32[1,1]{1,0:T(1,128)} %bitcast.12.level_ref, f32[1024,128]{1,0:T(8,128)S(1)} %copy-done.19, bf16[96,128]{1,0:T(8,128)(2,1)S(1)} %collective-permute-done.low_ref, ...), custom_call_target="tpu_custom_call" | custom-call | flops 3400000000 | bytes 10200000 | tf_op jit(solution)/shard_map/pallas_call | solution.py:632
  17.4 1.9 %collective-permute-start.2 = (bf16[128,768]{1,0:T(8,128)(2,1)S(1)}, bf16[128,768]{1,0:T(8,128)(2,1)S(1)}, u32[]{:S(2)}, u32[]{:S(2)}) collective-permute-start(bf16[128,768]{1,0:T(8,128)(2,1)S(1)} %get-tuple-element.26.refs_0_), channel_id=1, source_target_pairs={{0,2},{1,3},{2,0},{3,1},{4,6},{5,7},{6,4},{7,5},{8,10},{9,11},{10,... | collective-permute-start | bytes 589832 | tf_op jit(solution)/shard_map/ppermute | solution.py:550
  19.3 0.5 %collective-permute-start.4 = (bf16[128,768]{1,0:T(8,128)(2,1)S(1)}, bf16[128,768]{1,0:T(8,128)(2,1)S(1)}, u32[]{:S(2)}, u32[]{:S(2)}) collective-permute-start(bf16[128,768]{1,0:T(8,128)(2,1)S(1)} %get-tuple-element.26.refs_0_), channel_id=1, source_target_pairs={{0,1},{1,0},{2,3},{3,2},{4,5},{5,4},{6,7},{7,6},{8,9},{9,8},{10,11... | collective-permute-start | bytes 589832 | tf_op jit(solution)/shard_map/ppermute | solution.py:550
  19.9 7.0 %collective-permute-done.2.refs_2_ = bf16[128,768]{1,0:T(8,128)(2,1)S(1)} collective-permute-done((bf16[128,768]{1,0:T(8,128)(2,1)S(1)}, bf16[128,768]{1,0:T(8,128)(2,1)S(1)}, u32[]{:S(2)}, u32[]{:S(2)}) %collective-permute-start.2) | collective-permute-done | bytes 196640 | tf_op jit(solution)/shard_map/ppermute | solution.py:550
  26.9 1.3 %collective-permute-done.4.refs_1_ = bf16[128,768]{1,0:T(8,128)(2,1)S(1)} collective-permute-done((bf16[128,768]{1,0:T(8,128)(2,1)S(1)}, bf16[128,768]{1,0:T(8,128)(2,1)S(1)}, u32[]{:S(2)}, u32[]{:S(2)}) %collective-permute-start.4) | collective-permute-done | bytes 196640 | tf_op jit(solution)/shard_map/ppermute | solution.py:550
  28.2 2.0 %collective-permute-start.3 = (bf16[128,768]{1,0:T(8,128)(2,1)S(1)}, bf16[128,768]{1,0:T(8,128)(2,1)S(1)}, u32[]{:S(2)}, u32[]{:S(2)}) collective-permute-start(bf16[128,768]{1,0:T(8,128)(2,1)S(1)} %collective-permute-done.2.refs_2_), channel_id=1, source_target_pairs={{0,1},{1,0},{2,3},{3,2},{4,5},{5,4},{6,7},{7,6},{8,9},{9,8},{10,11... | collective-permute-start | bytes 589832 | tf_op jit(solution)/shard_map/ppermute | solution.py:550
  30.3 0.0 slice-start.1
  30.3 0.0 copy-start.2
  30.3 0.0 copy-start.6
  30.3 3.8 %shard_map.260 = (bf16[128,768]{1,0:T(8,128)(2,1)S(1)}, f32[128,768]{1,0:T(8,128)S(1)}, f32[16,128,128]{2,1,0:T(8,128)S(1)}, f32[16,128,128]{2,1,0:T(8,128)S(1)}, bf16[1,16,128,128]{3,2,1,0:T(8,128)(2,1)S(1)}) custom-call(bf16[128,768]{1,0:T(8,128)(2,1)S(1)} %get-tuple-element.26.refs_0_, bf16[128,768]{1,0:T(8,128)(2,1)S(1)} %collective-permute-done.4.refs_1_, ...), custom_call_target="tpu_custom_call" | custom-call | flops 4000000000 | bytes 12000000 | tf_op jit(solution)/shard_map/pallas_call | solution.py:661
  34.1 1.6 %collective-permute-done.3.refs_0_ = bf16[128,768]{1,0:T(8,128)(2,1)S(1)} collective-permute-done((bf16[128,768]{1,0:T(8,128)(2,1)S(1)}, bf16[128,768]{1,0:T(8,128)(2,1)S(1)}, u32[]{:S(2)}, u32[]{:S(2)}) %collective-permute-start.3) | collective-permute-done | bytes 196640 | tf_op jit(solution)/shard_map/ppermute | solution.py:550
  35.8 0.0 copy-start.11
  35.8 0.0 copy-start.16
  35.8 4.5 %shard_map.261 = (bf16[1,128,768]{2,1,0:T(8,128)(2,1)}, f32[1024,128]{1,0:T(8,128)S(1)}, bf16[1024,128]{1,0:T(8,128)(2,1)S(1)}, bf16[96,128]{1,0:T(8,128)(2,1)S(1)}, bf16[96,128]{1,0:T(8,128)(2,1)S(1)}) custom-call(bf16[128,768]{1,0:T(8,128)(2,1)S(1)} %collective-permute-done.3.refs_0_, bf16[128,768]{1,0:T(8,128)(2,1)S(1)} %get-tuple-element.29.refs_1_, ...), custom_call_target="tpu_custom_call" | custom-call | flops 6000000000 | bytes 18000000 | tf_op jit(solution)/shard_map/pallas_call | solution.py:681
  40.3 1.8 %collective-permute-start.8 = (bf16[96,128]{1,0:T(8,128)(2,1)S(1)}, bf16[96,128]{1,0:T(8,128)(2,1)S(1)}, u32[]{:S(2)}, u32[]{:S(2)}) collective-permute-start(bf16[96,128]{1,0:T(8,128)(2,1)S(1)} %get-tuple-element.39), channel_id=1, source_target_pairs={{0,1},{1,0},{2,3},{3,2},{4,5},{5,4},{6,7},{7,6},{8,9},{9,8},{10,11... | collective-permute-start | bytes 73736 | tf_op jit(solution)/shard_map/ppermute | solution.py:537
  42.1 2.5 %collective-permute-start.9 = (bf16[96,128]{1,0:T(8,128)(2,1)S(1)}, bf16[96,128]{1,0:T(8,128)(2,1)S(1)}, u32[]{:S(2)}, u32[]{:S(2)}) collective-permute-start(bf16[96,128]{1,0:T(8,128)(2,1)S(1)} %get-tuple-element.41), channel_id=1, source_target_pairs={{0,0},{3,3},{1,2},{2,1},{4,4},{7,7},{5,6},{6,5},{8,8},{11,11},{9,1... | collective-permute-start | bytes 73736 | tf_op jit(solution)/shard_map/ppermute | solution.py:536
  44.7 2.1 %shard_map.262.inner_ref = f32[3,1,1024]{2,1,0:T(1,128)S(1)} custom-call(s32[1,32]{1,0:T(1,128)S(1)} %bitcast.30, f32[1,1]{1,0:T(1,128)} %bitcast.13.level_ref, f32[3,1,1024]{2,1,0:T(1,128)S(1)} %bitcast.21, f32[3,1,1024]{2,1,0:T(1,128)S(1)} %bitcast.24, f32[1024,128]{1,0:T(8,128)S(1)} %get-tuple-element.38.state_ref, ...), custom_call_target="tpu_custom_call" | custom-call | flops 2700000000 | bytes 8100000 | tf_op jit(solution)/shard_map/pallas_call | solution.py:709
  46.8 1.0 %collective-permute-done.9.high_ref = bf16[96,128]{1,0:T(8,128)(2,1)S(1)} collective-permute-done((bf16[96,128]{1,0:T(8,128)(2,1)S(1)}, bf16[96,128]{1,0:T(8,128)(2,1)S(1)}, u32[]{:S(2)}, u32[]{:S(2)}) %collective-permute-start.9) | collective-permute-done | bytes 24608 | tf_op jit(solution)/shard_map/ppermute | solution.py:536
  47.8 1.9 %shard_map.263 = f32[3,1,1024]{2,1,0:T(1,128)} custom-call(s32[1,32]{1,0:T(1,128)S(1)} %bitcast.31, f32[1,1]{1,0:T(1,128)} %bitcast.14.level_ref, f32[3,1,1024]{2,1,0:T(1,128)S(1)} %bitcast.22, f32[3,1,1024]{2,1,0:T(1,128)S(1)} %bitcast.25, f32[1024,128]{1,0:T(8,128)S(1)} %get-tuple-element.38.state_ref, bf16[96,128]{1,0:T(8,128)(2,1)S(1)} %collective-permute-done.8.low_ref, ...), custom_call_target="tpu_custom_call" | custom-call | flops 2000000000 | bytes 6000000 | tf_op jit(solution)/shard_map/pallas_call | solution.py:720
  (45 shorter events, 0.1 us)
Async XLA Ops:
  4.0 10.3 %collective-permute-start.1 = (bf16[96,128]{1,0:T(8,128)(2,1)}, bf16[96,128]{1,0:T(8,128)(2,1)S(1)}, u32[]{:S(2)}, u32[]{:S(2)}) collective-permute-start(bf16[96,128]{1,0:T(8,128)(2,1)} %get-tuple-element.25), channel_id=1, source_target_pairs={{0,0},{3,3},{1,2},{2,1},{4,4},{7,7},{5,6},{6,5},{8,8},{11,11},{9,1... | collective-permute-start | bytes 73736 | tf_op jit(solution)/shard_map/ppermute | solution.py:536
  7.5 6.8 %collective-permute-start = (bf16[96,128]{1,0:T(8,128)(2,1)}, bf16[96,128]{1,0:T(8,128)(2,1)S(1)}, u32[]{:S(2)}, u32[]{:S(2)}) collective-permute-start(bf16[96,128]{1,0:T(8,128)(2,1)} %get-tuple-element.23), channel_id=1, source_target_pairs={{0,1},{1,0},{2,3},{3,2},{4,5},{5,4},{6,7},{7,6},{8,9},{9,8},{10,11... | collective-permute-start | bytes 73736 | tf_op jit(solution)/shard_map/ppermute | solution.py:537
  7.6 6.7 %copy-start.21 = (f32[768]{0:T(1024)S(1)}, f32[768]{0:T(1024)}, u32[]{:S(2)}) copy-start(f32[768]{0:T(1024)} %param.41) | copy-start | bytes 9220
  7.6 6.7 %copy-start.4 = (bf16[128,768]{1,0:T(8,128)(2,1)S(1)}, bf16[128,768]{1,0:T(8,128)(2,1)}, u32[]{:S(2)}) copy-start(bf16[128,768]{1,0:T(8,128)(2,1)} %lift_ref.1) | copy-start | bytes 589828
  7.6 6.7 %copy-start.5 = (bf16[128,768]{1,0:T(8,128)(2,1)S(1)}, bf16[128,768]{1,0:T(8,128)(2,1)}, u32[]{:S(2)}) copy-start(bf16[128,768]{1,0:T(8,128)(2,1)} %single_ref.1) | copy-start | bytes 589828
  7.6 6.7 %copy-start.7 = (bf16[2,128,384]{2,1,0:T(8,128)(2,1)S(1)}, bf16[2,128,384]{2,1,0:T(8,128)(2,1)}, u32[]{:S(2)}) copy-start(bf16[2,128,384]{2,1,0:T(8,128)(2,1)} %w_qkv_ref.5) | copy-start | bytes 589828
  7.6 6.7 %copy-start.8 = (bf16[2,128,128]{2,1,0:T(8,128)(2,1)S(1)}, bf16[2,128,128]{2,1,0:T(8,128)(2,1)}, u32[]{:S(2)}) copy-start(bf16[2,128,128]{2,1,0:T(8,128)(2,1)} %w_out_ref.5) | copy-start | bytes 196612
  7.6 6.7 %copy-start.9 = (s32[4096]{0:T(1024)S(1)}, s32[4096]{0:T(1024)}, u32[]{:S(2)}) copy-start(s32[4096]{0:T(1024)} %param.34) | copy-start | bytes 49156
  7.6 6.7 %copy-start.12 = (f32[2,768]{1,0:T(2,128)S(1)}, f32[2,768]{1,0:T(2,128)}, u32[]{:S(2)}) copy-start(f32[2,768]{1,0:T(2,128)} %refs_10_.1) | copy-start | bytes 18436
  7.6 6.7 %copy-start.13 = (s32[1024]{0:T(1024)S(1)}, s32[1024]{0:T(1024)}, u32[]{:S(2)}) copy-start(s32[1024]{0:T(1024)} %param.32) | copy-start | bytes 12292
  7.7 6.7 %copy-start.17 = (s32[32]{0:T(128)S(1)}, s32[32]{0:T(128)}, u32[]{:S(2)}) copy-start(s32[32]{0:T(128)} %param.33) | copy-start | bytes 388
  7.7 6.7 %copy-start.19 = (f32[1024,128]{1,0:T(8,128)S(1)}, f32[1024,128]{1,0:T(8,128)}, u32[]{:S(2)}) copy-start(f32[1024,128]{1,0:T(8,128)} %get-tuple-element.22.state_ref) | copy-start | bytes 1572868
  7.7 6.7 %copy-start.20 = (bf16[1024,128]{1,0:T(8,128)(2,1)S(1)}, bf16[1024,128]{1,0:T(8,128)(2,1)}, u32[]{:S(2)}) copy-start(bf16[1024,128]{1,0:T(8,128)(2,1)} %get-tuple-element.24.mid_ref) | copy-start | bytes 786436
  12.7 15.5 %collective-permute-start.6 = (bf16[16,128,128]{2,1,0:T(8,128)(2,1)}, bf16[16,128,128]{2,1,0:T(8,128)(2,1)S(1)}, u32[]{:S(2)}, u32[]{:S(2)}) collective-permute-start(bf16[16,128,128]{2,1,0:T(8,128)(2,1)} %shard_map.259.refs_3_), channel_id=1, source_target_pairs={{0,8},{4,12},{8,0},{12,4},{1,9},{5,13},{9,1},{13,5},{2,10},{6,14},... | collective-permute-start | bytes 1572872 | tf_op jit(solution)/shard_map/ppermute | solution.py:550
  14.4 5.5 %copy-start.3 = (bf16[16,128,128]{2,1,0:T(8,128)(2,1)S(1)}, bf16[16,128,128]{2,1,0:T(8,128)(2,1)}, u32[]{:S(2)}) copy-start(bf16[16,128,128]{2,1,0:T(8,128)(2,1)} %shard_map.259.refs_3_) | copy-start | bytes 1572868
  14.4 15.8 %copy-start = (bf16[768,2304]{1,0:T(8,128)(2,1)S(1)}, bf16[768,2304]{1,0:T(8,128)(2,1)}, u32[]{:S(2)}) copy-start(bf16[768,2304]{1,0:T(8,128)(2,1)} %refs_8_.3) | copy-start | bytes 10616836
  14.4 15.8 %copy-start.14 = (s32[512]{0:T(512)S(1)}, s32[512]{0:T(512)}, u32[]{:S(2)}) copy-start(s32[512]{0:T(512)} %param.35) | copy-start | bytes 6148
  14.4 21.3 %slice-start = ((s8[4718592]{0:T(1024)(128)(4,1)}), s8[4194304]{0:T(1024)(128)(4,1)S(1)}, s32[]{:S(2)}) async-start(s8[4718592]{0:T(1024)(128)(4,1)} %bitcast.15), calls=%async_computation | async-start | bytes 8388608
  17.4 9.4 %collective-permute-start.2 = (bf16[128,768]{1,0:T(8,128)(2,1)S(1)}, bf16[128,768]{1,0:T(8,128)(2,1)S(1)}, u32[]{:S(2)}, u32[]{:S(2)}) collective-permute-start(bf16[128,768]{1,0:T(8,128)(2,1)S(1)} %get-tuple-element.26.refs_0_), channel_id=1, source_target_pairs={{0,2},{1,3},{2,0},{3,1},{4,6},{5,7},{6,4},{7,5},{8,10},{9,11},{10,... | collective-permute-start | bytes 589832 | tf_op jit(solution)/shard_map/ppermute | solution.py:550
  19.3 8.9 %collective-permute-start.4 = (bf16[128,768]{1,0:T(8,128)(2,1)S(1)}, bf16[128,768]{1,0:T(8,128)(2,1)S(1)}, u32[]{:S(2)}, u32[]{:S(2)}) collective-permute-start(bf16[128,768]{1,0:T(8,128)(2,1)S(1)} %get-tuple-element.26.refs_0_), channel_id=1, source_target_pairs={{0,1},{1,0},{2,3},{3,2},{4,5},{5,4},{6,7},{7,6},{8,9},{9,8},{10,11... | collective-permute-start | bytes 589832 | tf_op jit(solution)/shard_map/ppermute | solution.py:550
  19.9 10.4 %collective-permute-start.5 = (bf16[16,128,128]{2,1,0:T(8,128)(2,1)S(1)}, bf16[16,128,128]{2,1,0:T(8,128)(2,1)S(1)}, u32[]{:S(2)}, u32[]{:S(2)}) collective-permute-start(bf16[16,128,128]{2,1,0:T(8,128)(2,1)S(1)} %copy-done.3), channel_id=1, source_target_pairs={{0,4},{4,0},{8,12},{12,8},{1,5},{5,1},{9,13},{13,9},{2,6},{6,2},{1... | collective-permute-start | bytes 1572872 | tf_op jit(solution)/shard_map/ppermute | solution.py:550
  28.2 2.1 %collective-permute-start.7 = (bf16[16,128,128]{2,1,0:T(8,128)(2,1)S(1)}, bf16[16,128,128]{2,1,0:T(8,128)(2,1)S(1)}, u32[]{:S(2)}, u32[]{:S(2)}) collective-permute-start(bf16[16,128,128]{2,1,0:T(8,128)(2,1)S(1)} %collective-permute-done.6.refs_5_), channel_id=1, source_target_pairs={{0,4},{4,0},{8,12},{12,8},{1,5},{5,1},{9,13},{13,9},{2,6},{6,2},{1... | collective-permute-start | bytes 1572872 | tf_op jit(solution)/shard_map/ppermute | solution.py:550
  28.2 7.5 %collective-permute-start.3 = (bf16[128,768]{1,0:T(8,128)(2,1)S(1)}, bf16[128,768]{1,0:T(8,128)(2,1)S(1)}, u32[]{:S(2)}, u32[]{:S(2)}) collective-permute-start(bf16[128,768]{1,0:T(8,128)(2,1)S(1)} %collective-permute-done.2.refs_2_), channel_id=1, source_target_pairs={{0,1},{1,0},{2,3},{3,2},{4,5},{5,4},{6,7},{7,6},{8,9},{9,8},{10,11... | collective-permute-start | bytes 589832 | tf_op jit(solution)/shard_map/ppermute | solution.py:550
  30.3 5.5 %slice-start.1 = ((s8[4718592]{0:T(1024)(128)(4,1)}), s8[524288]{0:T(1024)(128)(4,1)S(1)}, s32[]{:S(2)}) async-start(s8[4718592]{0:T(1024)(128)(4,1)} %bitcast.15), calls=%async_computation.1 | async-start | bytes 1048576
  30.3 5.5 %copy-start.1 = (bf16[1536,768]{1,0:T(8,128)(2,1)S(1)}, bf16[1536,768]{1,0:T(8,128)(2,1)}, u32[]{:S(2)}) copy-start(bf16[1536,768]{1,0:T(8,128)(2,1)} %refs_12_.1) | copy-start | bytes 7077892
  30.3 5.5 %copy-start.2 = (bf16[768,768]{1,0:T(8,128)(2,1)S(1)}, bf16[768,768]{1,0:T(8,128)(2,1)}, u32[]{:S(2)}) copy-start(bf16[768,768]{1,0:T(8,128)(2,1)} %refs_9_.1) | copy-start | bytes 3538948
  35.8 8.9 %copy-start.10 = (f32[1,3,1024]{2,0,1:T(1,128)S(1)}, f32[1,3,1024]{2,0,1:T(1,128)}, u32[]{:S(2)}) copy-start(f32[1,3,1024]{2,0,1:T(1,128)} %param.26) | copy-start | bytes 36868
  35.8 8.9 %copy-start.11 = (f32[1,3,1024]{2,0,1:T(1,128)S(1)}, f32[1,3,1024]{2,0,1:T(1,128)}, u32[]{:S(2)}) copy-start(f32[1,3,1024]{2,0,1:T(1,128)} %param.27) | copy-start | bytes 36868
  35.8 8.9 %copy-start.16 = (bf16[3,128]{1,0:T(4,128)(2,1)S(1)}, bf16[3,128]{1,0:T(4,128)(2,1)}, u32[]{:S(2)}) copy-start(bf16[3,128]{1,0:T(4,128)(2,1)} %coord_out_ref.3) | copy-start | bytes 2308
  35.8 8.9 %copy-start.18 = (f32[128]{0:T(128)S(1)}, f32[128]{0:T(128)}, u32[]{:S(2)}) copy-start(f32[128]{0:T(128)} %param.50) | copy-start | bytes 1540
  40.3 6.4 %collective-permute-start.8 = (bf16[96,128]{1,0:T(8,128)(2,1)S(1)}, bf16[96,128]{1,0:T(8,128)(2,1)S(1)}, u32[]{:S(2)}, u32[]{:S(2)}) collective-permute-start(bf16[96,128]{1,0:T(8,128)(2,1)S(1)} %get-tuple-element.39), channel_id=1, source_target_pairs={{0,1},{1,0},{2,3},{3,2},{4,5},{5,4},{6,7},{7,6},{8,9},{9,8},{10,11... | collective-permute-start | bytes 73736 | tf_op jit(solution)/shard_map/ppermute | solution.py:537
  42.1 5.7 %collective-permute-start.9 = (bf16[96,128]{1,0:T(8,128)(2,1)S(1)}, bf16[96,128]{1,0:T(8,128)(2,1)S(1)}, u32[]{:S(2)}, u32[]{:S(2)}) collective-permute-start(bf16[96,128]{1,0:T(8,128)(2,1)S(1)} %get-tuple-element.41), channel_id=1, source_target_pairs={{0,0},{3,3},{1,2},{2,1},{4,4},{7,7},{5,6},{6,5},{8,8},{11,11},{9,1... | collective-permute-start | bytes 73736 | tf_op jit(solution)/shard_map/ppermute | solution.py:536
  (2 other events, 10.9 us)
